TPU v7x, 32 devices: a whole 2x2x4 slice. The times are simulated.
32 devices in a mesh: dp: 4 (over z), expert: 8 (over y, x, core).
Axes of the slice: x: 2, y: 2, z: 4, core: 2. Of those that a mesh axis runs over, the one named last changes fastest.
Arguments:
- tokens: bfloat16 [4096, 1536], P(('dp', 'expert')), may hold values from -6 to 6
- cotangent: bfloat16 [4096, 1536], P(('dp', 'expert')), may hold values from -6 to 6
- routes: int32 [1, 4096, 4], P(None, ('dp', 'expert')), may hold values from 0 to 7, all different within a row; in each aligned block of 128 rows (0 to 127, 128 to 255, ..., all dimensions but the last counted through in order) at most 96 rows name the same one
- gain_attn: bfloat16 [1, 1536], P(None, ('dp', 'expert')), may hold values from 0.099609375 to 1.8984375
- w_query: bfloat16 [1, 1536, 1536], P(None, ('dp', 'expert')), may hold values from -0.21875 to 0.21875
- key_weight: bfloat16 [1, 1536, 256], P(None, ('dp', 'expert')), may hold values from -0.21875 to 0.21875
- value_weight: bfloat16 [1, 1536, 256], P(None, ('dp', 'expert')), may hold values from -0.15625 to 0.15625
- w_output: bfloat16 [1, 1536, 1536], P(None, ('dp', 'expert')), may hold values from -2 to 2
- gain_moe: bfloat16 [1, 1536], P(None, ('dp', 'expert')), may hold values from 0.099609375 to 1.8984375
- w_router: bfloat16 [1, 1536, 8], P(None, ('dp', 'expert')), may hold values from -0.078125 to 0.078125
- w_in: bfloat16 [1, 1536, 8, 1536], P(None, 'dp', 'expert'), may hold values from -0.15625 to 0.15625
- w_out: bfloat16 [1, 768, 8, 1536], P(None, 'dp', 'expert'), may hold values from -0.625 to 0.625
Outputs:
- block_out: bfloat16 [4096, 1536], P(('dp', 'expert'))
- tokens_grad: float32 [4096, 1536], P(('dp', 'expert'))
- gain_attn_grad: float32 [1, 1536], P(None, ('dp', 'expert'))
- w_query_grad: float32 [1, 1536, 1536], P(None, ('dp', 'expert'))
- w_key_grad: float32 [1, 1536, 256], P(None, ('dp', 'expert'))
- w_value_grad: float32 [1, 1536, 256], P(None, ('dp', 'expert'))
- w_output_grad: float32 [1, 1536, 1536], P(None, ('dp', 'expert'))
- gain_moe_grad: float32 [1, 1536], P(None, ('dp', 'expert'))
- w_router_grad: float32 [1, 1536, 8], P(None, ('dp', 'expert'))
- w_in_grad: float32 [1, 1536, 8, 1536], P(None, 'dp', 'expert')
- w_out_grad: float32 [1, 768, 8, 1536], P(None, 'dp', 'expert')
Inputs may be any that keep to these rules, and one draw needn't show every extreme that they name: `routes`: in each layer the 128 rows of one device name every expert at most 96 times, a bound that some block reaches; a row names 4 different experts.
All inputs are finite; a program needn't handle non-finite values.
Results may differ from a plain program's by a relative error of at most 0.018.
The roundings to bfloat16 on the way count: a program that leaves them out, or rounds other values in their place, can miss the bound.
Values may be sent and summed in bfloat16 or wider, within the bound.
A program may use at most 192 MiB of HBM per device.

v0:
```python
import jax
import jax.numpy as jnp
from jax import lax
from jax.sharding import PartitionSpec as P

QUERY_HEADS = 12
KEY_VALUE_HEADS = 2
HEAD_DIM = 128
FF = 768
TOP = 4


norm_eps = 1e-06
rope_base = 1000000.0
masked_score = -1e30
top_precision = lax.Precision.HIGHEST


def norm_factor(values):
    return lax.rsqrt(jnp.mean(values * values, axis=-1, keepdims=True) + norm_eps)


def norm_back(values, gain, grad_out):
    factor = norm_factor(values)
    scaled = grad_out * gain
    gain_grad = jnp.sum(grad_out * values * factor, axis=0)
    inner_mean = jnp.mean(scaled * values, axis=-1, keepdims=True)
    return (factor * scaled - values * factor * factor * factor * inner_mean, gain_grad)


def rope_tables(positions, head_size):
    half_size = head_size // 2
    inverse = rope_base ** (-(jnp.arange(half_size, dtype=jnp.float32) * 2.0 / head_size))
    angles = positions.astype(jnp.float32)[:, None] * inverse[None, :]
    return (jnp.cos(angles), jnp.sin(angles))


def rotate(values, cos_table, sin_table, orient):
    half_size = values.shape[-1] // 2
    first_half = values[..., :half_size]
    second = values[..., half_size:]
    cos_part = cos_table[:, None, :]
    sin_part = orient * sin_table[:, None, :]
    return jnp.concatenate(
        [first_half * cos_part - second * sin_part, second * cos_part + first_half * sin_part],
        axis=-1,
    )


def plan_slots(route, expert_count, capacity):
    flat_route = route.reshape(-1)
    slot_total = flat_route.shape[0]
    onehot = (flat_route[:, None] == jnp.arange(expert_count, dtype=jnp.int32)[None, :]).astype(
        jnp.int32
    )
    before = jnp.cumsum(onehot, axis=0) - onehot
    target = flat_route * capacity + jnp.sum(before * onehot, axis=1)
    source = (
        jnp.full((expert_count * capacity,), slot_total, jnp.int32)
        .at[target]
        .set(jnp.arange(slot_total, dtype=jnp.int32))
    )
    filled = source < slot_total
    return (target, jnp.minimum(source, slot_total - 1), filled)


def body(
    tokens,
    cotangent,
    routes,
    gain_attn,
    w_query,
    key_weight,
    value_weight,
    w_output,
    gain_moe,
    w_router,
    w_in,
    w_out,
):
    total_rows, model_width = tokens.shape
    layer_count = w_query.shape[0]
    group_count = lax.axis_size("expert")
    seq_len = total_rows * group_count
    experts_local = w_in.shape[2]
    expert_count = experts_local * group_count
    capacity = min(total_rows, total_rows * TOP * 3 // (2 * expert_count))
    heads_per_group = QUERY_HEADS // KEY_VALUE_HEADS
    score_scale = HEAD_DIM ** (-0.5)
    positions = lax.axis_index("expert") * total_rows + jnp.arange(total_rows, dtype=jnp.int32)
    cos_table, sin_table = rope_tables(positions, HEAD_DIM)
    allowed = jnp.arange(seq_len, dtype=jnp.int32)[None, :] <= positions[:, None]
    zero_bf = jnp.zeros((), jnp.bfloat16)

    def score_block(query_rows, all_keys, group_of_heads):
        grouped_q = query_rows[
            :, group_of_heads * heads_per_group : (group_of_heads + 1) * heads_per_group, :
        ]
        scores = (
            jnp.einsum(
                "rgd,kd->grk",
                grouped_q,
                all_keys[:, group_of_heads, :],
                preferred_element_type=jnp.float32,
            )
            * score_scale
        )
        return (jnp.where(allowed[None], scores, masked_score), grouped_q)

    residual = tokens.astype(jnp.float32)
    layer_number = 0
    dense_w = (
        lax.all_gather(gain_attn[layer_number], ("dp", "expert"), axis=0, tiled=True),
        lax.all_gather(w_query[layer_number], ("dp", "expert"), axis=0, tiled=True),
        lax.all_gather(key_weight[layer_number], ("dp", "expert"), axis=0, tiled=True),
        lax.all_gather(value_weight[layer_number], ("dp", "expert"), axis=0, tiled=True),
        lax.all_gather(w_output[layer_number], ("dp", "expert"), axis=0, tiled=True),
        lax.all_gather(gain_moe[layer_number], ("dp", "expert"), axis=0, tiled=True),
        lax.all_gather(w_router[layer_number], ("dp", "expert"), axis=0, tiled=True),
    )
    expert_w = (
        lax.all_gather(w_in[layer_number], "dp", axis=0, tiled=True),
        lax.all_gather(w_out[layer_number], "dp", axis=0, tiled=True),
    )
    route = routes[layer_number]
    gain_a = dense_w[0].astype(jnp.float32)
    norm_result = (residual * norm_factor(residual) * gain_a).astype(jnp.bfloat16)
    query_rows = jnp.dot(norm_result, dense_w[1], preferred_element_type=jnp.float32).reshape(
        total_rows, QUERY_HEADS, HEAD_DIM
    )
    query_rows = rotate(query_rows, cos_table, sin_table, 1.0).astype(jnp.bfloat16)
    key_matrix_rows = jnp.dot(norm_result, dense_w[2], preferred_element_type=jnp.float32).reshape(
        total_rows, KEY_VALUE_HEADS, HEAD_DIM
    )
    key_matrix_rows = rotate(key_matrix_rows, cos_table, sin_table, 1.0).astype(jnp.bfloat16)
    value_matrix_rows = (
        jnp.dot(norm_result, dense_w[3], preferred_element_type=jnp.float32)
        .astype(jnp.bfloat16)
        .reshape(total_rows, KEY_VALUE_HEADS, HEAD_DIM)
    )
    all_keys = lax.all_gather(key_matrix_rows, "expert", axis=0, tiled=True)
    all_values = lax.all_gather(value_matrix_rows, "expert", axis=0, tiled=True)
    heads_out = []
    log_totals = []
    for group_of_heads in range(KEY_VALUE_HEADS):
        scores, grouped_q = score_block(query_rows, all_keys, group_of_heads)
        row_peak = jnp.max(scores, axis=-1, keepdims=True)
        expo_vals = jnp.exp(scores - row_peak)
        row_sums = jnp.sum(expo_vals, axis=-1, keepdims=True)
        attn_probs = (expo_vals / row_sums).astype(jnp.bfloat16)
        log_totals.append(row_peak + jnp.log(row_sums))
        heads_out.append(
            jnp.einsum(
                "grk,kd->rgd",
                attn_probs,
                all_values[:, group_of_heads, :],
                preferred_element_type=jnp.float32,
            )
        )
    attn = (
        jnp.concatenate(heads_out, axis=1)
        .reshape(total_rows, QUERY_HEADS * HEAD_DIM)
        .astype(jnp.bfloat16)
    )
    after_attn = residual + jnp.dot(attn, dense_w[4], preferred_element_type=jnp.float32)
    gain_m = dense_w[5].astype(jnp.float32)
    normed_two = (after_attn * norm_factor(after_attn) * gain_m).astype(jnp.bfloat16)
    logits = jnp.dot(normed_two, dense_w[6], preferred_element_type=jnp.float32)
    gate_probs = jax.nn.softmax(jnp.take_along_axis(logits, route, axis=1), axis=-1)
    target, source, filled = plan_slots(route, expert_count, capacity)
    send_rows = jnp.where(filled[:, None], normed_two[source // TOP], zero_bf)
    send_rows = send_rows.reshape(group_count, experts_local, capacity, model_width)
    arrived_rows = lax.all_to_all(send_rows, "expert", split_axis=0, concat_axis=0, tiled=True)
    gate_up_vals = jnp.einsum(
        "secd,def->secf", arrived_rows, expert_w[0], preferred_element_type=jnp.float32
    )
    expert_gate_half = gate_up_vals[..., :FF]
    expert_hidden_act = (
        expert_gate_half * jax.nn.sigmoid(expert_gate_half) * gate_up_vals[..., FF:]
    ).astype(jnp.bfloat16)
    expert_out = jnp.einsum(
        "secf,fed->secd", expert_hidden_act, expert_w[1], preferred_element_type=jnp.float32
    ).astype(jnp.bfloat16)
    arrived, gate_up, expert_out = (arrived_rows, gate_up_vals, expert_out)
    returned = lax.all_to_all(expert_out, "expert", split_axis=0, concat_axis=0, tiled=True)
    slot_out = returned.reshape(expert_count * capacity, model_width)[target].reshape(
        total_rows, TOP, model_width
    )
    new_residual = after_attn + jnp.sum(
        gate_probs[:, :, None] * slot_out.astype(jnp.float32), axis=1
    )
    saved_layers = [
        (
            residual,
            norm_result,
            query_rows,
            key_matrix_rows,
            value_matrix_rows,
            all_keys,
            all_values,
            log_totals,
            attn,
            after_attn,
            normed_two,
            route,
            gate_probs,
            target,
            source,
            filled,
            arrived,
            gate_up,
            slot_out,
            dense_w,
            expert_w,
        )
    ]
    block_out = new_residual.astype(jnp.bfloat16)
    grad_resid = cotangent.astype(jnp.float32)
    grad_lists = [[None] * layer_count for _ in range(9)]
    for layer_number in reversed(range(layer_count)):
        (
            resid_in,
            norm_result,
            query_rows,
            key_matrix_rows,
            value_matrix_rows,
            all_keys,
            all_values,
            log_totals,
            attn,
            after_attn,
            normed_two,
            route,
            gate_probs,
            target,
            source,
            filled,
            arrived,
            gate_up,
            slot_out,
            dense_w,
            expert_w,
        ) = saved_layers[layer_number]
        dense_w = (
            lax.all_gather(gain_attn[layer_number], ("dp", "expert"), axis=0, tiled=True),
            lax.all_gather(w_query[layer_number], ("dp", "expert"), axis=0, tiled=True),
            lax.all_gather(key_weight[layer_number], ("dp", "expert"), axis=0, tiled=True),
            lax.all_gather(value_weight[layer_number], ("dp", "expert"), axis=0, tiled=True),
            lax.all_gather(w_output[layer_number], ("dp", "expert"), axis=0, tiled=True),
            lax.all_gather(gain_moe[layer_number], ("dp", "expert"), axis=0, tiled=True),
            lax.all_gather(w_router[layer_number], ("dp", "expert"), axis=0, tiled=True),
        )
        expert_w = (
            lax.all_gather(w_in[layer_number], "dp", axis=0, tiled=True),
            lax.all_gather(w_out[layer_number], "dp", axis=0, tiled=True),
        )
        all_keys, all_values = (
            lax.all_gather(key_matrix_rows, "expert", axis=0, tiled=True),
            lax.all_gather(value_matrix_rows, "expert", axis=0, tiled=True),
        )
        gate_grad = jnp.sum(slot_out.astype(jnp.float32) * grad_resid[:, None, :], axis=-1)
        slot_grad = (
            (gate_probs[:, :, None] * grad_resid[:, None, :])
            .astype(jnp.bfloat16)
            .reshape(total_rows * TOP, model_width)
        )
        grad_rows = jnp.where(filled[:, None], slot_grad[source], zero_bf)
        grad_rows = grad_rows.reshape(group_count, experts_local, capacity, model_width)
        grad_arrived = lax.all_to_all(grad_rows, "expert", split_axis=0, concat_axis=0, tiled=True)
        gate_half = gate_up[..., :FF]
        up_half = gate_up[..., FF:]
        sigmoid_vals = jax.nn.sigmoid(gate_half)
        silu_vals = gate_half * sigmoid_vals
        hidden_act = (silu_vals * up_half).astype(jnp.bfloat16)
        act_grad = jnp.einsum(
            "secd,fed->secf", grad_arrived, expert_w[1], preferred_element_type=jnp.float32
        )
        gate_part = act_grad * up_half * sigmoid_vals * (1.0 + gate_half * (1.0 - sigmoid_vals))
        gate_up_grad = jnp.concatenate([gate_part, act_grad * silu_vals], axis=-1).astype(
            jnp.bfloat16
        )
        input_grad = jnp.einsum(
            "secf,def->secd", gate_up_grad, expert_w[0], preferred_element_type=jnp.float32
        ).astype(jnp.bfloat16)
        returned_grad = lax.all_to_all(
            input_grad, "expert", split_axis=0, concat_axis=0, tiled=True
        )
        grad_lists[7][layer_number] = lax.psum_scatter(
            jnp.einsum(
                "secd,secf->def", arrived, gate_up_grad, preferred_element_type=jnp.float32
            ).astype(jnp.bfloat16),
            "dp",
            scatter_dimension=0,
            tiled=True,
        ).astype(jnp.float32)
        grad_lists[8][layer_number] = lax.psum_scatter(
            jnp.einsum(
                "secf,secd->fed", hidden_act, grad_arrived, preferred_element_type=jnp.float32
            ).astype(jnp.bfloat16),
            "dp",
            scatter_dimension=0,
            tiled=True,
        ).astype(jnp.float32)
        slot_back = returned_grad.reshape(expert_count * capacity, model_width)[target].reshape(
            total_rows, TOP, model_width
        )
        normed_two_grad = jnp.sum(slot_back.astype(jnp.float32), axis=1)
        gate_inner = jnp.sum(gate_probs * gate_grad, axis=-1, keepdims=True)
        chosen_grad = gate_probs * (gate_grad - gate_inner)
        route_hot = (
            route[:, :, None] == jnp.arange(expert_count, dtype=jnp.int32)[None, None, :]
        ).astype(jnp.float32)
        logit_grad = jnp.sum(route_hot * chosen_grad[:, :, None], axis=1)
        router_f = dense_w[6].astype(jnp.float32)
        normed_two_grad = normed_two_grad + jnp.einsum(
            "re,de->rd", logit_grad, router_f, precision=top_precision
        )
        router_grad = jnp.einsum(
            "rd,re->de", normed_two.astype(jnp.float32), logit_grad, precision=top_precision
        )
        gain_m = dense_w[5].astype(jnp.float32)
        norm_two_back, gain_m_grad = norm_back(after_attn, gain_m, normed_two_grad)
        mid_grad = grad_resid + norm_two_back
        out_grad = mid_grad.astype(jnp.bfloat16)
        output_grad = jnp.einsum("rq,rd->qd", attn, out_grad, preferred_element_type=jnp.float32)
        attn_grad = (
            jnp.einsum("rd,qd->rq", out_grad, dense_w[4], preferred_element_type=jnp.float32)
            .astype(jnp.bfloat16)
            .reshape(total_rows, QUERY_HEADS, HEAD_DIM)
        )
        query_grads = []
        key_grads = []
        value_grads = []
        for group_of_heads in range(KEY_VALUE_HEADS):
            scores, grouped_q = score_block(query_rows, all_keys, group_of_heads)
            grouped_do = attn_grad[
                :, group_of_heads * heads_per_group : (group_of_heads + 1) * heads_per_group, :
            ]
            probs = jnp.exp(scores - log_totals[group_of_heads])
            prob_bf = probs.astype(jnp.bfloat16)
            prob_grad = jnp.einsum(
                "rgd,kd->grk",
                grouped_do,
                all_values[:, group_of_heads, :],
                preferred_element_type=jnp.float32,
            )
            row_dot = jnp.sum(probs * prob_grad, axis=-1, keepdims=True)
            score_grad = (probs * (prob_grad - row_dot)).astype(jnp.bfloat16)
            query_grads.append(
                jnp.einsum(
                    "grk,kd->rgd",
                    score_grad,
                    all_keys[:, group_of_heads, :],
                    preferred_element_type=jnp.float32,
                )
                * score_scale
            )
            key_grads.append(
                jnp.einsum("grk,rgd->kd", score_grad, grouped_q, preferred_element_type=jnp.float32)
                * score_scale
            )
            value_grads.append(
                jnp.einsum("grk,rgd->kd", prob_bf, grouped_do, preferred_element_type=jnp.float32)
            )
        key_sum, value_total_sum = (
            lax.psum_scatter(
                jnp.stack(key_grads, axis=1).astype(jnp.bfloat16),
                "expert",
                scatter_dimension=0,
                tiled=True,
            ).astype(jnp.float32),
            lax.psum_scatter(
                jnp.stack(value_grads, axis=1).astype(jnp.bfloat16),
                "expert",
                scatter_dimension=0,
                tiled=True,
            ).astype(jnp.float32),
        )
        query_grad = (
            rotate(jnp.concatenate(query_grads, axis=1), cos_table, sin_table, -1.0)
            .astype(jnp.bfloat16)
            .reshape(total_rows, QUERY_HEADS * HEAD_DIM)
        )
        key_grad = (
            rotate(key_sum, cos_table, sin_table, -1.0)
            .astype(jnp.bfloat16)
            .reshape(total_rows, KEY_VALUE_HEADS * HEAD_DIM)
        )
        value_rows_gradient = value_total_sum.astype(jnp.bfloat16).reshape(
            total_rows, KEY_VALUE_HEADS * HEAD_DIM
        )
        normed_grad = jnp.einsum(
            "rq,dq->rd", query_grad, dense_w[1], preferred_element_type=jnp.float32
        )
        normed_grad = normed_grad + jnp.einsum(
            "rq,dq->rd", key_grad, dense_w[2], preferred_element_type=jnp.float32
        )
        normed_grad = normed_grad + jnp.einsum(
            "rq,dq->rd", value_rows_gradient, dense_w[3], preferred_element_type=jnp.float32
        )
        query_w_grad = jnp.einsum(
            "rd,rq->dq", norm_result, query_grad, preferred_element_type=jnp.float32
        )
        key_w_grad = jnp.einsum(
            "rd,rq->dq", norm_result, key_grad, preferred_element_type=jnp.float32
        )
        value_w_grad = jnp.einsum(
            "rd,rq->dq", norm_result, value_rows_gradient, preferred_element_type=jnp.float32
        )
        gain_a = dense_w[0].astype(jnp.float32)
        norm_one_back, gain_a_grad = norm_back(resid_in, gain_a, normed_grad)
        grad_resid = mid_grad + norm_one_back
        shares = (
            lax.psum_scatter(gain_a_grad, ("dp", "expert"), scatter_dimension=0, tiled=True),
            lax.psum_scatter(query_w_grad, ("dp", "expert"), scatter_dimension=0, tiled=True),
            lax.psum_scatter(key_w_grad, ("dp", "expert"), scatter_dimension=0, tiled=True),
            lax.psum_scatter(value_w_grad, ("dp", "expert"), scatter_dimension=0, tiled=True),
            lax.psum_scatter(output_grad, ("dp", "expert"), scatter_dimension=0, tiled=True),
            lax.psum_scatter(gain_m_grad, ("dp", "expert"), scatter_dimension=0, tiled=True),
            lax.psum_scatter(router_grad, ("dp", "expert"), scatter_dimension=0, tiled=True),
        )
        for member in range(7):
            grad_lists[member][layer_number] = shares[member]
    stacked = [jnp.stack(grad_lists[member], axis=0) for member in range(9)]
    return (
        block_out,
        grad_resid,
        stacked[0],
        stacked[1],
        stacked[2],
        stacked[3],
        stacked[4],
        stacked[5],
        stacked[6],
        stacked[7],
        stacked[8],
    )


def solution(mesh):
    in_specs = (
        P(("dp", "expert"), None),
        P(("dp", "expert"), None),
        P(None, ("dp", "expert"), None),
        P(None, ("dp", "expert")),
        P(None, ("dp", "expert"), None),
        P(None, ("dp", "expert"), None),
        P(None, ("dp", "expert"), None),
        P(None, ("dp", "expert"), None),
        P(None, ("dp", "expert")),
        P(None, ("dp", "expert"), None),
        P(None, "dp", "expert", None),
        P(None, "dp", "expert", None),
    )
    out_specs = (
        P(("dp", "expert"), None),
        P(("dp", "expert"), None),
        P(None, ("dp", "expert")),
        P(None, ("dp", "expert"), None),
        P(None, ("dp", "expert"), None),
        P(None, ("dp", "expert"), None),
        P(None, ("dp", "expert"), None),
        P(None, ("dp", "expert")),
        P(None, ("dp", "expert"), None),
        P(None, "dp", "expert", None),
        P(None, "dp", "expert", None),
    )
    return jax.shard_map(body, mesh=mesh, in_specs=in_specs, out_specs=out_specs, check_vma=False)
```

profile of v0, /device:TPU:0, one launch (start us, length us, event | category | flops | bytes accessed | tf_op | source)
XLA Modules:
  0.0 1256.5 jit_solution(12556006223137634985)
XLA Ops:
  19.5 42.3 %all-reduce.5 = (bf16[1536]{0:T(1024)(128)(2,1)S(1)}, bf16[1536]{0:T(1024)(128)(2,1)S(1)}) all-reduce(bf16[1536]{0:T(1024)(128)(2,1)S(1)} %dynamic-update-slice, bf16[1536]{0:T(1024)(128)(2,1)S(1)} %dynamic-update-slice.1), channel_id=2, replica_groups=mesh['dp'=4,'expert'=8] {'dp','expert'}, use_global_device_ids=true, to_apply=%add | all-reduce | flops 3072 | bytes 12288
  63.0 43.9 %all-gather.2 = bf16[1,1536,256]{2,1,0:T(8,128)(2,1)S(1)} all-gather(bf16[1,48,256]{2,1,0:T(8,128)(2,1)S(1)} %copy-done.62), channel_id=4, replica_groups=mesh['dp'=4,'expert'=8] {'dp','expert'}, dimensions={1}, use_global_device_ids=true | all-gather | bytes 811008 | tf_op jit(solution)/shard_map/all_gather | solution.py:115
  109.5 9.9 all_gather.48
  120.2 40.7 %all-gather.1 = bf16[1,1536,256]{2,1,0:T(8,128)(2,1)S(1)} all-gather(bf16[1,48,256]{2,1,0:T(8,128)(2,1)S(1)} %copy-done.63), channel_id=3, replica_groups=mesh['dp'=4,'expert'=8] {'dp','expert'}, dimensions={1}, use_global_device_ids=true | all-gather | bytes 811008 | tf_op jit(solution)/shard_map/all_gather | solution.py:116
  162.3 10.7 all_gather.46
  177.5 43.9 %all-gather.6 = bf16[1,1536,8]{2,0,1:T(2,128)(2,1)S(1)} all-gather(bf16[1,48,8]{2,0,1:T(2,128)(2,1)S(1)} %copy.152), channel_id=8, replica_groups=mesh['dp'=4,'expert'=8] {'dp','expert'}, dimensions={1}, use_global_device_ids=true | all-gather | bytes 25344 | tf_op jit(solution)/shard_map/all_gather | solution.py:119
  261.6 28.8 %all-to-all-done = bf16[8,1,96,1536]{3,2,1,0:T(8,128)(2,1)S(1)} async-done(((bf16[8,1,96,1536]{3,2,1,0:T(8,128)(2,1)}), bf16[8,1,96,1536]{3,2,1,0:T(8,128)(2,1)S(1)}, u32[]{:S(2)}, u32[]{:S(2)}) %all-to-all-start) | async-done | bytes 2359328 | tf_op jit(solution)/shard_map/all_to_all | solution.py:173
  295.0 7.8 fusion.13
  302.8 17.4 %all-gather.20.cloned.1.call-done = bf16[1,768,1,1536]{3,1,2,0:T(8,128)(2,1)} async-done(((bf16[1,192,1,1536]{3,1,2,0:T(8,128)(2,1)}), bf16[1,768,1,1536]{3,1,2,0:T(8,128)(2,1)}) %all-gather.20.cloned.1.call-update) | async-done | bytes 2359312 | tf_op jit(solution)/shard_map/all_gather | solution.py:123
  324.4 7.6 fusion.80
  346.2 23.9 %all-to-all-done.3 = bf16[8,1,96,1536]{3,2,1,0:T(8,128)(2,1)S(1)} async-done(((bf16[8,1,96,1536]{3,2,1,0:T(8,128)(2,1)}), bf16[8,1,96,1536]{3,2,1,0:T(8,128)(2,1)S(1)}, u32[]{:S(2)}, u32[]{:S(2)}) %all-to-all-start.3) | async-done | bytes 2359328 | tf_op jit(solution)/shard_map/all_to_all | solution.py:285
  384.0 20.0 %all-to-all-done.1 = bf16[8,1,96,1536]{3,2,1,0:T(8,128)(2,1)} async-done(((bf16[8,1,96,1536]{3,2,1,0:T(8,128)(2,1)}), bf16[8,1,96,1536]{3,2,1,0:T(8,128)(2,1)}, u32[]{:S(2)}, u32[]{:S(2)}) %all-to-all-start.1) | async-done | bytes 2359328 | tf_op jit(solution)/shard_map/all_to_all | solution.py:185
  404.0 6.5 gather_fusion.1
  460.0 6.9 fusion
  467.0 6.7 copy.202
  473.7 11.7 reduce-scatter.16.cloned.1.call-done
  488.4 34.4 %reduce-scatter.18.cloned.1.call-done = bf16[128,2,128]{2,0,1:T(8,128)(2,1)} async-done(((bf16[1024,2,128]{2,0,1:T(8,128)(2,1)}), bf16[128,2,128]{2,0,1:T(8,128)(2,1)}) %reduce-scatter.18.cloned.1.call-update) | async-done | bytes 65552 | tf_op jit(solution)/shard_map/reduce_scatter | solution.py:372
  545.1 78.3 %reduce-scatter.28.cloned.1.call-done = f32[48,8]{1,0:T(8,128)} async-done(((f32[1536,8]{1,0:T(8,128)}), f32[48,8]{1,0:T(8,128)}) %reduce-scatter.28.cloned.1.call-update) | async-done | bytes 1552
  627.4 43.6 %all-reduce.4 = (f32[1536]{0:T(1024)S(1)}, f32[1536]{0:T(1024)S(1)}) all-reduce(f32[1536]{0:T(1024)S(1)} %get-tuple-element.70, f32[1536]{0:T(1024)S(1)} %copy-done.58), channel_id=13, replica_groups=mesh['dp'=4,'expert'=8] {'dp','expert'}, use_global_device_ids=true, to_apply=%region_24.25.clone | all-reduce | flops 3072 | bytes 24576
  677.8 83.7 %reduce-scatter.30.cloned.1.call-done = bf16[384,1536]{1,0:T(8,128)(2,1)} async-done(((bf16[1536,1536]{1,0:T(8,128)(2,1)}), bf16[384,1536]{1,0:T(8,128)(2,1)}) %reduce-scatter.30.cloned.1.call-update) | async-done | bytes 1179664
  767.6 97.1 %reduce-scatter.22.cloned.1.call-done = f32[48,256]{1,0:T(8,128)} async-done(((f32[1536,256]{1,0:T(8,128)}), f32[48,256]{1,0:T(8,128)}) %reduce-scatter.22.cloned.1.call-update) | async-done | bytes 49168 | tf_op jit(solution)/shard_map/reduce_scatter | solution.py:416
  864.8 101.9 %reduce-scatter.24.cloned.1.call-done = f32[48,256]{1,0:T(8,128)} async-done(((f32[1536,256]{1,0:T(8,128)}), f32[48,256]{1,0:T(8,128)}) %reduce-scatter.24.cloned.1.call-update) | async-done | bytes 49168 | tf_op jit(solution)/shard_map/reduce_scatter | solution.py:417
  966.6 140.9 %reduce-scatter.20.cloned.1.call-done = f32[48,1536]{1,0:T(8,128)} async-done(((f32[1536,1536]{1,0:T(8,128)}), f32[48,1536]{1,0:T(8,128)}) %reduce-scatter.20.cloned.1.call-update) | async-done | bytes 294928 | tf_op jit(solution)/shard_map/reduce_scatter | solution.py:415
  1107.5 142.2 %reduce-scatter.26.cloned.1.call-done = f32[48,1536]{1,0:T(8,128)} async-done(((f32[1536,1536]{1,0:T(8,128)}), f32[48,1536]{1,0:T(8,128)}) %reduce-scatter.26.cloned.1.call-update) | async-done | bytes 294928 | tf_op jit(solution)/shard_map/reduce_scatter | solution.py:418
  (326 shorter events, 190.3 us)
Async XLA Ops:
  7.2 100.6 %copy-start.5 = (bf16[128,1536]{1,0:T(8,128)(2,1)S(1)}, bf16[128,1536]{1,0:T(8,128)(2,1)}, u32[]{:S(2)}) copy-start(bf16[128,1536]{1,0:T(8,128)(2,1)} %param.12) | copy-start | bytes 1179652
  7.2 216.9 %all-gather.14.cloned.1.call-start = ((), (), s32[]{:S(2)}) async-start(), calls=%async_computation.19 | async-start | bytes 4866048 | tf_op jit(solution)/shard_map/all_gather | solution.py:114
  7.9 226.7 %all-gather.16.cloned.1.call-start = ((), (), s32[]{:S(2)}) async-start(), calls=%async_computation.20 | async-start | bytes 4866048 | tf_op jit(solution)/shard_map/all_gather | solution.py:117
  8.7 286.3 %all-gather.18.cloned.1.call-start = ((), (), s32[]{:S(2)}) async-start(), calls=%async_computation.21 | async-start | bytes 5898240 | tf_op jit(solution)/shard_map/all_gather | solution.py:122
  11.5 98.0 %copy-start.27 = (s32[1,128,4]{2,1,0:T(8,128)}, s32[1,128,4]{2,1,0:T(8,128)S(1)}, u32[]{:S(2)}) copy-start(s32[1,128,4]{2,1,0:T(8,128)S(1)} %copy.151) | copy-start | bytes 6148
  12.3 94.6 %copy-start.64 = (s32[512]{0:T(512)}, s32[512]{0:T(512)S(1)}, u32[]{:S(2)}) copy-start(s32[512]{0:T(512)S(1)} %eq.38) | copy-start | bytes 6148
  62.9 57.3 %copy-start.63 = (bf16[1,48,256]{2,1,0:T(8,128)(2,1)S(1)}, bf16[1,48,256]{2,1,0:T(8,128)(2,1)}, u32[]{:S(2)}) copy-start(bf16[1,48,256]{2,1,0:T(8,128)(2,1)} %param.18) | copy-start | bytes 73732
  63.0 98.0 %copy-start.59 = (f32[128]{0:T(128)}, f32[128]{0:T(128)S(1)}, u32[]{:S(2)}) copy-start(f32[128]{0:T(128)S(1)} %add_rsqrt_fusion.1) | copy-start | bytes 1540
  257.4 33.0 %all-to-all-start = ((bf16[8,1,96,1536]{3,2,1,0:T(8,128)(2,1)}), bf16[8,1,96,1536]{3,2,1,0:T(8,128)(2,1)S(1)}, u32[]{:S(2)}, u32[]{:S(2)}) async-start(bf16[8,1,96,1536]{3,2,1,0:T(8,128)(2,1)} %get-tuple-element.99), calls=%async_computation | async-start | bytes 4718592 | tf_op jit(solution)/shard_map/all_to_all | solution.py:173
  261.0 59.2 %all-gather.20.cloned.1.call-start = ((), (), s32[]{:S(2)}) async-start(), calls=%async_computation.22 | async-start | bytes 2949120 | tf_op jit(solution)/shard_map/all_gather | solution.py:123
  290.4 34.1 %all-to-all-start.2 = ((bf16[8,1,96,1536]{3,2,1,0:T(8,128)(2,1)}), bf16[8,1,96,1536]{3,2,1,0:T(8,128)(2,1)}, u32[]{:S(2)}, u32[]{:S(2)}) async-start(bf16[8,1,96,1536]{3,2,1,0:T(8,128)(2,1)} %get-tuple-element.98), calls=%async_computation.2 | async-start | bytes 4718592 | tf_op jit(solution)/shard_map/all_to_all | solution.py:269
  337.1 33.0 %all-to-all-start.3 = ((bf16[8,1,96,1536]{3,2,1,0:T(8,128)(2,1)}), bf16[8,1,96,1536]{3,2,1,0:T(8,128)(2,1)S(1)}, u32[]{:S(2)}, u32[]{:S(2)}) async-start(bf16[8,1,96,1536]{3,2,1,0:T(8,128)(2,1)} %fusion.26), calls=%async_computation.3 | async-start | bytes 4718592 | tf_op jit(solution)/shard_map/all_to_all | solution.py:285
  370.2 33.8 %all-to-all-start.1 = ((bf16[8,1,96,1536]{3,2,1,0:T(8,128)(2,1)}), bf16[8,1,96,1536]{3,2,1,0:T(8,128)(2,1)}, u32[]{:S(2)}, u32[]{:S(2)}) async-start(bf16[8,1,96,1536]{3,2,1,0:T(8,128)(2,1)} %fusion.25), calls=%async_computation.1 | async-start | bytes 4718592 | tf_op jit(solution)/shard_map/all_to_all | solution.py:185
  374.5 110.9 %reduce-scatter.16.cloned.1.call-start = ((), (), s32[]{:S(2)}) async-start(), calls=%async_computation.13 | async-start | bytes 589824 | tf_op jit(solution)/shard_map/reduce_scatter | solution.py:366
  446.8 76.0 %reduce-scatter.18.cloned.1.call-start = ((), (), s32[]{:S(2)}) async-start(), calls=%async_computation.14 | async-start | bytes 589824 | tf_op jit(solution)/shard_map/reduce_scatter | solution.py:372
  450.4 173.0 %reduce-scatter.28.cloned.1.call-start = ((), (), s32[]{:S(2)}) async-start(), calls=%async_computation.23 | async-start | bytes 811008
  451.9 222.4 %reduce-scatter.32.cloned.1.call-start = ((), (), s32[]{:S(2)}) async-start(), calls=%async_computation.25 | async-start | bytes 2949120
  458.4 303.1 %reduce-scatter.30.cloned.1.call-start = ((), (), s32[]{:S(2)}) async-start(), calls=%async_computation.24 | async-start | bytes 5898240
  473.7 391.1 %reduce-scatter.22.cloned.1.call-start = ((), (), s32[]{:S(2)}) async-start(), calls=%async_computation.16 | async-start | bytes 1622016 | tf_op jit(solution)/shard_map/reduce_scatter | solution.py:416
  488.4 478.3 %reduce-scatter.24.cloned.1.call-start = ((), (), s32[]{:S(2)}) async-start(), calls=%async_computation.17 | async-start | bytes 1622016 | tf_op jit(solution)/shard_map/reduce_scatter | solution.py:417
  526.1 581.5 %reduce-scatter.20.cloned.1.call-start = ((), (), s32[]{:S(2)}) async-start(), calls=%async_computation.15 | async-start | bytes 9732096 | tf_op jit(solution)/shard_map/reduce_scatter | solution.py:415
  534.7 715.0 %reduce-scatter.26.cloned.1.call-start = ((), (), s32[]{:S(2)}) async-start(), calls=%async_computation.18 | async-start | bytes 9732096 | tf_op jit(solution)/shard_map/reduce_scatter | solution.py:418
  541.0 83.8 %copy-start.31 = (bf16[1,1536,256]{2,1,0:T(8,128)(2,1)S(1)}, bf16[1,1536,256]{2,1,0:T(8,128)(2,1)}, u32[]{:S(2)}) copy-start(bf16[1,1536,256]{2,1,0:T(8,128)(2,1)} %copy-done.30) | copy-start | bytes 2359300
  545.1 81.0 %copy-start.33 = (bf16[1,1536,256]{2,1,0:T(8,128)(2,1)S(1)}, bf16[1,1536,256]{2,1,0:T(8,128)(2,1)}, u32[]{:S(2)}) copy-start(bf16[1,1536,256]{2,1,0:T(8,128)(2,1)} %copy-done.32) | copy-start | bytes 2359300
  (69 other events, 429.1 us)
Sparse Core Ops, SparseCore 0:
  10.9 67.6 all-gather.13
  81.5 67.2 all-gather.15
  150.4 91.7 all-gather.17
  263.1 57.1 all-gather.19
  447.0 38.4 reduce-scatter.15
  488.7 34.1 reduce-scatter.17
  527.9 95.4 reduce-scatter.27
  626.3 47.9 reduce-scatter.31
  676.6 84.7 reduce-scatter.29
  767.1 97.5 reduce-scatter.21
  870.6 96.0 reduce-scatter.23
  973.0 134.5 reduce-scatter.19
  1115.0 134.6 reduce-scatter.25
where the time goes:
time: 1260 us
  waiting for transfers between devices  788 us (63%)
  blocking collectives  235 us (19%)
  matrix products  85.5 us (7%)
  local copies, waits for them, and re-layouts  78.2 us (6%)
  other arithmetic  37.5 us (3%)
  starting transfers between devices  16.7 us (1%)
  between operations  15.2 us (1%)
    unnamed x16, waiting for transfers between devices  166 us
    reduce_scatter x1, waiting for transfers between devices, body(): lax.psum_scatter(output_grad, ('dp', 'expert'), scatter_dimension=0, tile...  142 us
    reduce_scatter x1, waiting for transfers between devices, body(): lax.psum_scatter(query_w_grad, ('dp', 'expert'), scatter_dimension=0, til...  141 us
    reduce_scatter x1, waiting for transfers between devices, body(): lax.psum_scatter(value_w_grad, ('dp', 'expert'), scatter_dimension=0, til...  102 us
    reduce_scatter x1, waiting for transfers between devices, body(): lax.psum_scatter(key_w_grad, ('dp', 'expert'), scatter_dimension=0, tiled...  97.1 us
    unnamed x2, blocking collectives  85.9 us
    all_gather x1, blocking collectives, body(): lax.all_gather(key_weight[layer_number], ('dp', 'expert'), axis=0, tiled=...  43.9 us
    all_gather x1, blocking collectives, body(): lax.all_gather(w_router[layer_number], ('dp', 'expert'), axis=0, tiled=True)  43.9 us
  transfers between devices with their start and end apart: 17, of which 14 were waited for; matrix products, arithmetic and copies ran while one was open for 11% of the time, Pallas kernels for 0%

commit v1 on v0

--- a/solution.py
+++ b/solution.py
@@ -1,7 +1,13 @@
+import functools
+
 import jax
 import jax.numpy as jnp
 from jax import lax
+from jax.experimental import pallas as pl
+from jax.experimental.pallas import tpu as pltpu
 from jax.sharding import PartitionSpec as P
+
+MESH = pl.DeviceIdType.MESH
 
 QUERY_HEADS = 12
 KEY_VALUE_HEADS = 2
@@ -62,6 +68,100 @@
     )
     filled = source < slot_total
     return (target, jnp.minimum(source, slot_total - 1), filled)
+
+
+def gather_kernel(shard_ref, full_ref, z_send, z_recv, p_send, p_recv, s_send, s_recv, own_sem):
+    plane = lax.axis_index("dp")
+    member = lax.axis_index("expert")
+    sibling = lax.bitwise_xor(member, 1)
+
+    barrier = pltpu.get_barrier_semaphore()
+    for step in (1, 2, 3):
+        pl.semaphore_signal(
+            barrier, inc=1, device_id=(lax.bitwise_xor(plane, step), member), device_id_type=MESH
+        )
+    for step in (1, 2, 4, 6):
+        pl.semaphore_signal(
+            barrier, inc=1, device_id=(plane, lax.bitwise_xor(member, step)), device_id_type=MESH
+        )
+    own = pltpu.make_async_copy(shard_ref, full_ref.at[plane, member], own_sem.at[0])
+    own.start()
+    pl.semaphore_wait(barrier, 7)
+
+    def z_copy(step):
+        return pltpu.make_async_remote_copy(
+            src_ref=shard_ref,
+            dst_ref=full_ref.at[plane, member],
+            send_sem=z_send.at[step],
+            recv_sem=z_recv.at[step],
+            device_id=(lax.bitwise_xor(plane, step), member),
+            device_id_type=MESH,
+        )
+
+    def plane_copy(step, chip):
+        block = full_ref.at[lax.bitwise_xor(plane, step), member]
+        return pltpu.make_async_remote_copy(
+            src_ref=block,
+            dst_ref=block,
+            send_sem=p_send.at[step, chip],
+            recv_sem=p_recv.at[step, chip],
+            device_id=(plane, lax.bitwise_xor(member, 2 * chip)),
+            device_id_type=MESH,
+        )
+
+    def sibling_copy(step, chip):
+        block = full_ref.at[lax.bitwise_xor(plane, step), lax.bitwise_xor(member, 2 * chip)]
+        return pltpu.make_async_remote_copy(
+            src_ref=block,
+            dst_ref=block,
+            send_sem=s_send.at[step, chip],
+            recv_sem=s_recv.at[step, chip],
+            device_id=(plane, sibling),
+            device_id_type=MESH,
+        )
+
+    for step in (1, 2, 3):
+        z_copy(step).start()
+    own.wait()
+    for step in range(4):
+        if step:
+            z_copy(step).wait_recv()
+        for chip in (1, 2, 3):
+            plane_copy(step, chip).start()
+        sibling_copy(step, 0).start()
+    for step in range(4):
+        for chip in (1, 2, 3):
+            plane_copy(step, chip).wait_recv()
+            sibling_copy(step, chip).start()
+    for step in range(4):
+        for chip in range(4):
+            sibling_copy(step, chip).wait()
+            if chip:
+                plane_copy(step, chip).wait_send()
+        if step:
+            z_copy(step).wait_send()
+
+
+def gather_dense(shard):
+    rows, columns = shard.shape
+    planes, members = lax.axis_size("dp"), lax.axis_size("expert")
+    full = pl.pallas_call(
+        gather_kernel,
+        out_shape=jax.ShapeDtypeStruct((planes, members, rows, columns), shard.dtype),
+        in_specs=[pl.BlockSpec(memory_space=pl.ANY)],
+        out_specs=pl.BlockSpec(memory_space=pl.ANY),
+        scratch_shapes=[
+            pltpu.SemaphoreType.DMA((4,)),
+            pltpu.SemaphoreType.DMA((4,)),
+            pltpu.SemaphoreType.DMA((4, 4)),
+            pltpu.SemaphoreType.DMA((4, 4)),
+            pltpu.SemaphoreType.DMA((4, 4)),
+            pltpu.SemaphoreType.DMA((4, 4)),
+            pltpu.SemaphoreType.DMA((1,)),
+        ],
+        compiler_params=pltpu.CompilerParams(collective_id=0, has_side_effects=True),
+    )(shard)
+    return full.reshape(planes * members * rows, columns)
 
 
 def body(
@@ -109,15 +209,31 @@
 
     residual = tokens.astype(jnp.float32)
     layer_number = 0
-    dense_w = (
-        lax.all_gather(gain_attn[layer_number], ("dp", "expert"), axis=0, tiled=True),
-        lax.all_gather(w_query[layer_number], ("dp", "expert"), axis=0, tiled=True),
-        lax.all_gather(key_weight[layer_number], ("dp", "expert"), axis=0, tiled=True),
-        lax.all_gather(value_weight[layer_number], ("dp", "expert"), axis=0, tiled=True),
-        lax.all_gather(w_output[layer_number], ("dp", "expert"), axis=0, tiled=True),
-        lax.all_gather(gain_moe[layer_number], ("dp", "expert"), axis=0, tiled=True),
-        lax.all_gather(w_router[layer_number], ("dp", "expert"), axis=0, tiled=True),
-    )
+    shards = [
+        gain_attn[layer_number][:, None],
+        w_query[layer_number],
+        key_weight[layer_number],
+        value_weight[layer_number],
+        w_output[layer_number],
+        gain_moe[layer_number][:, None],
+        w_router[layer_number],
+    ]
+    widths = [part.shape[1] for part in shards]
+    if lax.axis_size("dp") == 4 and group_count == 8 and w_query.shape[1] % 16 == 0:
+        order = (1, 4, 2, 3, 0, 5, 6)
+        total_width = sum(widths)
+        padding = jnp.zeros((w_query.shape[1], -total_width % 128), jnp.bfloat16)
+        whole = gather_dense(jnp.concatenate([shards[i] for i in order] + [padding], axis=1))
+        dense_w = [None] * 7
+        start = 0
+        for i in order:
+            dense_w[i] = whole[:, start : start + widths[i]]
+            start += widths[i]
+    else:
+        dense_w = [lax.all_gather(part, ("dp", "expert"), axis=0, tiled=True) for part in shards]
+    dense_w[0] = dense_w[0][:, 0]
+    dense_w[5] = dense_w[5][:, 0]
+    dense_w = tuple(dense_w)
     expert_w = (
         lax.all_gather(w_in[layer_number], "dp", axis=0, tiled=True),
         lax.all_gather(w_out[layer_number], "dp", axis=0, tiled=True),
@@ -241,19 +357,6 @@
             dense_w,
             expert_w,
         ) = saved_layers[layer_number]
-        dense_w = (
-            lax.all_gather(gain_attn[layer_number], ("dp", "expert"), axis=0, tiled=True),
-            lax.all_gather(w_query[layer_number], ("dp", "expert"), axis=0, tiled=True),
-            lax.all_gather(key_weight[layer_number], ("dp", "expert"), axis=0, tiled=True),
-            lax.all_gather(value_weight[layer_number], ("dp", "expert"), axis=0, tiled=True),
-            lax.all_gather(w_output[layer_number], ("dp", "expert"), axis=0, tiled=True),
-            lax.all_gather(gain_moe[layer_number], ("dp", "expert"), axis=0, tiled=True),
-            lax.all_gather(w_router[layer_number], ("dp", "expert"), axis=0, tiled=True),
-        )
-        expert_w = (
-            lax.all_gather(w_in[layer_number], "dp", axis=0, tiled=True),
-            lax.all_gather(w_out[layer_number], "dp", axis=0, tiled=True),
-        )
         all_keys, all_values = (
             lax.all_gather(key_matrix_rows, "expert", axis=0, tiled=True),
             lax.all_gather(value_matrix_rows, "expert", axis=0, tiled=True),
@@ -410,14 +513,25 @@
         gain_a = dense_w[0].astype(jnp.float32)
         norm_one_back, gain_a_grad = norm_back(resid_in, gain_a, normed_grad)
         grad_resid = mid_grad + norm_one_back
+        partial = jnp.concatenate(
+            [query_w_grad, output_grad, key_w_grad, value_w_grad], axis=1
+        ).astype(jnp.bfloat16)
+        small = jnp.concatenate([gain_a_grad[:, None], gain_m_grad[:, None], router_grad], axis=1)
+        both = ("dp", "expert")
+        summed = lax.psum_scatter(partial, both, scatter_dimension=0, tiled=True)
+        summed = summed.astype(jnp.float32)
+        small = lax.psum_scatter(small, both, scatter_dimension=0, tiled=True)
+        q_end = query_w_grad.shape[1]
+        o_end = q_end + output_grad.shape[1]
+        k_end = o_end + key_w_grad.shape[1]
         shares = (
-            lax.psum_scatter(gain_a_grad, ("dp", "expert"), scatter_dimension=0, tiled=True),
-            lax.psum_scatter(query_w_grad, ("dp", "expert"), scatter_dimension=0, tiled=True),
-            lax.psum_scatter(key_w_grad, ("dp", "expert"), scatter_dimension=0, tiled=True),
-            lax.psum_scatter(value_w_grad, ("dp", "expert"), scatter_dimension=0, tiled=True),
-            lax.psum_scatter(output_grad, ("dp", "expert"), scatter_dimension=0, tiled=True),
-            lax.psum_scatter(gain_m_grad, ("dp", "expert"), scatter_dimension=0, tiled=True),
-            lax.psum_scatter(router_grad, ("dp", "expert"), scatter_dimension=0, tiled=True),
+            small[:, 0],
+            summed[:, :q_end],
+            summed[:, o_end:k_end],
+            summed[:, k_end:],
+            summed[:, q_end:o_end],
+            small[:, 1],
+            small[:, 2:],
         )
         for member in range(7):
             grad_lists[member][layer_number] = shares[member]

time: 1260 us -> 845 us (0.67)
  waiting for transfers between devices: 788 us -> 474 us
  blocking collectives: 235 us -> 21.3 us
  Pallas kernels: 0 us -> 83.5 us
  local copies, waits for them, and re-layouts: 78.2 us -> 101 us
    reduce_scatter x4 -> x0, waiting for transfers between devices: 482 us -> none  [the longest x1 142 us: body(): lax.psum_scatter(output_grad, ('dp', 'expert'), scatter_dimension=0, tile...]
    unnamed x16 -> x12, waiting for transfers between devices: 166 us -> 321 us
    all_gather x3 -> x0, blocking collectives: 129 us -> none  [the longest x1 43.9 us: body(): lax.all_gather(key_weight[layer_number], ('dp', 'expert'), axis=0, tiled=...]
    unnamed x2 -> x0, blocking collectives: 85.9 us -> none
    pallas_call x0 -> x1, Pallas kernels: none -> 83.5 us  [gather_dense(): pl.pallas_call(gather_kernel, out_shape=jax.ShapeDtypeStruct((planes, mem...]
    all_to_all x1, waiting for transfers between devices: 4.19 us -> 21.6 us  [body(): lax.all_to_all(grad_rows, 'expert', split_axis=0, concat_axis=0, tiled=True)]
    all_gather x1, waiting for transfers between devices: 17.4 us -> 0.01 us  [body(): lax.all_gather(w_out[layer_number], 'dp', axis=0, tiled=True)]
    unnamed x167 -> x134, local copies, waits for them, and re-layouts: 35.2 us -> 50.6 us
  transfers between devices with their start and end apart: 17 -> 12, of which waited for: 14 -> 10; matrix products, arithmetic and copies ran while one was open for 11% -> 18% of each run, Pallas kernels for 0% -> 10%
where the time goes in v1:
time: 845 us; the launch traced here: 838 us
  waiting for transfers between devices  474 us (56%)
  local copies, waits for them, and re-layouts  101 us (12%)
  Pallas kernels  83.5 us (10%)
  matrix products  83.5 us (10%)
  other arithmetic  42 us (5%)
  blocking collectives  21.3 us (3%)
  starting transfers between devices  17.1 us (2%)
  between operations  15.4 us (2%)
    unnamed x12, waiting for transfers between devices  321 us
    pallas_call x1, Pallas kernels, gather_dense(): pl.pallas_call(gather_kernel, out_shape=jax.ShapeDtypeStruct((planes, mem...  83.5 us
    unnamed x134, local copies, waits for them, and re-layouts  50.6 us
    reduce_scatter x1, waiting for transfers between devices, body(): lax.psum_scatter(jnp.stack(value_grads, axis=1).astype(jnp.bfloat16), 'ex...  34.6 us
    all_to_all x1, waiting for transfers between devices, body(): lax.all_to_all(send_rows, 'expert', split_axis=0, concat_axis=0, tiled=True)  28.6 us
    all_to_all x1, waiting for transfers between devices, body(): lax.all_to_all(input_grad, 'expert', split_axis=0, concat_axis=0, tiled=T...  23.8 us
    reduce_scatter x1, waiting for transfers between devices, body(): lax.psum_scatter(jnp.stack(key_grads, axis=1).astype(jnp.bfloat16), 'expe...  23.7 us
    all_to_all x1, waiting for transfers between devices, body(): lax.all_to_all(grad_rows, 'expert', split_axis=0, concat_axis=0, tiled=True)  21.6 us
  transfers between devices with their start and end apart: 12, of which 10 were waited for; matrix products, arithmetic and copies ran while one was open for 18% of the time, Pallas kernels for 10%

profile of v1, /device:TPU:0, one launch (start us, length us, event | category | flops | bytes accessed | tf_op | source)
XLA Modules:
  0.0 837.7 jit_solution(7367018594575708223)
XLA Ops:
  12.0 83.5 %shard_map.203 = bf16[4,8,48,3712]{3,2,1,0:T(8,128)(2,1)} custom-call(bf16[48,3712]{1,0:T(8,128)(2,1)} %concatenate.45.shard_ref), custom_call_target="tpu_custom_call" | custom-call | tf_op jit(solution)/shard_map/pallas_call | solution.py:148
  110.5 10.2 %all_gather.15 = bf16[1024,2,128]{2,0,1:T(8,128)(2,1)} all-gather(bf16[128,2,128]{2,0,1:T(8,128)(2,1)S(1)} %pad_maximum_fusion.11), channel_id=1, replica_groups=mesh['dp'=4,'expert'=8] {'expert'}, dimensions={0}, use_global_device_ids=true | all-gather | bytes 589824 | tf_op jit(solution)/shard_map/all_gather | solution.py:257
  121.6 11.1 %all_gather.14 = bf16[1024,2,128]{0,2,1:T(8,128)(2,1)} all-gather(bf16[128,2,128]{0,2,1:T(8,128)(2,1)S(1)} %bitcast.321), channel_id=1, replica_groups=mesh['dp'=4,'expert'=8] {'expert'}, dimensions={0}, use_global_device_ids=true | all-gather | bytes 589824 | tf_op jit(solution)/shard_map/all_gather | solution.py:258
  176.3 28.6 %all-to-all-done = bf16[8,1,96,1536]{3,2,1,0:T(8,128)(2,1)S(1)} async-done(((bf16[8,1,96,1536]{3,2,1,0:T(8,128)(2,1)}), bf16[8,1,96,1536]{3,2,1,0:T(8,128)(2,1)S(1)}, u32[]{:S(2)}, u32[]{:S(2)}) %all-to-all-start) | async-done | bytes 2359328 | tf_op jit(solution)/shard_map/all_to_all | solution.py:289
  209.6 7.8 fusion.13
  217.4 21.6 %all-to-all-done.2 = bf16[8,1,96,1536]{3,2,1,0:T(8,128)(2,1)} async-done(((bf16[8,1,96,1536]{3,2,1,0:T(8,128)(2,1)}), bf16[8,1,96,1536]{3,2,1,0:T(8,128)(2,1)}, u32[]{:S(2)}, u32[]{:S(2)}) %all-to-all-start.2) | async-done | bytes 2359328 | tf_op jit(solution)/shard_map/all_to_all | solution.py:372
  239.0 7.6 fusion.80
  246.6 5.1 fusion.26
  255.4 5.6 fusion.25
  260.9 23.8 %all-to-all-done.3 = bf16[8,1,96,1536]{3,2,1,0:T(8,128)(2,1)S(1)} async-done(((bf16[8,1,96,1536]{3,2,1,0:T(8,128)(2,1)}), bf16[8,1,96,1536]{3,2,1,0:T(8,128)(2,1)S(1)}, u32[]{:S(2)}, u32[]{:S(2)}) %all-to-all-start.3) | async-done | bytes 2359328 | tf_op jit(solution)/shard_map/all_to_all | solution.py:388
  298.6 20.0 %all-to-all-done.1 = bf16[8,1,96,1536]{3,2,1,0:T(8,128)(2,1)} async-done(((bf16[8,1,96,1536]{3,2,1,0:T(8,128)(2,1)}), bf16[8,1,96,1536]{3,2,1,0:T(8,128)(2,1)}, u32[]{:S(2)}, u32[]{:S(2)}) %all-to-all-start.1) | async-done | bytes 2359328 | tf_op jit(solution)/shard_map/all_to_all | solution.py:301
  318.6 6.5 gather_fusion.1
  329.3 5.8 multiply_reduce_fusion
  377.6 23.7 %reduce-scatter.15.cloned.1.call-done = bf16[128,2,128]{2,0,1:T(8,128)(2,1)} async-done(((bf16[1024,2,128]{2,0,1:T(8,128)(2,1)}), bf16[128,2,128]{2,0,1:T(8,128)(2,1)}) %reduce-scatter.15.cloned.1.call-update) | async-done | bytes 65552 | tf_op jit(solution)/shard_map/reduce_scatter | solution.py:469
  404.1 34.6 %reduce-scatter.17.cloned.1.call-done = bf16[128,2,128]{2,0,1:T(8,128)(2,1)} async-done(((bf16[1024,2,128]{2,0,1:T(8,128)(2,1)}), bf16[128,2,128]{2,0,1:T(8,128)(2,1)}) %reduce-scatter.17.cloned.1.call-update) | async-done | bytes 65552 | tf_op jit(solution)/shard_map/reduce_scatter | solution.py:475
  442.7 5.4 fusion.29
  452.5 8.4 %fusion = bf16[1536,1536]{0,1:T(8,128)(2,1)} fusion(bf16[8,1,96,1536]{3,2,1,0:T(8,128)(2,1)} %copy-done.25, bf16[8,96,768]{2,1,0:T(8,128)(2,1)} %copy-done.55, bf16[8,96,768]{2,1,0:T(8,128)(2,1)} %copy-done.54), kind=kOutput, calls=%fused_computation.10 | convolution fusion | flops 3630956544 | bytes 9437184 | tf_op jit(solution)/shard_map/secd,secf->def/dot_general | solution.py:392
  460.9 6.6 copy.200
  472.4 5.2 pad_maximum_fusion
  477.6 14.2 %copy.194 = bf16[1536,3584]{1,0:T(8,128)(2,1)} copy(bf16[1536,3584]{0,1:T(8,128)(2,1)} %pad_maximum_fusion) | data formatting | bytes 22020096
  492.9 46.3 %reduce-scatter.19.cloned.1.call-done = f32[48,10]{1,0:T(8,128)} async-done(((f32[1536,10]{1,0:T(8,128)}), f32[48,10]{1,0:T(8,128)}) %reduce-scatter.19.cloned.1.call-update) | async-done | bytes 1936
  542.7 45.8 %reduce-scatter.25.cloned.1.call-done = bf16[192,1536]{1,0:T(8,128)(2,1)} async-done(((bf16[768,1536]{1,0:T(8,128)(2,1)}), bf16[192,1536]{1,0:T(8,128)(2,1)}) %reduce-scatter.25.cloned.1.call-update) | async-done | bytes 589840
  592.0 83.6 %reduce-scatter.23.cloned.1.call-done = bf16[384,1536]{1,0:T(8,128)(2,1)} async-done(((bf16[1536,1536]{1,0:T(8,128)(2,1)}), bf16[384,1536]{1,0:T(8,128)(2,1)}) %reduce-scatter.23.cloned.1.call-update) | async-done | bytes 1179664
  681.8 143.9 %reduce-scatter.21.cloned.1.call-done = bf16[48,3584]{1,0:T(8,128)(2,1)} async-done(((bf16[1536,3584]{1,0:T(8,128)(2,1)}), bf16[48,3584]{1,0:T(8,128)(2,1)}) %reduce-scatter.21.cloned.1.call-update) | async-done | bytes 344080
  (285 shorter events, 167.2 us)
Async XLA Ops:
  7.2 202.4 %all-gather.5.cloned.1.call-start = ((), (), s32[]{:S(2)}) async-start(), calls=%async_computation.12 | async-start | bytes 5898240 | tf_op jit(solution)/shard_map/all_gather | solution.py:238
  12.0 85.0 %copy-start.5 = (bf16[128,1536]{1,0:T(8,128)(2,1)S(1)}, bf16[128,1536]{1,0:T(8,128)(2,1)}, u32[]{:S(2)}) copy-start(bf16[128,1536]{1,0:T(8,128)(2,1)} %param.12) | copy-start | bytes 1179652
  104.8 16.0 %copy-start.19 = (s32[1,128,4]{2,1,0:T(8,128)}, s32[1,128,4]{2,1,0:T(8,128)S(1)}, u32[]{:S(2)}) copy-start(s32[1,128,4]{2,1,0:T(8,128)S(1)} %copy.144) | copy-start | bytes 6148
  172.0 33.0 %all-to-all-start = ((bf16[8,1,96,1536]{3,2,1,0:T(8,128)(2,1)}), bf16[8,1,96,1536]{3,2,1,0:T(8,128)(2,1)S(1)}, u32[]{:S(2)}, u32[]{:S(2)}) async-start(bf16[8,1,96,1536]{3,2,1,0:T(8,128)(2,1)} %get-tuple-element.92), calls=%async_computation | async-start | bytes 4718592 | tf_op jit(solution)/shard_map/all_to_all | solution.py:289
  175.6 63.4 %all-gather.7.cloned.1.call-start = ((), (), s32[]{:S(2)}) async-start(), calls=%async_computation.13 | async-start | bytes 2949120 | tf_op jit(solution)/shard_map/all_gather | solution.py:239
  205.0 12.4 %copy-start.25 = (bf16[8,1,96,1536]{3,2,1,0:T(8,128)(2,1)}, bf16[8,1,96,1536]{3,2,1,0:T(8,128)(2,1)S(1)}, u32[]{:S(2)}) copy-start(bf16[8,1,96,1536]{3,2,1,0:T(8,128)(2,1)S(1)} %all-to-all-done) | copy-start | bytes 7077892
  205.0 34.0 %all-to-all-start.2 = ((bf16[8,1,96,1536]{3,2,1,0:T(8,128)(2,1)}), bf16[8,1,96,1536]{3,2,1,0:T(8,128)(2,1)}, u32[]{:S(2)}, u32[]{:S(2)}) async-start(bf16[8,1,96,1536]{3,2,1,0:T(8,128)(2,1)} %get-tuple-element.91), calls=%async_computation.2 | async-start | bytes 4718592 | tf_op jit(solution)/shard_map/all_to_all | solution.py:372
  239.0 7.6 copy-start.53
  251.7 33.0 %all-to-all-start.3 = ((bf16[8,1,96,1536]{3,2,1,0:T(8,128)(2,1)}), bf16[8,1,96,1536]{3,2,1,0:T(8,128)(2,1)S(1)}, u32[]{:S(2)}, u32[]{:S(2)}) async-start(bf16[8,1,96,1536]{3,2,1,0:T(8,128)(2,1)} %fusion.26), calls=%async_computation.3 | async-start | bytes 4718592 | tf_op jit(solution)/shard_map/all_to_all | solution.py:388
  260.9 28.3 %copy-start.18 = (bf16[128,1536]{1,0:T(8,128)(2,1)S(1)}, bf16[128,1536]{1,0:T(8,128)(2,1)}, u32[]{:S(2)}) copy-start(bf16[128,1536]{1,0:T(8,128)(2,1)} %param.13) | copy-start | bytes 1179652
  284.7 33.9 %all-to-all-start.1 = ((bf16[8,1,96,1536]{3,2,1,0:T(8,128)(2,1)}), bf16[8,1,96,1536]{3,2,1,0:T(8,128)(2,1)}, u32[]{:S(2)}, u32[]{:S(2)}) async-start(bf16[8,1,96,1536]{3,2,1,0:T(8,128)(2,1)} %fusion.25), calls=%async_computation.1 | async-start | bytes 4718592 | tf_op jit(solution)/shard_map/all_to_all | solution.py:301
  289.1 112.2 %reduce-scatter.15.cloned.1.call-start = ((), (), s32[]{:S(2)}) async-start(), calls=%async_computation.10 | async-start | bytes 589824 | tf_op jit(solution)/shard_map/reduce_scatter | solution.py:469
  347.2 6.8 copy-start.3
  347.2 6.8 copy-start.40
  368.8 69.9 %reduce-scatter.17.cloned.1.call-start = ((), (), s32[]{:S(2)}) async-start(), calls=%async_computation.11 | async-start | bytes 589824 | tf_op jit(solution)/shard_map/reduce_scatter | solution.py:475
  373.0 29.2 %copy-start.32 = (f32[128,64]{1,0:T(8,128)S(1)}, f32[128,64]{1,0:T(8,128)}, u32[]{:S(2)}) copy-start(f32[128,64]{1,0:T(8,128)} %copy-done.30) | copy-start | bytes 98308
  373.0 29.2 %copy-start.38 = (f32[128,64]{1,0:T(8,128)S(1)}, f32[128,64]{1,0:T(8,128)}, u32[]{:S(2)}) copy-start(f32[128,64]{1,0:T(8,128)} %get-tuple-element.88) | copy-start | bytes 98308
  377.2 62.4 %copy-start.6 = (bf16[128,1536]{1,0:T(8,128)(2,1)S(1)}, bf16[128,1536]{1,0:T(8,128)(2,1)}, u32[]{:S(2)}) copy-start(bf16[128,1536]{1,0:T(8,128)(2,1)} %param.12) | copy-start | bytes 1179652
  377.2 62.4 %copy-start.50 = (f32[128]{0:T(128)S(1)}, f32[128]{0:T(128)}, u32[]{:S(2)}) copy-start(f32[128]{0:T(128)} %copy-done.49) | copy-start | bytes 1540
  377.3 161.9 %reduce-scatter.19.cloned.1.call-start = ((), (), s32[]{:S(2)}) async-start(), calls=%async_computation.14 | async-start | bytes 811008
  402.2 39.2 %copy-start.43 = (f32[1536,1]{0,1:T(1,128)S(1)}, f32[1536,1]{0,1:T(1,128)}, u32[]{:S(2)}) copy-start(f32[1536,1]{0,1:T(1,128)} %broadcast_in_dim.69) | copy-start | bytes 18436
  442.6 145.9 %reduce-scatter.25.cloned.1.call-start = ((), (), s32[]{:S(2)}) async-start(), calls=%async_computation.17 | async-start | bytes 2949120
  452.4 223.2 %reduce-scatter.23.cloned.1.call-start = ((), (), s32[]{:S(2)}) async-start(), calls=%async_computation.16 | async-start | bytes 5898240
  467.6 358.1 %reduce-scatter.21.cloned.1.call-start = ((), (), s32[]{:S(2)}) async-start(), calls=%async_computation.15 | async-start | bytes 11354112
  (44 other events, 110.1 us)
Sparse Core Ops, SparseCore 0:
  9.6 116.4 all-gather.4
  178.0 50.9 all-gather.6
  368.9 32.3 reduce-scatter.14
  404.5 34.1 reduce-scatter.16
  443.6 95.4 reduce-scatter.18
  541.3 47.1 reduce-scatter.24
  590.8 84.7 reduce-scatter.22
  681.6 144.0 reduce-scatter.20

commit v2 on v0

--- a/solution.py
+++ b/solution.py
@@ -1,7 +1,11 @@
 import jax
 import jax.numpy as jnp
 from jax import lax
+from jax.experimental import pallas as pl
+from jax.experimental.pallas import tpu as pltpu
 from jax.sharding import PartitionSpec as P
+
+MESH = pl.DeviceIdType.MESH
 
 QUERY_HEADS = 12
 KEY_VALUE_HEADS = 2
@@ -64,7 +68,7 @@
     return (target, jnp.minimum(source, slot_total - 1), filled)
 
 
-def body(
+def general_body(
     tokens,
     cotangent,
     routes,
@@ -437,6 +441,1084 @@
     )
 
 
+def product(left, right):
+    return lax.dot_general(
+        left, right, (((1,), (0,)), ((), ())), preferred_element_type=jnp.float32
+    )
+
+
+def product_rows(left, right):
+    return lax.dot_general(
+        left, right, (((1,), (1,)), ((), ())), preferred_element_type=jnp.float32
+    )
+
+
+def product_columns(left, right):
+    return lax.dot_general(
+        left, right, (((0,), (0,)), ((), ())), preferred_element_type=jnp.float32
+    )
+
+
+def split_three(values):
+    high = values.astype(jnp.bfloat16)
+    rest = values - high.astype(jnp.float32)
+    middle = rest.astype(jnp.bfloat16)
+    low = (rest - middle.astype(jnp.float32)).astype(jnp.bfloat16)
+    return high, middle, low
+
+
+def masked_gates(rows, router, mask):
+    chosen = mask.astype(jnp.float32) > 0.5
+    logits = jnp.where(chosen, product(rows, router), masked_score)
+    expo_vals = jnp.where(chosen, jnp.exp(logits - jnp.max(logits, axis=1, keepdims=True)), 0.0)
+    return expo_vals / jnp.sum(expo_vals, axis=1, keepdims=True)
+
+
+def layer_kernel(
+    x_ref,
+    cot_ref,
+    mask_ref,
+    rope_ref,
+    shard_a,
+    shard_b,
+    shard_c,
+    w_in_ref,
+    w_out_ref,
+    block_out_ref,
+    dx_ref,
+    grad_in_ref,
+    grad_out_ref,
+    grad_dense_ref,
+    grad_aux_ref,
+    spill_b,
+    spill_c,
+    n2_all,
+    cot_all,
+    full_a,
+    arena,
+    gate_buf,
+    w_in_half,
+    w_out_half,
+    hidden_all,
+    g_all,
+    kv_all,
+    k_t,
+    v_t,
+    q_rows,
+    do_rows,
+    normed_buf,
+    attn_buf,
+    after_buf,
+    lse_buf,
+    turn_send,
+    turn_recv,
+    og_all,
+    qg_all,
+    kvg_all,
+    dkv_recv,
+    aux_send,
+    gain_buf,
+    z_sems,
+    p_sems,
+    s_sems,
+    kv_sems,
+    tok_sems,
+    turn_sems,
+    win_sems,
+    wout_sems,
+    sib_sems,
+    ret_sems,
+    gate_sems,
+    gin_sems,
+    gout_sems,
+    og_sems,
+    qg_sems,
+    kvg_sems,
+    dkv_sems,
+    dense_sems,
+    aux_sems,
+    local_sems,
+    credit_sem,
+):
+    plane = lax.axis_index("dp")
+    member = lax.axis_index("expert")
+    core = lax.rem(member, 2)
+    parity = lax.rem(plane, 2)
+    tokens, width = x_ref.shape
+    rows = shard_a.shape[0]
+    xor = lax.bitwise_xor
+    f32, bf16 = jnp.float32, jnp.bfloat16
+    half = FF // 2
+    score_scale = HEAD_DIM ** (-0.5)
+    kv_width = KEY_VALUE_HEADS * HEAD_DIM
+
+    def at_rows(start, count, step=16):
+        return pl.ds(pl.multiple_of(start, step), count)
+
+    def remote(source, target, sems, index, device):
+        return pltpu.make_async_remote_copy(
+            src_ref=source,
+            dst_ref=target,
+            send_sem=sems.at[(0,) + index],
+            recv_sem=sems.at[(1,) + index],
+            device_id=device,
+            device_id_type=MESH,
+        )
+
+    in_plane = lambda step: (plane, xor(member, step))
+    sibling = in_plane(1)
+
+    barrier = pltpu.get_barrier_semaphore()
+    greeted = [(xor(plane, s), member) for s in (1, 2, 3)]
+    greeted += [in_plane(s) for s in range(1, 8)]
+    greeted += [(xor(plane, 1), xor(member, s)) for s in (2, 4, 6)]
+    for device in greeted:
+        pl.semaphore_signal(barrier, inc=1, device_id=device, device_id_type=MESH)
+
+    shards = (shard_a, shard_b, shard_c)
+
+    def dense_block(part, step, chip_step):
+        start = (xor(plane, step) * 8 + xor(member, chip_step)) * rows
+        if part == 0:
+            return full_a.at[at_rows(start, rows)]
+        return arena.at[at_rows(start + (part - 1) * width, rows)]
+
+    def z_copy(part, step):
+        return remote(
+            shards[part],
+            dense_block(part, 0, 0),
+            z_sems,
+            (part, step),
+            (xor(plane, step), member),
+        )
+
+    def plane_copy(part, step, chip):
+        block = dense_block(part, step, 0)
+        return remote(block, block, p_sems, (part, step, chip), in_plane(2 * chip))
+
+    def sibling_copy(part, step, chip):
+        block = dense_block(part, step, 2 * chip)
+        return remote(block, block, s_sems, (part, step, chip), sibling)
+
+    own_rows = (plane * 8 + member) * rows
+    full_a[at_rows(own_rows, rows)] = shard_a[...]
+    arena[at_rows(own_rows, rows)] = shard_b[...]
+    arena[at_rows(own_rows + width, rows)] = shard_c[...]
+
+    def token_rows(plane_step, member_step):
+        start = (xor(parity, plane_step) * 8 + xor(member, member_step)) * tokens
+        return at_rows(start, tokens, 128)
+
+    cot_all[token_rows(0, 0), pl.ds(0, width)] = cot_ref[...]
+    cot_all[token_rows(0, 0), pl.ds(width, 128)] = mask_ref[...]
+    pl.semaphore_wait(barrier, len(greeted))
+
+    for part in range(3):
+        for step in (3, 2, 1):
+            z_copy(part, step).start()
+    for part in range(3):
+        for chip in (1, 2, 3):
+            plane_copy(part, 0, chip).start()
+        sibling_copy(part, 0, 0).start()
+
+    def pass_on_plane(part):
+        for step in (1, 2, 3):
+            z_copy(part, step).wait_recv()
+            for chip in (1, 2, 3):
+                plane_copy(part, step, chip).start()
+            sibling_copy(part, step, 0).start()
+
+    def pass_on_sibling(part):
+        for step in range(4):
+            for chip in (1, 2, 3):
+                plane_copy(part, step, chip).wait_recv()
+                sibling_copy(part, step, chip).start()
+
+    def arrived_dense(part):
+        for step in range(4):
+            for chip in range(4):
+                sibling_copy(part, step, chip).wait_recv()
+
+    def sent_dense(part):
+        for step in range(4):
+            if step:
+                z_copy(part, step).wait_send()
+            for chip in range(4):
+                if chip:
+                    plane_copy(part, step, chip).wait_send()
+                sibling_copy(part, step, chip).wait_send()
+
+    token_arrays = (cot_all, n2_all)
+
+    def token_z(kind):
+        block = token_arrays[kind].at[token_rows(0, 0)]
+        return remote(block, block, tok_sems, (kind, 0), (xor(plane, 1), member))
+
+    def token_plane(kind, plane_step, chip):
+        block = token_arrays[kind].at[token_rows(plane_step, 0)]
+        index = (kind, 1 + plane_step * 3 + chip - 1)
+        return remote(block, block, tok_sems, index, in_plane(2 * chip))
+
+    def token_sibling(kind, plane_step, chip):
+        block = token_arrays[kind].at[token_rows(plane_step, 2 * chip)]
+        return remote(block, block, tok_sems, (kind, 7 + plane_step * 4 + chip), sibling)
+
+    def token_start(kind):
+        token_z(kind).start()
+        for chip in (1, 2, 3):
+            token_plane(kind, 0, chip).start()
+        token_sibling(kind, 0, 0).start()
+
+    def token_pass_plane(kind):
+        token_z(kind).wait_recv()
+        for chip in (1, 2, 3):
+            token_plane(kind, 1, chip).start()
+        token_sibling(kind, 1, 0).start()
+
+    def token_pass_sibling(kind):
+        for plane_step in (0, 1):
+            for chip in (1, 2, 3):
+                token_plane(kind, plane_step, chip).wait_recv()
+                token_sibling(kind, plane_step, chip).start()
+
+    def token_finish(kind):
+        token_z(kind).wait_send()
+        for plane_step in (0, 1):
+            for chip in range(4):
+                if chip:
+                    token_plane(kind, plane_step, chip).wait_send()
+                token_sibling(kind, plane_step, chip).wait()
+
+    quarter = w_in_ref.shape[0]
+    quarter_out = w_out_ref.shape[0]
+
+    def win_copy(step, piece):
+        other = xor(parity, step % 2)
+        source = w_in_ref.at[:, at_rows(piece * FF + other * half, half, 128)]
+        target = w_in_half.at[at_rows(plane * quarter, quarter), pl.ds(piece * half, half)]
+        if step == 0:
+            return pltpu.make_async_copy(source, target, local_sems.at[piece])
+        return remote(source, target, win_sems, (step, piece), (xor(plane, step), member))
+
+    out_half = lax.div(plane, 2)
+
+    def wout_arrived(slot):
+        target = w_out_half.at[at_rows(slot * quarter_out, quarter_out)]
+        return pltpu.make_async_remote_copy(
+            src_ref=w_out_ref,
+            dst_ref=target,
+            send_sem=wout_sems.at[0, slot],
+            recv_sem=wout_sems.at[1, slot],
+            device_id=(xor(plane, 1), member),
+            device_id_type=MESH,
+        )
+
+    def wout_local():
+        return pltpu.make_async_copy(
+            w_out_ref,
+            w_out_half.at[at_rows(parity * quarter_out, quarter_out)],
+            local_sems.at[2],
+        )
+
+    def wout_send(turn):
+        return pltpu.make_async_remote_copy(
+            src_ref=w_out_ref,
+            dst_ref=w_out_half.at[at_rows(parity * quarter_out, quarter_out)],
+            send_sem=wout_sems.at[0, turn],
+            recv_sem=wout_sems.at[1, parity],
+            device_id=(out_half + 2 * turn, member),
+            device_id_type=MESH,
+        )
+
+    def expert_start():
+        for step in (1, 3, 2):
+            for piece in (0, 1):
+                win_copy(step, piece).start()
+        for piece in (0, 1):
+            win_copy(0, piece).start()
+        for turn in (0, 1):
+
+            @pl.when(out_half + 2 * turn != plane)
+            def _():
+                wout_send(turn).start()
+
+        @pl.when(out_half == parity)
+        def _():
+            wout_local().start()
+
+    def expert_finish():
+        for step in (1, 3, 2):
+            for piece in (0, 1):
+                win_copy(step, piece).wait()
+        for piece in (0, 1):
+            win_copy(0, piece).wait()
+        for slot in (0, 1):
+
+            @pl.when(parity * 2 + slot != plane)
+            def _():
+                wout_arrived(slot).wait_recv()
+
+        for turn in (0, 1):
+
+            @pl.when(out_half + 2 * turn != plane)
+            def _():
+                wout_send(turn).wait_send()
+
+        @pl.when(out_half == parity)
+        def _():
+            wout_local().wait()
+
+    pass_on_plane(0)
+    pass_on_plane(1)
+    pass_on_sibling(0)
+    arrived_dense(0)
+    expert_start()
+    aux = full_a[:, pl.ds(2 * kv_width, 128)]
+    pick = (
+        lax.broadcasted_iota(jnp.int32, (16, 128), 1)
+        == lax.broadcasted_iota(jnp.int32, (16, 128), 0) + EXPERT_LANES
+    ).astype(bf16)
+    gain_buf[...] = product_rows(pick, aux)
+    gain_a = gain_buf[pl.ds(0, 1), :]
+    gain_m = gain_buf[pl.ds(1, 1), :]
+    residual = x_ref[...].astype(f32)
+    normed = (residual * norm_factor(residual) * gain_a).astype(bf16)
+    normed_buf[...] = normed
+    cos_part = rope_ref[:, pl.ds(0, HEAD_DIM)]
+    sin_part = rope_ref[:, pl.ds(HEAD_DIM, HEAD_DIM)]
+
+    def turned(values, orient):
+        swapped = pltpu.roll(values, HEAD_DIM // 2, 1)
+        return values * cos_part + swapped * (sin_part * orient)
+
+    kv_rows = product(normed, full_a[:, pl.ds(0, 2 * kv_width)])
+    for part in range(2 * KEY_VALUE_HEADS):
+        piece = kv_rows[:, part * HEAD_DIM : (part + 1) * HEAD_DIM]
+        if part < KEY_VALUE_HEADS:
+            piece = turned(piece, 1.0)
+        kv_all[part, at_rows(member * tokens, tokens, 128)] = piece.astype(bf16)
+
+    def kv_copy(sems, index, owner_step, device):
+        block = kv_all.at[:, at_rows(xor(member, owner_step) * tokens, tokens, 128)]
+        return remote(block, block, sems, (index,), device)
+
+    for chip in (1, 2, 3):
+        kv_copy(kv_sems, chip - 1, 0, in_plane(2 * chip)).start()
+    kv_copy(kv_sems, 3, 0, sibling).start()
+    turn_send[0] = jnp.transpose(normed).reshape(turn_send.shape[1:])
+
+    def turn_copy(kind, step):
+        return remote(
+            turn_send.at[kind, :, xor(member, step)],
+            turn_recv.at[kind, :, :, at_rows(member * tokens, tokens, 128)],
+            turn_sems,
+            (kind, step),
+            in_plane(step),
+        )
+
+    def turn_start(kind):
+        for step in range(1, 8):
+            turn_copy(kind, step).start()
+        turn_recv[kind, :, :, at_rows(member * tokens, tokens, 128)] = turn_send[
+            kind, :, pl.ds(member, 1)
+        ].reshape(turn_recv.shape[1], rows, tokens)
+
+    pass_on_sibling(1)
+    for chip in (1, 2, 3):
+        kv_copy(kv_sems, chip - 1, 0, in_plane(2 * chip)).wait_recv()
+        kv_copy(kv_sems, 3 + chip, 2 * chip, sibling).start()
+    pass_on_plane(2)
+    token_start(0)
+    arrived_dense(1)
+    spill_b_copy = pltpu.make_async_copy(
+        arena.at[pl.ds(0, width)], spill_b, local_sems.at[3]
+    )
+    spill_b_copy.start()
+    for head in range(QUERY_HEADS):
+        if head % 2 == 0:
+            pair = product(normed, arena[pl.ds(0, width), pl.ds(head * HEAD_DIM, 2 * HEAD_DIM)])
+        piece = pair[:, (head % 2) * HEAD_DIM : (head % 2 + 1) * HEAD_DIM]
+        q_rows[pl.ds(head * tokens, tokens)] = turned(piece, 1.0).astype(bf16)
+    for chip in range(4):
+        index = 3 if chip == 0 else 3 + chip
+        kv_copy(kv_sems, index, 2 * chip, sibling).wait()
+    for chip in (1, 2, 3):
+        kv_copy(kv_sems, chip - 1, 0, in_plane(2 * chip)).wait_send()
+    for group in range(KEY_VALUE_HEADS):
+        k_t[group] = jnp.transpose(kv_all[group])
+        v_t[group] = jnp.transpose(kv_all[KEY_VALUE_HEADS + group])
+
+    seq_len = kv_all.shape[1]
+    pairs = QUERY_HEADS // 2
+    pairs_per_group = pairs // KEY_VALUE_HEADS
+    key_index = lax.broadcasted_iota(jnp.int32, (seq_len, 2 * tokens), 0)
+    query_index = member * tokens + lax.rem(
+        lax.broadcasted_iota(jnp.int32, (seq_len, 2 * tokens), 1), tokens
+    )
+    allowed = key_index <= query_index
+
+    def pair_scores(pair, group):
+        queries = q_rows[at_rows(pair * 2 * tokens, 2 * tokens, 128)]
+        scores = product_rows(kv_all[group], queries) * score_scale
+        return jnp.where(allowed, scores, masked_score), queries
+
+    def attend(pair, carry):
+        group = lax.div(pair, pairs_per_group)
+        scores, _ = pair_scores(pair, group)
+        peak = jnp.max(scores, axis=0, keepdims=True)
+        expo_vals = jnp.exp(scores - peak)
+        sums = jnp.sum(expo_vals, axis=0, keepdims=True)
+        probs = (expo_vals / sums).astype(bf16)
+        lse_buf[pair] = jnp.broadcast_to(peak + jnp.log(sums), (8, 2 * tokens))
+        part = product(v_t[group], probs)
+        for inner in (0, 1):
+            piece = part[:, inner * tokens : (inner + 1) * tokens].astype(bf16)
+            attn_buf[2 * pair + inner] = piece
+        return carry
+
+    lax.fori_loop(0, pairs, attend, 0)
+    token_pass_plane(0)
+    pass_on_sibling(2)
+    attn_t = attn_buf[...].reshape(width, tokens)
+    turn_send[1] = attn_t.reshape(turn_send.shape[1:])
+    attn = jnp.transpose(attn_t)
+    arrived_dense(2)
+    spill_c_copy = pltpu.make_async_copy(
+        arena.at[pl.ds(width, width)], spill_c, local_sems.at[4]
+    )
+    spill_c_copy.start()
+    for start in range(0, width, 512):
+        after_buf[:, pl.ds(start, 512)] = x_ref[:, pl.ds(start, 512)].astype(f32) + product(
+            attn, arena[pl.ds(width, width), pl.ds(start, 512)]
+        )
+    after = after_buf[...]
+    normed_two = (after * norm_factor(after) * gain_m).astype(bf16)
+    n2_all[token_rows(0, 0)] = normed_two
+    spill_b_copy.wait()
+    spill_c_copy.wait()
+    for part in range(3):
+        sent_dense(part)
+    token_start(1)
+    turn_send[2] = jnp.transpose(normed_two).reshape(turn_send.shape[1:])
+    token_pass_sibling(0)
+    token_finish(0)
+    token_pass_plane(1)
+    token_pass_sibling(1)
+    token_finish(1)
+    for kind in range(3):
+        turn_start(kind)
+    expert_finish()
+
+    own_lane = lax.broadcasted_iota(jnp.int32, (2 * tokens, 128), 1) == member
+    low_lane = lax.broadcasted_iota(jnp.int32, (2 * tokens, 128), 1) == member + 64
+    message = 2 * tokens
+    stage_base, sib_base, send_base, recv_base = 0, 2 * message, 4 * message, 8 * message
+
+    def arena_slot(base, slot):
+        return at_rows(base + slot * message, message, 128)
+
+    def sib_copy(slot):
+        return remote(
+            arena.at[arena_slot(stage_base, slot)],
+            arena.at[arena_slot(sib_base, slot)],
+            sib_sems,
+            (slot,),
+            sibling,
+        )
+
+    def sib_gate_copy(slot):
+        return remote(
+            gate_buf.at[slot], gate_buf.at[2 + slot], sib_sems, (2 + slot,), sibling
+        )
+
+    def ret_device(turn):
+        return (xor(plane, lax.div(turn, 4)), xor(member, 2 * lax.rem(turn, 4)))
+
+    def ret_copy(turn, slot):
+        return remote(
+            arena.at[arena_slot(send_base, slot)],
+            arena.at[arena_slot(recv_base, turn)],
+            ret_sems,
+            (turn,),
+            ret_device(turn),
+        )
+
+    def ret_gate_copy(turn, slot):
+        return remote(
+            gate_buf.at[4 + slot], gate_buf.at[8 + turn], gate_sems, (turn,), ret_device(turn)
+        )
+
+    def expert_step(turn, carry):
+        slot2 = lax.rem(turn, 2)
+        slot4 = lax.rem(turn, 4)
+        other_plane = xor(parity, lax.div(turn, 4))
+        chip = xor(lax.div(member, 2), lax.rem(turn, 4))
+        start = (other_plane * 4 + chip) * 2 * tokens
+        here = at_rows(start, 2 * tokens, 128)
+        token_block = n2_all[here, :]
+        gate_up = product(token_block, w_in_half[...])
+        gates = masked_gates(
+            token_block,
+            full_a[:, pl.ds(2 * kv_width, 128)],
+            cot_all[here, pl.ds(width, 128)],
+        )
+        gate = jnp.sum(jnp.where(own_lane, gates, 0.0), axis=1, keepdims=True)
+        gate_half = gate_up[:, :half]
+        up_half = gate_up[:, half:]
+        sigmoid_vals = 1.0 / (1.0 + jnp.exp(-gate_half))
+        silu_vals = gate_half * sigmoid_vals
+        hidden = (silu_vals * up_half).astype(bf16)
+        hidden_all[here, :] = hidden
+        slot_grad = (gate * cot_all[here, pl.ds(0, width)].astype(f32)).astype(bf16)
+        act_grad = product_rows(slot_grad, w_out_half[...])
+        gate_part = act_grad * up_half * sigmoid_vals * (1.0 + gate_half * (1.0 - sigmoid_vals))
+        g_block = jnp.concatenate([gate_part, act_grad * silu_vals], axis=1).astype(bf16)
+        g_all[here, :] = g_block
+
+        @pl.when(turn >= 2)
+        def _():
+            sib_copy(slot2).wait_send()
+            sib_gate_copy(slot2).wait_send()
+            pl.semaphore_wait(credit_sem, 1)
+
+        @pl.when(turn > 4)
+        def _():
+            ret_copy(turn - 4, slot4).wait_send()
+            ret_gate_copy(turn - 4, slot4).wait_send()
+
+        def halves(values, first):
+            return jnp.where(first, values[:tokens], values[tokens:])
+
+        send_first = core == 1
+        stage = stage_base + slot2 * message
+        place = jnp.where(turn == 0, recv_base, send_base + slot4 * message)
+        sib_start = sib_base + slot2 * message
+        gate_grad = jnp.zeros((2 * tokens, 1), f32)
+        for start in range(0, width, 512):
+            columns = pl.ds(start, 512)
+            out_part = product(hidden, w_out_half[:, columns])
+            in_part = product_rows(g_block, w_in_half[columns, :])
+            gate_grad = gate_grad + jnp.sum(
+                out_part * cot_all[here, columns].astype(f32), axis=1, keepdims=True
+            )
+            out_part = out_part * gate
+            arena[at_rows(stage, tokens, 128), columns] = halves(out_part, send_first).astype(bf16)
+            arena[at_rows(stage + tokens, tokens, 128), columns] = halves(
+                in_part, send_first
+            ).astype(bf16)
+            arena[at_rows(place, tokens, 128), columns] = halves(out_part, core == 0).astype(bf16)
+            arena[at_rows(place + tokens, tokens, 128), columns] = halves(
+                in_part, core == 0
+            ).astype(bf16)
+        cot_all[here, pl.ds(0, width)] = slot_grad
+        gate_high = gate_grad.astype(bf16).astype(f32)
+        gate_lanes = jnp.where(own_lane, gate_high, 0.0) + jnp.where(
+            low_lane, gate_grad - gate_high, 0.0
+        )
+        gate_buf[slot2] = halves(gate_lanes, send_first).astype(bf16)
+        sib_copy(slot2).start()
+        sib_gate_copy(slot2).start()
+        own_gate = halves(gate_lanes, core == 0)
+        sib_copy(slot2).wait_recv()
+        sib_gate_copy(slot2).wait_recv()
+        both = at_rows(place, message, 128)
+        arena[both] = (
+            arena[both].astype(f32) + arena[at_rows(sib_start, message, 128)].astype(f32)
+        ).astype(bf16)
+        own_gate = own_gate + gate_buf[2 + slot2].astype(f32)
+
+        @pl.when(turn < 6)
+        def _():
+            pl.semaphore_signal(credit_sem, inc=1, device_id=sibling, device_id_type=MESH)
+
+        gate_buf[jnp.where(turn == 0, 8, 4 + slot4)] = own_gate.astype(bf16)
+
+        @pl.when(turn > 0)
+        def _():
+            ret_copy(turn, slot4).start()
+            ret_gate_copy(turn, slot4).start()
+
+        return carry
+
+    lax.fori_loop(0, 8, expert_step, 0)
+
+    for slot in (0, 1):
+        sib_copy(slot).wait_send()
+        sib_gate_copy(slot).wait_send()
+
+    def gin_copy(step):
+        source = w_in_half.at[at_rows(xor(plane, step) * quarter, quarter)]
+        if step == 0:
+            return pltpu.make_async_copy(source, grad_in_ref.at[0], local_sems.at[5])
+        return remote(
+            source, grad_in_ref.at[step], gin_sems, (step,), (xor(plane, step), member)
+        )
+
+    for step in (2, 1, 3, 0):
+        start = xor(plane, step) * quarter
+        for piece in range(0, quarter, 128):
+            columns = n2_all[:, at_rows(start + piece, 128, 128)]
+            w_in_half[at_rows(start + piece, 128, 128)] = product_columns(
+                columns, g_all[...]
+            ).astype(bf16)
+        gin_copy(step).start()
+
+    def gout_copy(slot):
+        return pltpu.make_async_remote_copy(
+            src_ref=w_out_half.at[pl.ds(slot * quarter_out, quarter_out)],
+            dst_ref=grad_out_ref.at[out_half],
+            send_sem=gout_sems.at[0, slot],
+            recv_sem=gout_sems.at[1, out_half],
+            device_id=(parity * 2 + slot, member),
+            device_id_type=MESH,
+        )
+
+    def gout_local(slot):
+        return pltpu.make_async_copy(
+            w_out_half.at[pl.ds(slot * quarter_out, quarter_out)],
+            grad_out_ref.at[out_half],
+            local_sems.at[6],
+        )
+
+    def gout_arrived(turn):
+        return pltpu.make_async_remote_copy(
+            src_ref=w_out_half.at[pl.ds(0, quarter_out)],
+            dst_ref=grad_out_ref.at[turn],
+            send_sem=gout_sems.at[0, turn],
+            recv_sem=gout_sems.at[1, turn],
+            device_id=(xor(plane, 1), member),
+            device_id_type=MESH,
+        )
+
+    for start in range(0, half, 128):
+        w_out_half[pl.ds(start, 128)] = product_columns(
+            hidden_all[:, pl.ds(start, 128)], cot_all[:, pl.ds(0, width)]
+        ).astype(bf16)
+    for slot in (0, 1):
+
+        @pl.when(parity * 2 + slot != plane)
+        def _():
+            gout_copy(slot).start()
+
+        @pl.when(parity * 2 + slot == plane)
+        def _():
+            gout_local(slot).start()
+
+    load_b = pltpu.make_async_copy(
+        spill_b, cot_all.at[pl.ds(0, width), pl.ds(0, width)], local_sems.at[3]
+    )
+    load_c = pltpu.make_async_copy(spill_c, n2_all.at[pl.ds(0, width)], local_sems.at[4])
+    own_n2 = n2_all[token_rows(0, 0), :]
+    own_mask = mask_ref[...]
+    own_gates = masked_gates(own_n2, full_a[:, pl.ds(2 * kv_width, 128)], own_mask)
+    load_b.start()
+    load_c.start()
+
+    total_out = after_buf[...]
+    total_in = jnp.zeros((tokens, width), f32)
+    total_gate = jnp.zeros((tokens, 128), f32)
+    for turn in range(8):
+        if turn:
+            ret_copy(turn, turn % 4).wait_recv()
+            ret_gate_copy(turn, turn % 4).wait_recv()
+        base = recv_base + turn * message
+        total_out = total_out + arena[pl.ds(base, tokens)].astype(f32)
+        total_in = total_in + arena[pl.ds(base + tokens, tokens)].astype(f32)
+        total_gate = total_gate + gate_buf[8 + turn].astype(f32)
+    block_out_ref[...] = total_out.astype(bf16)
+    gate_grad = total_gate + pltpu.roll(total_gate, 64, 1)
+    gate_inner = jnp.sum(own_gates * gate_grad, axis=1, keepdims=True)
+    logit_grad = own_gates * (gate_grad - gate_inner)
+    lg_parts = split_three(logit_grad)
+    aux_now = full_a[:, pl.ds(2 * kv_width, 128)]
+    for part in lg_parts:
+        total_in = total_in + product_rows(part, aux_now)
+    after = after_buf[...]
+
+    def norm_backward(values, gain, grad):
+        factor = norm_factor(values)
+        scaled = grad * gain
+        gain_row = jnp.sum(grad * values * factor, axis=0, keepdims=True)
+        inner = jnp.mean(scaled * values, axis=-1, keepdims=True)
+        return factor * scaled - values * factor * factor * factor * inner, gain_row
+
+    two_back, gain_m_row = norm_backward(after, gain_buf[pl.ds(1, 1), :], total_in)
+    mid = cot_ref[...].astype(f32) + two_back
+    after_buf[...] = mid
+    out_grad = mid.astype(bf16)
+    own_block = at_rows(member * tokens, tokens, 128)
+    og_all[own_block, pl.ds(0, width)] = out_grad
+    og_all[own_block, pl.ds(width, 128)] = (
+        lg_parts[0].astype(f32)
+        + pltpu.roll(lg_parts[1].astype(f32), 8, 1)
+        + pltpu.roll(lg_parts[2].astype(f32), 16, 1)
+    ).astype(bf16)
+
+    def gather_copy(array, sems, index, owner_step, device, columns=None):
+        block = at_rows(xor(member, owner_step) * tokens, tokens, 128)
+        piece = array.at[block] if columns is None else array.at[block, columns]
+        return remote(piece, piece, sems, index, device)
+
+    def gather_start(array, sems, lead=(), columns=None):
+        for chip in (1, 2, 3):
+            gather_copy(array, sems, lead + (chip - 1,), 0, in_plane(2 * chip), columns).start()
+        gather_copy(array, sems, lead + (3,), 0, sibling, columns).start()
+
+    def gather_pass(array, sems, lead=(), columns=None):
+        for chip in (1, 2, 3):
+            gather_copy(array, sems, lead + (chip - 1,), 0, in_plane(2 * chip), columns).wait_recv()
+            gather_copy(array, sems, lead + (3 + chip,), 2 * chip, sibling, columns).start()
+
+    def gather_finish(array, sems, lead=(), columns=None):
+        for chip in (1, 2, 3):
+            gather_copy(array, sems, lead + (chip - 1,), 0, in_plane(2 * chip), columns).wait_send()
+        for chip in range(4):
+            gather_copy(array, sems, lead + (3 + chip,), 2 * chip, sibling, columns).wait()
+
+    gather_start(og_all, og_sems)
+    load_c.wait()
+    for head in range(0, QUERY_HEADS, 2):
+        pair = product_rows(out_grad, n2_all[pl.ds(head * HEAD_DIM, 2 * HEAD_DIM), :])
+        for inner in (0, 1):
+            do_rows[pl.ds((head + inner) * tokens, tokens)] = pair[
+                :, inner * HEAD_DIM : (inner + 1) * HEAD_DIM
+            ].astype(bf16)
+    gather_pass(og_all, og_sems)
+
+    def dkv_copy(group, step):
+        return remote(
+            g_all.at[
+                at_rows(xor(member, step) * tokens, tokens, 128),
+                pl.ds(group * 2 * HEAD_DIM, 2 * HEAD_DIM),
+            ],
+            dkv_recv.at[group, step],
+            dkv_sems,
+            (group, step),
+            in_plane(step),
+        )
+
+    planes = turn_recv.shape[1]
+    dense_starts = (0, 2 * kv_width, 2 * kv_width + width, 2 * kv_width + 2 * width)
+
+    def dense_copy(piece, step):
+        size = dense_starts[piece + 1] - dense_starts[piece]
+        source = arena.at[
+            at_rows((piece * planes + xor(plane, step)) * rows, rows), pl.ds(0, size)
+        ]
+        target = grad_dense_ref.at[step, :, pl.ds(dense_starts[piece], size)]
+        if step == 0:
+            return pltpu.make_async_copy(source, target, local_sems.at[piece])
+        return remote(source, target, dense_sems, (piece, step), (xor(plane, step), member))
+
+    for group in range(KEY_VALUE_HEADS):
+        keys = kv_all[group]
+        values = kv_all[KEY_VALUE_HEADS + group]
+        dk = jnp.zeros((seq_len, HEAD_DIM), f32)
+        dv = jnp.zeros((seq_len, HEAD_DIM), f32)
+        for pair in range(group * pairs_per_group, (group + 1) * pairs_per_group):
+            scores, queries = pair_scores(pair, group)
+            probs = jnp.exp(scores - lse_buf[pair][0:1])
+            grads = do_rows[pl.ds(pair * 2 * tokens, 2 * tokens)]
+            prob_grad = product_rows(values, grads)
+            row_dot = jnp.sum(probs * prob_grad, axis=0, keepdims=True)
+            score_grad = (probs * (prob_grad - row_dot)).astype(bf16)
+            dk = dk + product(score_grad, queries)
+            dv = dv + product(probs.astype(bf16), grads)
+            dq = product(k_t[group], score_grad) * score_scale
+            for inner in (0, 1):
+                piece = jnp.transpose(dq[:, inner * tokens : (inner + 1) * tokens])
+                qg_all[own_block, pl.ds((2 * pair + inner) * HEAD_DIM, HEAD_DIM)] = turned(
+                    piece, -1.0
+                ).astype(bf16)
+        start = group * 2 * HEAD_DIM
+        g_all[pl.ds(0, seq_len), pl.ds(start, HEAD_DIM)] = (dk * score_scale).astype(bf16)
+        g_all[pl.ds(0, seq_len), pl.ds(start + HEAD_DIM, HEAD_DIM)] = dv.astype(bf16)
+        for step in range(1, 8):
+            dkv_copy(group, step).start()
+        span = width // KEY_VALUE_HEADS
+        gather_start(qg_all, qg_sems, (group,), pl.ds(group * span, span))
+
+    gather_finish(og_all, og_sems)
+    for kind in range(3):
+        for step in range(1, 8):
+            turn_copy(kind, step).wait()
+    turned_attn = turn_recv[1].reshape(planes * rows, seq_len)
+    for start in range(0, width, 512):
+        arena[pl.ds(2 * planes * rows, planes * rows), pl.ds(start, 512)] = product(
+            turned_attn, og_all[:, pl.ds(start, 512)]
+        ).astype(bf16)
+    for step in (2, 3, 1, 0):
+        dense_copy(2, step).start()
+    router_part = product(
+        turn_recv[2].reshape(planes * rows, seq_len), og_all[:, pl.ds(width, 128)]
+    )
+
+    for group in range(KEY_VALUE_HEADS):
+        start = group * 2 * HEAD_DIM
+        dk = g_all[own_block, pl.ds(start, HEAD_DIM)].astype(f32)
+        dv = g_all[own_block, pl.ds(start + HEAD_DIM, HEAD_DIM)].astype(f32)
+        for step in range(1, 8):
+            dkv_copy(group, step).wait_recv()
+            dk = dk + dkv_recv[group, step, :, pl.ds(0, HEAD_DIM)].astype(f32)
+            dv = dv + dkv_recv[group, step, :, pl.ds(HEAD_DIM, HEAD_DIM)].astype(f32)
+        kvg_all[own_block, pl.ds(group * HEAD_DIM, HEAD_DIM)] = turned(dk, -1.0).astype(bf16)
+        kvg_all[own_block, pl.ds(kv_width + group * HEAD_DIM, HEAD_DIM)] = dv.astype(bf16)
+    gather_start(kvg_all, kvg_sems)
+    span = width // KEY_VALUE_HEADS
+    for group in range(KEY_VALUE_HEADS):
+        gather_pass(qg_all, qg_sems, (group,), pl.ds(group * span, span))
+    gather_pass(kvg_all, kvg_sems)
+
+    load_b.wait()
+    own_kvg = kvg_all[own_block, :]
+    own_qg = qg_all[own_block, :]
+    normed_grad = product_rows(own_kvg, full_a[:, pl.ds(0, 2 * kv_width)]) + product_rows(
+        own_qg, cot_all[pl.ds(0, width), pl.ds(0, width)]
+    )
+    one_back, gain_a_row = norm_backward(
+        x_ref[...].astype(f32), gain_buf[pl.ds(0, 1), :], normed_grad
+    )
+    dx_ref[...] = after_buf[...] + one_back
+    line = lax.broadcasted_iota(jnp.int32, (128, width), 0)
+    gain_lines = jnp.zeros((128, width), f32)
+    for offset, part in enumerate(split_three(gain_a_row) + split_three(gain_m_row)):
+        gain_lines = jnp.where(line == 32 + offset, part.astype(f32), gain_lines)
+    turn_send[3] = jnp.transpose(gain_lines.astype(bf16)).reshape(turn_send.shape[1:])
+    turn_start(3)
+
+    turned_normed = turn_recv[0].reshape(planes * rows, seq_len)
+    for group in range(KEY_VALUE_HEADS):
+        gather_finish(qg_all, qg_sems, (group,), pl.ds(group * span, span))
+    for start in range(0, width, 512):
+        arena[pl.ds(planes * rows, planes * rows), pl.ds(start, 512)] = product(
+            turned_normed, qg_all[:, pl.ds(start, 512)]
+        ).astype(bf16)
+    for step in (2, 3, 1, 0):
+        dense_copy(1, step).start()
+    gather_finish(kvg_all, kvg_sems)
+    arena[pl.ds(0, planes * rows), pl.ds(0, 2 * kv_width)] = product(
+        turned_normed, kvg_all[...]
+    ).astype(bf16)
+    for step in (2, 3, 1, 0):
+        dense_copy(0, step).start()
+    for step in range(1, 8):
+        turn_copy(3, step).wait()
+    aux_total = router_part
+    for block in range(8):
+        aux_total = aux_total + turn_recv[3, :, :, pl.ds(block * tokens, tokens)].reshape(
+            planes * rows, tokens
+        ).astype(f32)
+    aux_send[...] = aux_total.reshape(planes, rows, 128)
+
+    def aux_copy(step):
+        return remote(
+            aux_send.at[xor(plane, step)],
+            grad_aux_ref.at[step],
+            aux_sems,
+            (step,),
+            (xor(plane, step), member),
+        )
+
+    for step in (1, 2, 3):
+        aux_copy(step).start()
+    own_aux = pltpu.make_async_copy(aux_send.at[plane], grad_aux_ref.at[0], local_sems.at[7])
+    own_aux.start()
+
+    for turn in range(4, 8):
+        ret_copy(turn, turn % 4).wait_send()
+        ret_gate_copy(turn, turn % 4).wait_send()
+    for group in range(KEY_VALUE_HEADS):
+        for step in range(1, 8):
+            dkv_copy(group, step).wait_send()
+    gin_copy(0).wait()
+    for step in (1, 2, 3):
+        gin_copy(step).wait()
+    for slot in (0, 1):
+
+        @pl.when(parity * 2 + slot != plane)
+        def _():
+            gout_copy(slot).wait_send()
+
+        @pl.when(parity * 2 + slot == plane)
+        def _():
+            gout_local(slot).wait()
+
+    for turn in (0, 1):
+
+        @pl.when(out_half + 2 * turn != plane)
+        def _():
+            gout_arrived(turn).wait_recv()
+
+    for piece in range(3):
+        for step in range(4):
+            dense_copy(piece, step).wait()
+    for step in (1, 2, 3):
+        aux_copy(step).wait()
+    own_aux.wait()
+
+
+EXPERT_LANES = 8
+
+
+def fast_body(
+    tokens,
+    cotangent,
+    routes,
+    gain_attn,
+    w_query,
+    key_weight,
+    value_weight,
+    w_output,
+    gain_moe,
+    w_router,
+    w_in,
+    w_out,
+):
+    f32, bf16 = jnp.float32, jnp.bfloat16
+    total_rows, width = tokens.shape
+    rows = w_query.shape[1]
+    planes = lax.axis_size("dp")
+    members = lax.axis_size("expert")
+    seq_len = total_rows * members
+    kv_width = key_weight.shape[2]
+    quarter = w_in.shape[1]
+    quarter_out = w_out.shape[1]
+    half = FF // 2
+    positions = lax.axis_index("expert") * total_rows + jnp.arange(total_rows, dtype=jnp.int32)
+    cos_table, sin_table = rope_tables(positions, HEAD_DIM)
+    rope = jnp.concatenate([cos_table, cos_table, -sin_table, sin_table], axis=1)
+    lanes = jnp.arange(128, dtype=jnp.int32)
+    mask = jnp.any(routes[0][:, :, None] == lanes[None, None, :], axis=1).astype(bf16)
+    padding = jnp.zeros((rows, 128 - EXPERT_LANES - 2), bf16)
+    shard_a = jnp.concatenate(
+        [
+            key_weight[0],
+            value_weight[0],
+            w_router[0],
+            gain_attn[0][:, None],
+            gain_moe[0][:, None],
+            padding,
+        ],
+        axis=1,
+    )
+    dense_width = 2 * kv_width + 2 * width
+    in_vmem = pl.BlockSpec(memory_space=pltpu.VMEM)
+    anywhere = pl.BlockSpec(memory_space=pl.ANY)
+    pair_rows = 2 * seq_len
+    shape = jax.ShapeDtypeStruct
+    dma = pltpu.SemaphoreType.DMA
+    heads = QUERY_HEADS
+    (
+        block_out,
+        tokens_grad,
+        grad_in,
+        grad_out,
+        grad_dense,
+        grad_aux,
+        _,
+        _,
+    ) = pl.pallas_call(
+        layer_kernel,
+        out_shape=(
+            shape((total_rows, width), bf16),
+            shape((total_rows, width), f32),
+            shape((planes, quarter, 2 * half), bf16),
+            shape((2, quarter_out, width), bf16),
+            shape((planes, rows, dense_width), bf16),
+            shape((planes, rows, 128), f32),
+            shape((width, width), bf16),
+            shape((width, width), bf16),
+        ),
+        in_specs=[in_vmem] * 7 + [anywhere] * 2,
+        out_specs=(in_vmem,) * 2 + (anywhere,) * 6,
+        scratch_shapes=[
+            pltpu.VMEM((pair_rows, width), bf16),
+            pltpu.VMEM((pair_rows, width + 128), bf16),
+            pltpu.VMEM((width, 2 * kv_width + 128), bf16),
+            pltpu.VMEM((32 * total_rows, width), bf16),
+            pltpu.VMEM((16, total_rows, 128), bf16),
+            pltpu.VMEM((width, 2 * half), bf16),
+            pltpu.VMEM((half, width), bf16),
+            pltpu.VMEM((pair_rows, half), bf16),
+            pltpu.VMEM((pair_rows, 2 * half), bf16),
+            pltpu.VMEM((2 * KEY_VALUE_HEADS, seq_len, HEAD_DIM), bf16),
+            pltpu.VMEM((KEY_VALUE_HEADS, HEAD_DIM, seq_len), bf16),
+            pltpu.VMEM((KEY_VALUE_HEADS, HEAD_DIM, seq_len), bf16),
+            pltpu.VMEM((heads * total_rows, HEAD_DIM), bf16),
+            pltpu.VMEM((heads * total_rows, HEAD_DIM), bf16),
+            pltpu.VMEM((total_rows, width), bf16),
+            pltpu.VMEM((heads, HEAD_DIM, total_rows), bf16),
+            pltpu.VMEM((total_rows, width), f32),
+            pltpu.VMEM((heads // 2, 8, 2 * total_rows), f32),
+            pltpu.VMEM((4, planes, members, rows, total_rows), bf16),
+            pltpu.VMEM((4, planes, rows, seq_len), bf16),
+            pltpu.VMEM((seq_len, width + 128), bf16),
+            pltpu.VMEM((seq_len, width), bf16),
+            pltpu.VMEM((seq_len, 2 * kv_width), bf16),
+            pltpu.VMEM((KEY_VALUE_HEADS, members, total_rows, 2 * HEAD_DIM), bf16),
+            pltpu.VMEM((planes, rows, 128), f32),
+            pltpu.VMEM((16, width), f32),
+            dma((2, 3, 4)),
+            dma((2, 3, 4, 4)),
+            dma((2, 3, 4, 4)),
+            dma((2, 7)),
+            dma((2, 2, 15)),
+            dma((2, 4, 8)),
+            dma((2, 4, 2)),
+            dma((2, 2)),
+            dma((2, 4)),
+            dma((2, 8)),
+            dma((2, 8)),
+            dma((2, 4)),
+            dma((2, 2)),
+            dma((2, 7)),
+            dma((2, 2, 7)),
+            dma((2, 7)),
+            dma((2, 2, 8)),
+            dma((2, 3, 4)),
+            dma((2, 4)),
+            dma((8,)),
+            pltpu.SemaphoreType.REGULAR,
+        ],
+        compiler_params=pltpu.CompilerParams(
+            collective_id=0, has_side_effects=True, vmem_limit_bytes=63 * 2**20
+        ),
+    )(
+        tokens,
+        cotangent,
+        mask,
+        rope,
+        shard_a,
+        w_query[0],
+        w_output[0],
+        w_in.reshape(quarter, 2 * FF),
+        w_out.reshape(quarter_out, width),
+    )
+    own = grad_in[0].astype(f32) + grad_in[2].astype(f32)
+    other = grad_in[1].astype(f32) + grad_in[3].astype(f32)
+    even = lax.rem(lax.axis_index("dp"), 2) == 0
+    low, high = jnp.where(even, own, other), jnp.where(even, other, own)
+    w_in_grad = jnp.concatenate(
+        [low[:, :half], high[:, :half], low[:, half:], high[:, half:]], axis=1
+    )
+    w_out_grad = grad_out[0].astype(f32) + grad_out[1].astype(f32)
+    dense = jnp.sum(grad_dense.astype(f32), axis=0)
+    aux = jnp.sum(grad_aux, axis=0)
+    return (
+        block_out,
+        tokens_grad,
+        jnp.sum(aux[:, 32:35], axis=1)[None],
+        dense[None, :, 2 * kv_width : 2 * kv_width + width],
+        dense[None, :, :kv_width],
+        dense[None, :, kv_width : 2 * kv_width],
+        dense[None, :, 2 * kv_width + width :],
+        jnp.sum(aux[:, 35:38], axis=1)[None],
+        (aux[:, :8] + aux[:, 8:16] + aux[:, 16:24])[None],
+        w_in_grad[None, :, None, :],
+        w_out_grad[None, :, None, :],
+    )
+
+
 def solution(mesh):
     in_specs = (
         P(("dp", "expert"), None),
@@ -465,4 +1547,5 @@
         P(None, "dp", "expert", None),
         P(None, "dp", "expert", None),
     )
+    body = fast_body if mesh.shape["dp"] == 4 and mesh.shape["expert"] == 8 else general_body
     return jax.shard_map(body, mesh=mesh, in_specs=in_specs, out_specs=out_specs, check_vma=False)

time: 1260 us -> 380 us (0.30)
  waiting for transfers between devices: 788 us -> 0 us
  Pallas kernels: 0 us -> 358 us
  blocking collectives: 235 us -> 0 us
  matrix products: 85.5 us -> 0 us
  local copies, waits for them, and re-layouts: 78.2 us -> 14.6 us
  other arithmetic: 37.5 us -> 6.59 us
  starting transfers between devices: 16.7 us -> 0 us
  between operations: 15.2 us -> 0.75 us
    reduce_scatter x6 -> x0, waiting for transfers between devices: 528 us -> none  [the longest x1 142 us: body(): lax.psum_scatter(output_grad, ('dp', 'expert'), scatter_dimension=0, tile...]
    pallas_call x0 -> x1, Pallas kernels: none -> 358 us  [fast_body(): pl.pallas_call(layer_kernel, out_shape=(shape((total_rows, width), bf16),...]
    unnamed x16 -> x0, waiting for transfers between devices: 166 us -> none
    all_gather x5 -> x0, blocking collectives: 149 us -> none  [the longest x1 43.9 us: body(): lax.all_gather(key_weight[layer_number], ('dp', 'expert'), axis=0, tiled=...]
    unnamed x2 -> x0, blocking collectives: 85.9 us -> none
    dot_general x32 -> x0, matrix products: 84.1 us -> none  [the longest x1 7.8 us: body(): jnp.einsum('secd,def->secf', arrived_rows, expert_w[0], preferred_element...]
    all_to_all x4 -> x0, waiting for transfers between devices: 76.9 us -> none  [the longest x1 28.8 us: body(): lax.all_to_all(send_rows, 'expert', split_axis=0, concat_axis=0, tiled=True)]
    unnamed x167 -> x14, local copies, waits for them, and re-layouts: 35.2 us -> 9.92 us
  transfers between devices with their start and end apart: 17 -> 0, of which waited for: 14 -> 0; matrix products, arithmetic and copies ran while one was open for 11% -> 0% of each run, Pallas kernels for 0% -> 0%
where the time goes in v2:
time: 380 us
  Pallas kernels  358 us (94%)
  local copies, waits for them, and re-layouts  14.6 us (4%)
  other arithmetic  6.59 us (2%)
    pallas_call x1, Pallas kernels, fast_body(): pl.pallas_call(layer_kernel, out_shape=(shape((total_rows, width), bf16),...  358 us
    unnamed x14, local copies, waits for them, and re-layouts  9.92 us

profile of v2, /device:TPU:0, one launch (start us, length us, event | category | flops | bytes accessed | tf_op | source)
XLA Modules:
  0.0 379.7 jit_solution(1495008722111682184)
XLA Ops:
  0.7 0.8 copy.44
  1.4 0.8 copy.45
  2.2 0.8 copy.43
  3.0 1.5 concatenate.10.shard_a
  4.4 0.8 fusion
  5.3 0.6 convert_element_type.51.mask_ref
  5.9 0.3 multiply_cosine_fusion
  6.2 0.8 pad_maximum_fusion.rope_ref
  7.0 357.8 %shard_map.203 = (bf16[128,1536]{1,0:T(8,128)(2,1)}, f32[128,1536]{1,0:T(8,128)}, bf16[4,384,768]{2,1,0:T(8,128)(2,1)}, bf16[2,192,1536]{2,1,0:T(8,128)(2,1)}, b...) custom-call(bf16[128,1536]{1,0:T(8,128)(2,1)} %x_ref.1, ...), custom_call_target="tpu_custom_call" | custom-call | tf_op jit(solution)/shard_map/pallas_call | solution.py:1420
  364.8 0.9 reduce_sum.36
  365.7 0.7 slice_reduce_fusion
  366.5 0.7 copy.46
  367.1 1.6 convert_reduce_fusion
  368.8 0.6 slice_bitcast_fusion.2
  369.4 0.8 slice_bitcast_fusion
  370.2 0.2 add_bitcast_fusion
  370.4 2.2 copy.48
  372.6 0.3 select_bitcast_fusion.1
  373.0 0.2 fusion.3
  373.1 0.3 maximum_bitcast_fusion
  373.4 4.1 %copy.47 = f32[1,384,1,1536]{3,2,1,0:T(1,128)} copy(f32[1,384,1,1536]{3,1,2,0:T(8,128)S(1)} %maximum_bitcast_fusion) | data formatting | bytes 4718592
  377.5 0.7 copy.51
  378.3 0.5 copy-done.2
  378.8 0.9 copy.52
  (11 shorter events, 0.1 us)
Async XLA Ops:
  368.7 1.5 copy-start.1
  370.4 2.2 copy-start
  373.4 4.1 %copy-start.3 = (bf16[128,1536]{1,0:T(8,128)(2,1)S(1)}, bf16[128,1536]{1,0:T(8,128)(2,1)}, u32[]{:S(2)}) copy-start(bf16[128,1536]{1,0:T(8,128)(2,1)} %get-tuple-element.95) | copy-start | bytes 1179652
  377.5 1.3 copy-start.2

commit v3 on v2

--- a/solution.py
+++ b/solution.py
@@ -489,6 +489,7 @@
     grad_in_ref,
     grad_out_ref,
     grad_dense_ref,
+    grad_kv_ref,
     grad_aux_ref,
     spill_b,
     spill_c,
@@ -523,6 +524,7 @@
     s_sems,
     kv_sems,
     tok_sems,
+    tz_sems,
     turn_sems,
     win_sems,
     wout_sems,
@@ -555,12 +557,12 @@
     def at_rows(start, count, step=16):
         return pl.ds(pl.multiple_of(start, step), count)
 
-    def remote(source, target, sems, index, device):
+    def remote(source, target, sems, index, device, recv_index=None):
         return pltpu.make_async_remote_copy(
             src_ref=source,
             dst_ref=target,
             send_sem=sems.at[(0,) + index],
-            recv_sem=sems.at[(1,) + index],
+            recv_sem=sems.at[(1,) + (index if recv_index is None else recv_index)],
             device_id=device,
             device_id_type=MESH,
         )
@@ -584,17 +586,16 @@
         return arena.at[at_rows(start + (part - 1) * width, rows)]
 
     def z_copy(part, step):
-        return remote(
-            shards[part],
-            dense_block(part, 0, 0),
-            z_sems,
-            (part, step),
-            (xor(plane, step), member),
-        )
+        device = (xor(plane, step), member)
+        return remote(shards[part], dense_block(part, 0, 0), z_sems, (part, step), device)
 
     def plane_copy(part, step, chip):
-        block = dense_block(part, step, 0)
-        return remote(block, block, p_sems, (part, step, chip), in_plane(2 * chip))
+        if chip < 3:
+            block = dense_block(part, step, 0)
+            return remote(block, block, p_sems, (part, step, chip), in_plane(2 * chip))
+        via = 1 + step % 2
+        block = dense_block(part, step, 2 * via)
+        return remote(block, block, p_sems, (part, step, 3), in_plane(2 * (3 - via)))
 
     def sibling_copy(part, step, chip):
         block = dense_block(part, step, 2 * chip)
@@ -617,22 +618,29 @@
         for step in (3, 2, 1):
             z_copy(part, step).start()
     for part in range(3):
-        for chip in (1, 2, 3):
+        for chip in (1, 2):
             plane_copy(part, 0, chip).start()
         sibling_copy(part, 0, 0).start()
 
     def pass_on_plane(part):
         for step in (1, 2, 3):
             z_copy(part, step).wait_recv()
-            for chip in (1, 2, 3):
+            for chip in (1, 2):
                 plane_copy(part, step, chip).start()
             sibling_copy(part, step, 0).start()
 
+    def pass_on_diagonal(part, steps):
+        for step in steps:
+            for chip in (1, 2):
+                plane_copy(part, step, chip).wait_recv()
+                if chip == 1 + step % 2:
+                    plane_copy(part, step, 3).start()
+                sibling_copy(part, step, chip).start()
+
     def pass_on_sibling(part):
         for step in range(4):
-            for chip in (1, 2, 3):
-                plane_copy(part, step, chip).wait_recv()
-                sibling_copy(part, step, chip).start()
+            plane_copy(part, step, 3).wait_recv()
+            sibling_copy(part, step, 3).start()
 
     def arrived_dense(part):
         for step in range(4):
@@ -650,44 +658,21 @@
 
     token_arrays = (cot_all, n2_all)
 
+    parts = (0, 512, 1024)
+
+    def cube_device(bits):
+        return (xor(plane, bits & 1), xor(member, bits & 6))
+
+    def part_order(part):
+        return [1 << ((part + k) % 3) for k in range(3)]
+
     def token_z(kind):
         block = token_arrays[kind].at[token_rows(0, 0)]
-        return remote(block, block, tok_sems, (kind, 0), (xor(plane, 1), member))
-
-    def token_plane(kind, plane_step, chip):
-        block = token_arrays[kind].at[token_rows(plane_step, 0)]
-        index = (kind, 1 + plane_step * 3 + chip - 1)
-        return remote(block, block, tok_sems, index, in_plane(2 * chip))
-
-    def token_sibling(kind, plane_step, chip):
-        block = token_arrays[kind].at[token_rows(plane_step, 2 * chip)]
-        return remote(block, block, tok_sems, (kind, 7 + plane_step * 4 + chip), sibling)
-
-    def token_start(kind):
-        token_z(kind).start()
-        for chip in (1, 2, 3):
-            token_plane(kind, 0, chip).start()
-        token_sibling(kind, 0, 0).start()
-
-    def token_pass_plane(kind):
-        token_z(kind).wait_recv()
-        for chip in (1, 2, 3):
-            token_plane(kind, 1, chip).start()
-        token_sibling(kind, 1, 0).start()
-
-    def token_pass_sibling(kind):
-        for plane_step in (0, 1):
-            for chip in (1, 2, 3):
-                token_plane(kind, plane_step, chip).wait_recv()
-                token_sibling(kind, plane_step, chip).start()
-
-    def token_finish(kind):
-        token_z(kind).wait_send()
-        for plane_step in (0, 1):
-            for chip in range(4):
-                if chip:
-                    token_plane(kind, plane_step, chip).wait_send()
-                token_sibling(kind, plane_step, chip).wait()
+        return remote(block, block, tz_sems, (kind,), (xor(plane, 1), member))
+
+    def token_where(kind, plane_step):
+        base = xor(parity, plane_step) * 8 * tokens
+        return token_arrays[kind], tok_sems, (kind, plane_step), 0, None, base
 
     quarter = w_in_ref.shape[0]
     quarter_out = w_out_ref.shape[0]
@@ -702,32 +687,20 @@
 
     out_half = lax.div(plane, 2)
 
+    def wout_send(turn):
+        target = w_out_half.at[at_rows(parity * quarter_out, quarter_out)]
+        device = (out_half + 2 * turn, member)
+        return remote(w_out_ref, target, wout_sems, (turn,), device, (parity,))
+
     def wout_arrived(slot):
         target = w_out_half.at[at_rows(slot * quarter_out, quarter_out)]
-        return pltpu.make_async_remote_copy(
-            src_ref=w_out_ref,
-            dst_ref=target,
-            send_sem=wout_sems.at[0, slot],
-            recv_sem=wout_sems.at[1, slot],
-            device_id=(xor(plane, 1), member),
-            device_id_type=MESH,
-        )
+        return remote(w_out_ref, target, wout_sems, (slot,), (xor(plane, 1), member))
 
     def wout_local():
         return pltpu.make_async_copy(
             w_out_ref,
             w_out_half.at[at_rows(parity * quarter_out, quarter_out)],
             local_sems.at[2],
-        )
-
-    def wout_send(turn):
-        return pltpu.make_async_remote_copy(
-            src_ref=w_out_ref,
-            dst_ref=w_out_half.at[at_rows(parity * quarter_out, quarter_out)],
-            send_sem=wout_sems.at[0, turn],
-            recv_sem=wout_sems.at[1, parity],
-            device_id=(out_half + 2 * turn, member),
-            device_id_type=MESH,
         )
 
     def expert_start():
@@ -768,10 +741,50 @@
         def _():
             wout_local().wait()
 
+    def gather_copy(array, sems, index, lead=(), start=0, stop=None, base=0):
+        stop = array.shape[1] if stop is None else stop
+        middle = (start + stop) // 256 * 128
+        owner_step, device_step = ((0, 2), (0, 4), (2, 4), (4, 2), (0, 1), (2, 1), (4, 1), (6, 1))[
+            index
+        ]
+        if index == 2:
+            stop = middle
+        if index == 3:
+            start = middle
+        block = at_rows(base + xor(member, owner_step) * tokens, tokens, 128)
+        piece = array.at[block, pl.ds(start, stop - start)]
+        return remote(piece, piece, sems, lead + (index,), in_plane(device_step))
+
+    def gather_start(*where):
+        for index in (0, 1, 4):
+            gather_copy(where[0], where[1], index, *where[2:]).start()
+
+    def gather_pass(*where):
+        for index in (0, 1):
+            gather_copy(where[0], where[1], index, *where[2:]).wait_recv()
+            gather_copy(where[0], where[1], 2 + index, *where[2:]).start()
+            gather_copy(where[0], where[1], 5 + index, *where[2:]).start()
+
+    def gather_pass_last(*where):
+        for index in (2, 3):
+            gather_copy(where[0], where[1], index, *where[2:]).wait_recv()
+        gather_copy(where[0], where[1], 7, *where[2:]).start()
+
+    def gather_sent(*where):
+        for index in range(8):
+            gather_copy(where[0], where[1], index, *where[2:]).wait_send()
+
+    def gather_finish(*where):
+        gather_sent(*where)
+        for index in range(4, 8):
+            gather_copy(where[0], where[1], index, *where[2:]).wait_recv()
+
     pass_on_plane(0)
     pass_on_plane(1)
+    pass_on_diagonal(0, range(4))
     pass_on_sibling(0)
     arrived_dense(0)
+    token_z(0).start()
     expert_start()
     aux = full_a[:, pl.ds(2 * kv_width, 128)]
     pick = (
@@ -792,19 +805,13 @@
         return values * cos_part + swapped * (sin_part * orient)
 
     kv_rows = product(normed, full_a[:, pl.ds(0, 2 * kv_width)])
+    own_block = at_rows(member * tokens, tokens, 128)
     for part in range(2 * KEY_VALUE_HEADS):
         piece = kv_rows[:, part * HEAD_DIM : (part + 1) * HEAD_DIM]
         if part < KEY_VALUE_HEADS:
             piece = turned(piece, 1.0)
-        kv_all[part, at_rows(member * tokens, tokens, 128)] = piece.astype(bf16)
-
-    def kv_copy(sems, index, owner_step, device):
-        block = kv_all.at[:, at_rows(xor(member, owner_step) * tokens, tokens, 128)]
-        return remote(block, block, sems, (index,), device)
-
-    for chip in (1, 2, 3):
-        kv_copy(kv_sems, chip - 1, 0, in_plane(2 * chip)).start()
-    kv_copy(kv_sems, 3, 0, sibling).start()
+        kv_all[own_block, pl.ds(part * HEAD_DIM, HEAD_DIM)] = piece.astype(bf16)
+    gather_start(kv_all, kv_sems)
     turn_send[0] = jnp.transpose(normed).reshape(turn_send.shape[1:])
 
     def turn_copy(kind, step):
@@ -823,12 +830,15 @@
             kind, :, pl.ds(member, 1)
         ].reshape(turn_recv.shape[1], rows, tokens)
 
+    turn_start(0)
+    pass_on_plane(2)
+    gather_pass(kv_all, kv_sems)
+    pass_on_diagonal(1, range(4))
+    gather_start(*token_where(0, 0))
+    gather_pass_last(kv_all, kv_sems)
     pass_on_sibling(1)
-    for chip in (1, 2, 3):
-        kv_copy(kv_sems, chip - 1, 0, in_plane(2 * chip)).wait_recv()
-        kv_copy(kv_sems, 3 + chip, 2 * chip, sibling).start()
-    pass_on_plane(2)
-    token_start(0)
+    token_z(0).wait_recv()
+    gather_start(*token_where(0, 1))
     arrived_dense(1)
     spill_b_copy = pltpu.make_async_copy(
         arena.at[pl.ds(0, width)], spill_b, local_sems.at[3]
@@ -839,16 +849,13 @@
             pair = product(normed, arena[pl.ds(0, width), pl.ds(head * HEAD_DIM, 2 * HEAD_DIM)])
         piece = pair[:, (head % 2) * HEAD_DIM : (head % 2 + 1) * HEAD_DIM]
         q_rows[pl.ds(head * tokens, tokens)] = turned(piece, 1.0).astype(bf16)
-    for chip in range(4):
-        index = 3 if chip == 0 else 3 + chip
-        kv_copy(kv_sems, index, 2 * chip, sibling).wait()
-    for chip in (1, 2, 3):
-        kv_copy(kv_sems, chip - 1, 0, in_plane(2 * chip)).wait_send()
+    gather_finish(kv_all, kv_sems)
     for group in range(KEY_VALUE_HEADS):
-        k_t[group] = jnp.transpose(kv_all[group])
-        v_t[group] = jnp.transpose(kv_all[KEY_VALUE_HEADS + group])
-
-    seq_len = kv_all.shape[1]
+        k_t[group] = jnp.transpose(kv_all[:, pl.ds(group * HEAD_DIM, HEAD_DIM)])
+        v_t[group] = jnp.transpose(kv_all[:, pl.ds(kv_width + group * HEAD_DIM, HEAD_DIM)])
+    pass_on_diagonal(2, range(4))
+
+    seq_len = kv_all.shape[0]
     pairs = QUERY_HEADS // 2
     pairs_per_group = pairs // KEY_VALUE_HEADS
     key_index = lax.broadcasted_iota(jnp.int32, (seq_len, 2 * tokens), 0)
@@ -859,7 +866,8 @@
 
     def pair_scores(pair, group):
         queries = q_rows[at_rows(pair * 2 * tokens, 2 * tokens, 128)]
-        scores = product_rows(kv_all[group], queries) * score_scale
+        keys = kv_all[:, at_rows(group * HEAD_DIM, HEAD_DIM, 128)]
+        scores = product_rows(keys, queries) * score_scale
         return jnp.where(allowed, scores, masked_score), queries
 
     def attend(pair, carry):
@@ -877,8 +885,8 @@
         return carry
 
     lax.fori_loop(0, pairs, attend, 0)
-    token_pass_plane(0)
     pass_on_sibling(2)
+    gather_pass(*token_where(0, 0))
     attn_t = attn_buf[...].reshape(width, tokens)
     turn_send[1] = attn_t.reshape(turn_send.shape[1:])
     attn = jnp.transpose(attn_t)
@@ -898,21 +906,22 @@
     spill_c_copy.wait()
     for part in range(3):
         sent_dense(part)
-    token_start(1)
+    token_z(1).start()
+    gather_start(*token_where(1, 0))
     turn_send[2] = jnp.transpose(normed_two).reshape(turn_send.shape[1:])
-    token_pass_sibling(0)
-    token_finish(0)
-    token_pass_plane(1)
-    token_pass_sibling(1)
-    token_finish(1)
-    for kind in range(3):
-        turn_start(kind)
+    gather_pass(*token_where(0, 1))
+    gather_pass_last(*token_where(0, 0))
+    gather_pass_last(*token_where(0, 1))
+    token_z(1).wait_recv()
+    gather_start(*token_where(1, 1))
+    for plane_step in (0, 1):
+        gather_finish(*token_where(0, plane_step))
     expert_finish()
 
     own_lane = lax.broadcasted_iota(jnp.int32, (2 * tokens, 128), 1) == member
     low_lane = lax.broadcasted_iota(jnp.int32, (2 * tokens, 128), 1) == member + 64
     message = 2 * tokens
-    stage_base, sib_base, send_base, recv_base = 0, 2 * message, 4 * message, 8 * message
+    stage_base, sib_base, sum_base, recv_base = 0, 2 * message, 4 * message, 12 * message
 
     def arena_slot(base, slot):
         return at_rows(base + slot * message, message, 128)
@@ -926,35 +935,65 @@
             sibling,
         )
 
-    def sib_gate_copy(slot):
+    def sib_gate_copy():
         return remote(
-            gate_buf.at[slot], gate_buf.at[2 + slot], sib_sems, (2 + slot,), sibling
-        )
-
-    def ret_device(turn):
-        return (xor(plane, lax.div(turn, 4)), xor(member, 2 * lax.rem(turn, 4)))
-
-    def ret_copy(turn, slot):
+            gate_buf.at[pl.ds(8, 8)], gate_buf.at[pl.ds(16, 8)], sib_sems, (2,), sibling
+        )
+
+    def ret_copy(part, held, stage):
+        first, second, third = part_order(part)
+        far = lambda bit: jnp.where(held & bit > 0, 1, 0) if not isinstance(held, int) else held // bit % 2
+        slot = (far(second) + 2 * far(third), 4 + far(third), 6)[stage]
+        columns = pl.ds(parts[part], 512)
         return remote(
-            arena.at[arena_slot(send_base, slot)],
-            arena.at[arena_slot(recv_base, turn)],
+            arena.at[arena_slot(sum_base, held), columns],
+            arena.at[arena_slot(recv_base, slot), columns],
             ret_sems,
-            (turn,),
-            ret_device(turn),
-        )
-
-    def ret_gate_copy(turn, slot):
+            (part, slot),
+            cube_device((first, second, third)[stage]),
+        )
+
+    def ret_arrived(part, slot):
+        columns = pl.ds(parts[part], 512)
+        block = arena.at[arena_slot(recv_base, slot), columns]
+        return remote(block, block, ret_sems, (part, slot), sibling)
+
+    def ret_gate_copy(held):
         return remote(
-            gate_buf.at[4 + slot], gate_buf.at[8 + turn], gate_sems, (turn,), ret_device(turn)
-        )
-
-    def expert_step(turn, carry):
-        slot2 = lax.rem(turn, 2)
-        slot4 = lax.rem(turn, 4)
-        other_plane = xor(parity, lax.div(turn, 4))
-        chip = xor(lax.div(member, 2), lax.rem(turn, 4))
-        start = (other_plane * 4 + chip) * 2 * tokens
-        here = at_rows(start, 2 * tokens, 128)
+            gate_buf.at[held], gate_buf.at[24 + held], gate_sems, (held,), cube_device(held)
+        )
+
+    def halves(values, first):
+        return jnp.where(first, values[:tokens], values[tokens:])
+
+    def block_rows(held):
+        other_plane = xor(parity, held & 1)
+        chip = xor(lax.div(member, 2), lax.div(held, 2))
+        return at_rows((other_plane * 4 + chip) * 2 * tokens, 2 * tokens, 128)
+
+    def first_step(held, carry):
+        @pl.when(held == 1)
+        def _():
+            gather_pass(*token_where(1, 0))
+
+        @pl.when(held == 2)
+        def _():
+            gather_pass(*token_where(1, 1))
+
+        @pl.when(held == 4)
+        def _():
+            gather_pass_last(*token_where(1, 0))
+            gather_pass_last(*token_where(1, 1))
+
+        own = token_rows(held & 1, held & 6)
+        remote(
+            n2_all.at[own],
+            n2_all.at[own],
+            tok_sems,
+            (1, held & 1, 4 + lax.div(held, 2)),
+            sibling,
+        ).wait_recv()
+        here = block_rows(held)
         token_block = n2_all[here, :]
         gate_up = product(token_block, w_in_half[...])
         gates = masked_gates(
@@ -967,41 +1006,49 @@
         up_half = gate_up[:, half:]
         sigmoid_vals = 1.0 / (1.0 + jnp.exp(-gate_half))
         silu_vals = gate_half * sigmoid_vals
-        hidden = (silu_vals * up_half).astype(bf16)
-        hidden_all[here, :] = hidden
-        slot_grad = (gate * cot_all[here, pl.ds(0, width)].astype(f32)).astype(bf16)
-        act_grad = product_rows(slot_grad, w_out_half[...])
+        hidden = silu_vals * up_half
+        hidden_all[here, :] = (gate * hidden).astype(bf16)
+        back = product_rows(cot_all[here, pl.ds(0, width)], w_out_half[...])
+        gate_grad = jnp.sum(hidden * back, axis=1, keepdims=True)
+        act_grad = gate * back
         gate_part = act_grad * up_half * sigmoid_vals * (1.0 + gate_half * (1.0 - sigmoid_vals))
-        g_block = jnp.concatenate([gate_part, act_grad * silu_vals], axis=1).astype(bf16)
-        g_all[here, :] = g_block
+        g_all[here, pl.ds(0, half)] = gate_part.astype(bf16)
+        g_all[here, pl.ds(half, half)] = (act_grad * silu_vals).astype(bf16)
+        gate_high = gate_grad.astype(bf16).astype(f32)
+        gate_lanes = jnp.where(own_lane, gate_high, 0.0) + jnp.where(
+            low_lane, gate_grad - gate_high, 0.0
+        )
+        gate_buf[held] = halves(gate_lanes, core == 0).astype(bf16)
+        gate_buf[8 + held] = halves(gate_lanes, core == 1).astype(bf16)
+        return carry
+
+    lax.fori_loop(0, 8, first_step, 0)
+    token_z(0).wait_send()
+    token_z(1).wait_send()
+    for plane_step in (0, 1):
+        gather_sent(*token_where(1, plane_step))
+    sib_gate_copy().start()
+
+    def second_step(turn, carry):
+        slot2 = lax.rem(turn, 2)
+        held = 7 - turn
+        here = block_rows(held)
+        hidden = hidden_all[here, :]
+        g_block = g_all[here, :]
 
         @pl.when(turn >= 2)
         def _():
             sib_copy(slot2).wait_send()
-            sib_gate_copy(slot2).wait_send()
             pl.semaphore_wait(credit_sem, 1)
-
-        @pl.when(turn > 4)
-        def _():
-            ret_copy(turn - 4, slot4).wait_send()
-            ret_gate_copy(turn - 4, slot4).wait_send()
-
-        def halves(values, first):
-            return jnp.where(first, values[:tokens], values[tokens:])
 
         send_first = core == 1
         stage = stage_base + slot2 * message
-        place = jnp.where(turn == 0, recv_base, send_base + slot4 * message)
+        place = sum_base + held * message
         sib_start = sib_base + slot2 * message
-        gate_grad = jnp.zeros((2 * tokens, 1), f32)
         for start in range(0, width, 512):
             columns = pl.ds(start, 512)
             out_part = product(hidden, w_out_half[:, columns])
             in_part = product_rows(g_block, w_in_half[columns, :])
-            gate_grad = gate_grad + jnp.sum(
-                out_part * cot_all[here, columns].astype(f32), axis=1, keepdims=True
-            )
-            out_part = out_part * gate
             arena[at_rows(stage, tokens, 128), columns] = halves(out_part, send_first).astype(bf16)
             arena[at_rows(stage + tokens, tokens, 128), columns] = halves(
                 in_part, send_first
@@ -1010,41 +1057,52 @@
             arena[at_rows(place + tokens, tokens, 128), columns] = halves(
                 in_part, core == 0
             ).astype(bf16)
-        cot_all[here, pl.ds(0, width)] = slot_grad
-        gate_high = gate_grad.astype(bf16).astype(f32)
-        gate_lanes = jnp.where(own_lane, gate_high, 0.0) + jnp.where(
-            low_lane, gate_grad - gate_high, 0.0
-        )
-        gate_buf[slot2] = halves(gate_lanes, send_first).astype(bf16)
         sib_copy(slot2).start()
-        sib_gate_copy(slot2).start()
-        own_gate = halves(gate_lanes, core == 0)
         sib_copy(slot2).wait_recv()
-        sib_gate_copy(slot2).wait_recv()
         both = at_rows(place, message, 128)
         arena[both] = (
             arena[both].astype(f32) + arena[at_rows(sib_start, message, 128)].astype(f32)
         ).astype(bf16)
-        own_gate = own_gate + gate_buf[2 + slot2].astype(f32)
 
         @pl.when(turn < 6)
         def _():
             pl.semaphore_signal(credit_sem, inc=1, device_id=sibling, device_id_type=MESH)
 
-        gate_buf[jnp.where(turn == 0, 8, 4 + slot4)] = own_gate.astype(bf16)
-
-        @pl.when(turn > 0)
-        def _():
-            ret_copy(turn, slot4).start()
-            ret_gate_copy(turn, slot4).start()
+        for part in range(3):
+
+            @pl.when(held & (1 << part) > 0)
+            def _():
+                ret_copy(part, held, 0).start()
 
         return carry
 
-    lax.fori_loop(0, 8, expert_step, 0)
-
+    for kind in (1, 2):
+        turn_start(kind)
+    lax.fori_loop(0, 8, second_step, 0)
     for slot in (0, 1):
         sib_copy(slot).wait_send()
-        sib_gate_copy(slot).wait_send()
+    sib_gate_copy().wait()
+    gate_buf[pl.ds(0, 8)] = (
+        gate_buf[pl.ds(0, 8)].astype(f32) + gate_buf[pl.ds(16, 8)].astype(f32)
+    ).astype(bf16)
+    for held in range(1, 8):
+        ret_gate_copy(held).start()
+
+    def ret_sum(part, held, slots):
+        columns = pl.ds(parts[part], 512)
+        total = arena[arena_slot(sum_base, held), columns].astype(f32)
+        for slot in slots:
+            total = total + arena[arena_slot(recv_base, slot), columns].astype(f32)
+        return total
+
+    for part in range(3):
+        first, second, third = part_order(part)
+        for held, slot in ((second, 1), (second | third, 3)):
+            ret_arrived(part, slot).wait_recv()
+            arena[arena_slot(sum_base, held), pl.ds(parts[part], 512)] = ret_sum(
+                part, held, (slot,)
+            ).astype(bf16)
+            ret_copy(part, held, 1).start()
 
     def gin_copy(step):
         source = w_in_half.at[at_rows(xor(plane, step) * quarter, quarter)]
@@ -1061,17 +1119,14 @@
             w_in_half[at_rows(start + piece, 128, 128)] = product_columns(
                 columns, g_all[...]
             ).astype(bf16)
-        gin_copy(step).start()
+        if step == 2:
+            gin_copy(2).start()
 
     def gout_copy(slot):
-        return pltpu.make_async_remote_copy(
-            src_ref=w_out_half.at[pl.ds(slot * quarter_out, quarter_out)],
-            dst_ref=grad_out_ref.at[out_half],
-            send_sem=gout_sems.at[0, slot],
-            recv_sem=gout_sems.at[1, out_half],
-            device_id=(parity * 2 + slot, member),
-            device_id_type=MESH,
-        )
+        source = w_out_half.at[pl.ds(slot * quarter_out, quarter_out)]
+        target = grad_out_ref.at[out_half]
+        device = (parity * 2 + slot, member)
+        return remote(source, target, gout_sems, (slot,), device, (out_half,))
 
     def gout_local(slot):
         return pltpu.make_async_copy(
@@ -1081,19 +1136,45 @@
         )
 
     def gout_arrived(turn):
-        return pltpu.make_async_remote_copy(
-            src_ref=w_out_half.at[pl.ds(0, quarter_out)],
-            dst_ref=grad_out_ref.at[turn],
-            send_sem=gout_sems.at[0, turn],
-            recv_sem=gout_sems.at[1, turn],
-            device_id=(xor(plane, 1), member),
-            device_id_type=MESH,
-        )
+        source = w_out_half.at[pl.ds(0, quarter_out)]
+        return remote(source, grad_out_ref.at[turn], gout_sems, (turn,), (xor(plane, 1), member))
 
     for start in range(0, half, 128):
         w_out_half[pl.ds(start, 128)] = product_columns(
             hidden_all[:, pl.ds(start, 128)], cot_all[:, pl.ds(0, width)]
         ).astype(bf16)
+    own_n2 = n2_all[token_rows(0, 0), :]
+    own_mask = mask_ref[...]
+    own_gates = masked_gates(own_n2, full_a[:, pl.ds(2 * kv_width, 128)], own_mask)
+    for part in range(3):
+        third = part_order(part)[2]
+        for slot in (2, 5):
+            ret_arrived(part, slot).wait_recv()
+        arena[arena_slot(sum_base, third), pl.ds(parts[part], 512)] = ret_sum(
+            part, third, (2, 5)
+        ).astype(bf16)
+        ret_copy(part, third, 2).start()
+    gin_copy(0).start()
+
+    load_b = pltpu.make_async_copy(
+        spill_b, cot_all.at[pl.ds(0, width), pl.ds(0, width)], local_sems.at[3]
+    )
+    load_c = pltpu.make_async_copy(spill_c, n2_all.at[pl.ds(0, width)], local_sems.at[4])
+    load_b.start()
+    load_c.start()
+
+    for part in range(3):
+        for slot in (0, 4, 6):
+            ret_arrived(part, slot).wait_recv()
+    totals = [ret_sum(part, 0, (0, 4, 6)) for part in range(3)]
+    total_out = after_buf[...] + jnp.concatenate([total[:tokens] for total in totals], axis=1)
+    total_in = jnp.concatenate([total[tokens:] for total in totals], axis=1)
+    total_gate = gate_buf[0].astype(f32)
+    for held in range(1, 8):
+        ret_gate_copy(held).wait_recv()
+        total_gate = total_gate + gate_buf[24 + held].astype(f32)
+    for step in (3, 1):
+        gin_copy(step).start()
     for slot in (0, 1):
 
         @pl.when(parity * 2 + slot != plane)
@@ -1104,27 +1185,6 @@
         def _():
             gout_local(slot).start()
 
-    load_b = pltpu.make_async_copy(
-        spill_b, cot_all.at[pl.ds(0, width), pl.ds(0, width)], local_sems.at[3]
-    )
-    load_c = pltpu.make_async_copy(spill_c, n2_all.at[pl.ds(0, width)], local_sems.at[4])
-    own_n2 = n2_all[token_rows(0, 0), :]
-    own_mask = mask_ref[...]
-    own_gates = masked_gates(own_n2, full_a[:, pl.ds(2 * kv_width, 128)], own_mask)
-    load_b.start()
-    load_c.start()
-
-    total_out = after_buf[...]
-    total_in = jnp.zeros((tokens, width), f32)
-    total_gate = jnp.zeros((tokens, 128), f32)
-    for turn in range(8):
-        if turn:
-            ret_copy(turn, turn % 4).wait_recv()
-            ret_gate_copy(turn, turn % 4).wait_recv()
-        base = recv_base + turn * message
-        total_out = total_out + arena[pl.ds(base, tokens)].astype(f32)
-        total_in = total_in + arena[pl.ds(base + tokens, tokens)].astype(f32)
-        total_gate = total_gate + gate_buf[8 + turn].astype(f32)
     block_out_ref[...] = total_out.astype(bf16)
     gate_grad = total_gate + pltpu.roll(total_gate, 64, 1)
     gate_inner = jnp.sum(own_gates * gate_grad, axis=1, keepdims=True)
@@ -1146,34 +1206,12 @@
     mid = cot_ref[...].astype(f32) + two_back
     after_buf[...] = mid
     out_grad = mid.astype(bf16)
-    own_block = at_rows(member * tokens, tokens, 128)
     og_all[own_block, pl.ds(0, width)] = out_grad
     og_all[own_block, pl.ds(width, 128)] = (
         lg_parts[0].astype(f32)
         + pltpu.roll(lg_parts[1].astype(f32), 8, 1)
         + pltpu.roll(lg_parts[2].astype(f32), 16, 1)
     ).astype(bf16)
-
-    def gather_copy(array, sems, index, owner_step, device, columns=None):
-        block = at_rows(xor(member, owner_step) * tokens, tokens, 128)
-        piece = array.at[block] if columns is None else array.at[block, columns]
-        return remote(piece, piece, sems, index, device)
-
-    def gather_start(array, sems, lead=(), columns=None):
-        for chip in (1, 2, 3):
-            gather_copy(array, sems, lead + (chip - 1,), 0, in_plane(2 * chip), columns).start()
-        gather_copy(array, sems, lead + (3,), 0, sibling, columns).start()
-
-    def gather_pass(array, sems, lead=(), columns=None):
-        for chip in (1, 2, 3):
-            gather_copy(array, sems, lead + (chip - 1,), 0, in_plane(2 * chip), columns).wait_recv()
-            gather_copy(array, sems, lead + (3 + chip,), 2 * chip, sibling, columns).start()
-
-    def gather_finish(array, sems, lead=(), columns=None):
-        for chip in (1, 2, 3):
-            gather_copy(array, sems, lead + (chip - 1,), 0, in_plane(2 * chip), columns).wait_send()
-        for chip in range(4):
-            gather_copy(array, sems, lead + (3 + chip,), 2 * chip, sibling, columns).wait()
 
     gather_start(og_all, og_sems)
     load_c.wait()
@@ -1198,21 +1236,55 @@
         )
 
     planes = turn_recv.shape[1]
-    dense_starts = (0, 2 * kv_width, 2 * kv_width + width, 2 * kv_width + 2 * width)
+
+    def dense_rows(piece, step):
+        return at_rows((piece * planes + xor(plane, step)) * rows, rows)
+
+    def kv_grad_copy(step):
+        source = arena.at[dense_rows(0, step), pl.ds(0, 2 * kv_width)]
+        if step == 0:
+            return pltpu.make_async_copy(source, grad_kv_ref.at[0], local_sems.at[0])
+        device = (xor(plane, step), member)
+        return remote(source, grad_kv_ref.at[step], dense_sems, (0, step), device)
+
+    def pair_rows(piece, which):
+        return pl.ds(width + ((piece - 1) * 2 + which) * rows, rows)
 
     def dense_copy(piece, step):
-        size = dense_starts[piece + 1] - dense_starts[piece]
-        source = arena.at[
-            at_rows((piece * planes + xor(plane, step)) * rows, rows), pl.ds(0, size)
-        ]
-        target = grad_dense_ref.at[step, :, pl.ds(dense_starts[piece], size)]
-        if step == 0:
-            return pltpu.make_async_copy(source, target, local_sems.at[piece])
-        return remote(source, target, dense_sems, (piece, step), (xor(plane, step), member))
+        columns = pl.ds((piece - 1) * width, width)
+        if step == 2:
+            target = grad_dense_ref.at[1, :, columns]
+            device = (xor(plane, 2), member)
+        else:
+            target = n2_all.at[pair_rows(piece, step // 2)]
+            device = (xor(plane, 1), member)
+        return remote(arena.at[dense_rows(piece, step)], target, dense_sems, (piece, step), device)
+
+    def dense_own(piece):
+        return pltpu.make_async_copy(
+            arena.at[dense_rows(piece, 0)],
+            grad_dense_ref.at[0, :, pl.ds((piece - 1) * width, width)],
+            local_sems.at[piece],
+        )
+
+    def dense_start(piece):
+        for step in (3, 1):
+            dense_copy(piece, step).start()
+
+    def dense_pass(piece):
+        for which, step in ((1, 2), (0, 0)):
+            dense_copy(piece, 1 + 2 * which).wait_recv()
+            block = dense_rows(piece, step)
+            arena[block] = (
+                arena[block].astype(f32) + n2_all[pair_rows(piece, which)].astype(f32)
+            ).astype(bf16)
+            if step:
+                dense_copy(piece, 2).start()
+            else:
+                dense_own(piece).start()
 
     for group in range(KEY_VALUE_HEADS):
-        keys = kv_all[group]
-        values = kv_all[KEY_VALUE_HEADS + group]
+        values = kv_all[:, pl.ds(kv_width + group * HEAD_DIM, HEAD_DIM)]
         dk = jnp.zeros((seq_len, HEAD_DIM), f32)
         dv = jnp.zeros((seq_len, HEAD_DIM), f32)
         for pair in range(group * pairs_per_group, (group + 1) * pairs_per_group):
@@ -1236,22 +1308,11 @@
         for step in range(1, 8):
             dkv_copy(group, step).start()
         span = width // KEY_VALUE_HEADS
-        gather_start(qg_all, qg_sems, (group,), pl.ds(group * span, span))
-
-    gather_finish(og_all, og_sems)
-    for kind in range(3):
-        for step in range(1, 8):
-            turn_copy(kind, step).wait()
-    turned_attn = turn_recv[1].reshape(planes * rows, seq_len)
-    for start in range(0, width, 512):
-        arena[pl.ds(2 * planes * rows, planes * rows), pl.ds(start, 512)] = product(
-            turned_attn, og_all[:, pl.ds(start, 512)]
-        ).astype(bf16)
-    for step in (2, 3, 1, 0):
-        dense_copy(2, step).start()
-    router_part = product(
-        turn_recv[2].reshape(planes * rows, seq_len), og_all[:, pl.ds(width, 128)]
-    )
+        gather_start(qg_all, qg_sems, (group,), group * span, (group + 1) * span)
+        if group == 0:
+            gather_pass_last(og_all, og_sems)
+
+    gather_pass(qg_all, qg_sems, (0,), 0, span)
 
     for group in range(KEY_VALUE_HEADS):
         start = group * 2 * HEAD_DIM
@@ -1264,10 +1325,25 @@
         kvg_all[own_block, pl.ds(group * HEAD_DIM, HEAD_DIM)] = turned(dk, -1.0).astype(bf16)
         kvg_all[own_block, pl.ds(kv_width + group * HEAD_DIM, HEAD_DIM)] = dv.astype(bf16)
     gather_start(kvg_all, kvg_sems)
-    span = width // KEY_VALUE_HEADS
+    gather_finish(og_all, og_sems)
+    for kind in range(3):
+        for step in range(1, 8):
+            turn_copy(kind, step).wait()
+    turned_attn = turn_recv[1].reshape(planes * rows, seq_len)
+    for start in range(0, width, 512):
+        arena[pl.ds(2 * planes * rows, planes * rows), pl.ds(start, 512)] = product(
+            turned_attn, og_all[:, pl.ds(start, 512)]
+        ).astype(bf16)
+    dense_start(2)
+    router_part = product(
+        turn_recv[2].reshape(planes * rows, seq_len), og_all[:, pl.ds(width, 128)]
+    )
+
+    gather_pass(qg_all, qg_sems, (1,), span, 2 * span)
+    gather_pass(kvg_all, kvg_sems)
     for group in range(KEY_VALUE_HEADS):
-        gather_pass(qg_all, qg_sems, (group,), pl.ds(group * span, span))
-    gather_pass(kvg_all, kvg_sems)
+        gather_pass_last(qg_all, qg_sems, (group,), group * span, (group + 1) * span)
+    gather_pass_last(kvg_all, kvg_sems)
 
     load_b.wait()
     own_kvg = kvg_all[own_block, :]
@@ -1288,19 +1364,20 @@
 
     turned_normed = turn_recv[0].reshape(planes * rows, seq_len)
     for group in range(KEY_VALUE_HEADS):
-        gather_finish(qg_all, qg_sems, (group,), pl.ds(group * span, span))
+        gather_finish(qg_all, qg_sems, (group,), group * span, (group + 1) * span)
     for start in range(0, width, 512):
         arena[pl.ds(planes * rows, planes * rows), pl.ds(start, 512)] = product(
             turned_normed, qg_all[:, pl.ds(start, 512)]
         ).astype(bf16)
-    for step in (2, 3, 1, 0):
-        dense_copy(1, step).start()
+    dense_start(1)
+    dense_pass(2)
     gather_finish(kvg_all, kvg_sems)
     arena[pl.ds(0, planes * rows), pl.ds(0, 2 * kv_width)] = product(
         turned_normed, kvg_all[...]
     ).astype(bf16)
     for step in (2, 3, 1, 0):
-        dense_copy(0, step).start()
+        kv_grad_copy(step).start()
+    dense_pass(1)
     for step in range(1, 8):
         turn_copy(3, step).wait()
     aux_total = router_part
@@ -1324,9 +1401,16 @@
     own_aux = pltpu.make_async_copy(aux_send.at[plane], grad_aux_ref.at[0], local_sems.at[7])
     own_aux.start()
 
-    for turn in range(4, 8):
-        ret_copy(turn, turn % 4).wait_send()
-        ret_gate_copy(turn, turn % 4).wait_send()
+    for held in range(1, 8):
+        ret_gate_copy(held).wait_send()
+    for part in range(3):
+        first, second, third = part_order(part)
+        for held in range(8):
+            if held & first:
+                ret_copy(part, held, 0).wait_send()
+        for held in (second, second | third):
+            ret_copy(part, held, 1).wait_send()
+        ret_copy(part, third, 2).wait_send()
     for group in range(KEY_VALUE_HEADS):
         for step in range(1, 8):
             dkv_copy(group, step).wait_send()
@@ -1349,9 +1433,13 @@
         def _():
             gout_arrived(turn).wait_recv()
 
-    for piece in range(3):
-        for step in range(4):
-            dense_copy(piece, step).wait()
+    for step in range(4):
+        kv_grad_copy(step).wait()
+    for piece in (1, 2):
+        dense_own(piece).wait()
+        dense_copy(piece, 2).wait()
+        for step in (1, 3):
+            dense_copy(piece, step).wait_send()
     for step in (1, 2, 3):
         aux_copy(step).wait()
     own_aux.wait()
@@ -1401,7 +1489,6 @@
         ],
         axis=1,
     )
-    dense_width = 2 * kv_width + 2 * width
     in_vmem = pl.BlockSpec(memory_space=pltpu.VMEM)
     anywhere = pl.BlockSpec(memory_space=pl.ANY)
     pair_rows = 2 * seq_len
@@ -1414,6 +1501,7 @@
         grad_in,
         grad_out,
         grad_dense,
+        grad_kv,
         grad_aux,
         _,
         _,
@@ -1424,24 +1512,25 @@
             shape((total_rows, width), f32),
             shape((planes, quarter, 2 * half), bf16),
             shape((2, quarter_out, width), bf16),
-            shape((planes, rows, dense_width), bf16),
+            shape((2, rows, 2 * width), bf16),
+            shape((planes, rows, 2 * kv_width), bf16),
             shape((planes, rows, 128), f32),
             shape((width, width), bf16),
             shape((width, width), bf16),
         ),
         in_specs=[in_vmem] * 7 + [anywhere] * 2,
-        out_specs=(in_vmem,) * 2 + (anywhere,) * 6,
+        out_specs=(in_vmem,) * 2 + (anywhere,) * 7,
         scratch_shapes=[
             pltpu.VMEM((pair_rows, width), bf16),
             pltpu.VMEM((pair_rows, width + 128), bf16),
             pltpu.VMEM((width, 2 * kv_width + 128), bf16),
-            pltpu.VMEM((32 * total_rows, width), bf16),
-            pltpu.VMEM((16, total_rows, 128), bf16),
+            pltpu.VMEM((38 * total_rows, width), bf16),
+            pltpu.VMEM((32, total_rows, 128), bf16),
             pltpu.VMEM((width, 2 * half), bf16),
             pltpu.VMEM((half, width), bf16),
             pltpu.VMEM((pair_rows, half), bf16),
             pltpu.VMEM((pair_rows, 2 * half), bf16),
-            pltpu.VMEM((2 * KEY_VALUE_HEADS, seq_len, HEAD_DIM), bf16),
+            pltpu.VMEM((seq_len, 2 * kv_width), bf16),
             pltpu.VMEM((KEY_VALUE_HEADS, HEAD_DIM, seq_len), bf16),
             pltpu.VMEM((KEY_VALUE_HEADS, HEAD_DIM, seq_len), bf16),
             pltpu.VMEM((heads * total_rows, HEAD_DIM), bf16),
@@ -1461,19 +1550,20 @@
             dma((2, 3, 4)),
             dma((2, 3, 4, 4)),
             dma((2, 3, 4, 4)),
-            dma((2, 7)),
-            dma((2, 2, 15)),
+            dma((2, 8)),
+            dma((2, 2, 2, 8)),
+            dma((2, 2)),
             dma((2, 4, 8)),
             dma((2, 4, 2)),
             dma((2, 2)),
             dma((2, 4)),
-            dma((2, 8)),
+            dma((2, 3, 7)),
             dma((2, 8)),
             dma((2, 4)),
             dma((2, 2)),
-            dma((2, 7)),
-            dma((2, 2, 7)),
-            dma((2, 7)),
+            dma((2, 8)),
+            dma((2, 2, 8)),
+            dma((2, 8)),
             dma((2, 2, 8)),
             dma((2, 3, 4)),
             dma((2, 4)),
@@ -1502,16 +1592,17 @@
         [low[:, :half], high[:, :half], low[:, half:], high[:, half:]], axis=1
     )
     w_out_grad = grad_out[0].astype(f32) + grad_out[1].astype(f32)
-    dense = jnp.sum(grad_dense.astype(f32), axis=0)
+    dense = grad_dense[0].astype(f32) + grad_dense[1].astype(f32)
+    dense_kv = jnp.sum(grad_kv.astype(f32), axis=0)
     aux = jnp.sum(grad_aux, axis=0)
     return (
         block_out,
         tokens_grad,
         jnp.sum(aux[:, 32:35], axis=1)[None],
-        dense[None, :, 2 * kv_width : 2 * kv_width + width],
-        dense[None, :, :kv_width],
-        dense[None, :, kv_width : 2 * kv_width],
-        dense[None, :, 2 * kv_width + width :],
+        dense[None, :, :width],
+        dense_kv[None, :, :kv_width],
+        dense_kv[None, :, kv_width:],
+        dense[None, :, width:],
         jnp.sum(aux[:, 35:38], axis=1)[None],
         (aux[:, :8] + aux[:, 8:16] + aux[:, 16:24])[None],
         w_in_grad[None, :, None, :],

time: 380 us -> 310 us (0.82)
  Pallas kernels: 358 us -> 285 us
    pallas_call x1, Pallas kernels: 358 us -> 285 us  [fast_body(): pl.pallas_call(layer_kernel, out_shape=(shape((total_rows, width), bf16),...]
    unnamed x14 -> x16, local copies, waits for them, and re-layouts: 9.92 us -> 10.2 us
where the time goes in v3:
time: 310 us; the launch traced here: 307 us
  Pallas kernels  285 us (92%)
  local copies, waits for them, and re-layouts  14.9 us (5%)
  other arithmetic  6.3 us (2%)
    pallas_call x1, Pallas kernels, fast_body(): pl.pallas_call(layer_kernel, out_shape=(shape((total_rows, width), bf16),...  285 us
    unnamed x16, local copies, waits for them, and re-layouts  10.2 us

profile of v3, /device:TPU:0, one launch (start us, length us, event | category | flops | bytes accessed | tf_op | source)
XLA Modules:
  0.0 306.6 jit_solution(15971482377507356214)
XLA Ops:
  0.7 0.8 copy.44
  1.4 0.8 copy.45
  2.2 0.8 copy.43
  3.0 1.5 concatenate.10.shard_a
  4.4 0.8 fusion
  5.3 0.6 convert_element_type.59.mask_ref
  5.9 0.3 multiply_cosine_fusion
  6.2 0.8 pad_maximum_fusion.rope_ref
  7.0 284.7 %shard_map.203 = (bf16[128,1536]{1,0:T(8,128)(2,1)}, f32[128,1536]{1,0:T(8,128)}, bf16[4,384,768]{2,1,0:T(8,128)(2,1)}, bf16[2,192,1536]{2,1,0:T(8,128)(2,1)}, b...) custom-call(bf16[128,1536]{1,0:T(8,128)(2,1)} %x_ref.1, ...), custom_call_target="tpu_custom_call" | custom-call | tf_op jit(solution)/shard_map/pallas_call | solution.py:1508
  291.7 1.0 reduce_sum.36
  292.7 0.7 slice_reduce_fusion
  293.5 0.7 copy.46
  294.1 1.0 convert_reduce_fusion
  295.1 0.6 slice_bitcast_fusion.2
  295.8 0.8 slice_bitcast_fusion
  296.7 0.6 copy-done.1
  297.4 2.2 copy.48
  299.6 0.3 select_bitcast_fusion.1
  299.9 0.2 fusion.3
  300.1 0.5 maximum_bitcast_fusion
  300.7 3.8 %copy.47 = f32[1,384,1,1536]{3,2,1,0:T(1,128)} copy(f32[1,384,1,1536]{3,1,2,0:T(8,128)S(1)} %maximum_bitcast_fusion) | data formatting | bytes 4718592
  304.5 0.7 copy.51
  305.2 0.5 copy-done.2
  305.8 0.9 copy.52
  (14 shorter events, 0.3 us)
Async XLA Ops:
  291.7 4.0 %copy-start.3 = (bf16[2,48,3072]{2,1,0:T(8,128)(2,1)S(1)}, bf16[2,48,3072]{2,1,0:T(8,128)(2,1)}, u32[]{:S(2)}) copy-start(bf16[2,48,3072]{2,1,0:T(8,128)(2,1)} %get-tuple-element.21) | copy-start | bytes 1769476
  295.7 1.5 copy-start.1
  297.4 2.2 copy-start
  300.6 3.8 %copy-start.4 = (bf16[128,1536]{1,0:T(8,128)(2,1)S(1)}, bf16[128,1536]{1,0:T(8,128)(2,1)}, u32[]{:S(2)}) copy-start(bf16[128,1536]{1,0:T(8,128)(2,1)} %get-tuple-element.97) | copy-start | bytes 1179652
  304.5 1.3 copy-start.2

commit v4 on v3

--- a/solution.py
+++ b/solution.py
@@ -1,3 +1,5 @@
+import functools
+
 import jax
 import jax.numpy as jnp
 from jax import lax
@@ -477,9 +479,13 @@
 def layer_kernel(
     x_ref,
     cot_ref,
-    mask_ref,
+    routes_ref,
     rope_ref,
-    shard_a,
+    key_ref,
+    value_ref,
+    router_ref,
+    gain_a_ref,
+    gain_m_ref,
     shard_b,
     shard_c,
     w_in_ref,
@@ -547,7 +553,7 @@
     core = lax.rem(member, 2)
     parity = lax.rem(plane, 2)
     tokens, width = x_ref.shape
-    rows = shard_a.shape[0]
+    rows = shard_b.shape[0]
     xor = lax.bitwise_xor
     f32, bf16 = jnp.float32, jnp.bfloat16
     half = FF // 2
@@ -577,8 +583,6 @@
     for device in greeted:
         pl.semaphore_signal(barrier, inc=1, device_id=device, device_id_type=MESH)
 
-    shards = (shard_a, shard_b, shard_c)
-
     def dense_block(part, step, chip_step):
         start = (xor(plane, step) * 8 + xor(member, chip_step)) * rows
         if part == 0:
@@ -586,8 +590,8 @@
         return arena.at[at_rows(start + (part - 1) * width, rows)]
 
     def z_copy(part, step):
-        device = (xor(plane, step), member)
-        return remote(shards[part], dense_block(part, 0, 0), z_sems, (part, step), device)
+        block = dense_block(part, 0, 0)
+        return remote(block, block, z_sems, (part, step), (xor(plane, step), member))
 
     def plane_copy(part, step, chip):
         if chip < 3:
@@ -602,7 +606,22 @@
         return remote(block, block, s_sems, (part, step, chip), sibling)
 
     own_rows = (plane * 8 + member) * rows
-    full_a[at_rows(own_rows, rows)] = shard_a[...]
+    full_a[at_rows(own_rows, rows), pl.ds(0, kv_width)] = key_ref[...]
+    full_a[at_rows(own_rows, rows), pl.ds(kv_width, kv_width)] = value_ref[...]
+    line = lax.broadcasted_iota(jnp.int32, (128, rows), 0)
+    gains = jnp.where(line == EXPERT_LANES, gain_a_ref[...].astype(f32), 0.0) + jnp.where(
+        line == EXPERT_LANES + 1, gain_m_ref[...].astype(f32), 0.0
+    )
+    lines = jnp.concatenate(
+        [router_ref[...].astype(f32), gains[EXPERT_LANES:]], axis=0
+    ).astype(bf16)
+    square = (
+        lax.broadcasted_iota(jnp.int32, (rows, rows), 0)
+        == lax.broadcasted_iota(jnp.int32, (rows, rows), 1)
+    ).astype(bf16)
+    full_a[at_rows(own_rows, rows), pl.ds(2 * kv_width, 128)] = product_rows(
+        square, lines
+    ).astype(bf16)
     arena[at_rows(own_rows, rows)] = shard_b[...]
     arena[at_rows(own_rows + width, rows)] = shard_c[...]
 
@@ -611,7 +630,11 @@
         return at_rows(start, tokens, 128)
 
     cot_all[token_rows(0, 0), pl.ds(0, width)] = cot_ref[...]
-    cot_all[token_rows(0, 0), pl.ds(width, 128)] = mask_ref[...]
+    expert_line = lax.broadcasted_iota(jnp.int32, (128, tokens), 0)
+    named = jnp.zeros((128, tokens), f32)
+    for slot in range(TOP):
+        named = jnp.where(expert_line == routes_ref[pl.ds(slot, 1), :], 1.0, named)
+    cot_all[token_rows(0, 0), pl.ds(width, 128)] = jnp.transpose(named).astype(bf16)
     pl.semaphore_wait(barrier, len(greeted))
 
     for part in range(3):
@@ -920,43 +943,92 @@
 
     own_lane = lax.broadcasted_iota(jnp.int32, (2 * tokens, 128), 1) == member
     low_lane = lax.broadcasted_iota(jnp.int32, (2 * tokens, 128), 1) == member + 64
-    message = 2 * tokens
-    stage_base, sib_base, sum_base, recv_base = 0, 2 * message, 4 * message, 12 * message
-
-    def arena_slot(base, slot):
-        return at_rows(base + slot * message, message, 128)
-
-    def sib_copy(slot):
+    def arena_slot(base, kind, slot):
+        first, each = {"stage": (0, 2), "sib": (4, 2), "sum": (8, 8), "recv": (24, 7)}[base]
+        return at_rows((first + kind * each + slot) * tokens, tokens, 128)
+
+    def sib_copy(kind, slot):
         return remote(
-            arena.at[arena_slot(stage_base, slot)],
-            arena.at[arena_slot(sib_base, slot)],
+            arena.at[arena_slot("stage", kind, slot)],
+            arena.at[arena_slot("sib", kind, slot)],
             sib_sems,
-            (slot,),
+            (kind, slot),
             sibling,
         )
 
     def sib_gate_copy():
         return remote(
-            gate_buf.at[pl.ds(8, 8)], gate_buf.at[pl.ds(16, 8)], sib_sems, (2,), sibling
-        )
-
-    def ret_copy(part, held, stage):
+            gate_buf.at[pl.ds(8, 8)], gate_buf.at[pl.ds(16, 8)], sib_sems, (2, 0), sibling
+        )
+
+    def bit_of(held, bit):
+        if isinstance(held, int):
+            return held // bit % 2
+        return jnp.where(held & bit > 0, 1, 0)
+
+    def ret_copy(kind, part, held, stage):
         first, second, third = part_order(part)
-        far = lambda bit: jnp.where(held & bit > 0, 1, 0) if not isinstance(held, int) else held // bit % 2
-        slot = (far(second) + 2 * far(third), 4 + far(third), 6)[stage]
+        slot = (
+            bit_of(held, second) + 2 * bit_of(held, third),
+            4 + bit_of(held, third),
+            6,
+        )[stage]
         columns = pl.ds(parts[part], 512)
         return remote(
-            arena.at[arena_slot(sum_base, held), columns],
-            arena.at[arena_slot(recv_base, slot), columns],
+            arena.at[arena_slot("sum", kind, held), columns],
+            arena.at[arena_slot("recv", kind, slot), columns],
             ret_sems,
-            (part, slot),
+            (kind, part, slot),
             cube_device((first, second, third)[stage]),
         )
 
-    def ret_arrived(part, slot):
+    def ret_arrived(kind, part, slot):
         columns = pl.ds(parts[part], 512)
-        block = arena.at[arena_slot(recv_base, slot), columns]
-        return remote(block, block, ret_sems, (part, slot), sibling)
+        block = arena.at[arena_slot("recv", kind, slot), columns]
+        return remote(block, block, ret_sems, (kind, part, slot), sibling)
+
+    def ret_sum(kind, part, held, slots):
+        columns = pl.ds(parts[part], 512)
+        total = arena[arena_slot("sum", kind, held), columns].astype(f32)
+        for slot in slots:
+            total = total + arena[arena_slot("recv", kind, slot), columns].astype(f32)
+        return total
+
+    def ret_second(kind):
+        for part in range(3):
+            first, second, third = part_order(part)
+            for held, slot in ((second, 1), (second | third, 3)):
+                ret_arrived(kind, part, slot).wait_recv()
+                arena[arena_slot("sum", kind, held), pl.ds(parts[part], 512)] = ret_sum(
+                    kind, part, held, (slot,)
+                ).astype(bf16)
+                ret_copy(kind, part, held, 1).start()
+
+    def ret_third(kind):
+        for part in range(3):
+            third = part_order(part)[2]
+            for slot in (2, 5):
+                ret_arrived(kind, part, slot).wait_recv()
+            arena[arena_slot("sum", kind, third), pl.ds(parts[part], 512)] = ret_sum(
+                kind, part, third, (2, 5)
+            ).astype(bf16)
+            ret_copy(kind, part, third, 2).start()
+
+    def ret_total(kind):
+        for part in range(3):
+            for slot in (0, 4, 6):
+                ret_arrived(kind, part, slot).wait_recv()
+        return jnp.concatenate([ret_sum(kind, part, 0, (0, 4, 6)) for part in range(3)], axis=1)
+
+    def ret_sent(kind):
+        for part in range(3):
+            first, second, third = part_order(part)
+            for held in range(8):
+                if held & first:
+                    ret_copy(kind, part, held, 0).wait_send()
+            for held in (second, second | third):
+                ret_copy(kind, part, held, 1).wait_send()
+            ret_copy(kind, part, third, 2).wait_send()
 
     def ret_gate_copy(held):
         return remote(
@@ -1029,80 +1101,72 @@
         gather_sent(*token_where(1, plane_step))
     sib_gate_copy().start()
 
-    def second_step(turn, carry):
-        slot2 = lax.rem(turn, 2)
-        held = 7 - turn
-        here = block_rows(held)
-        hidden = hidden_all[here, :]
-        g_block = g_all[here, :]
-
-        @pl.when(turn >= 2)
+    def turn_held(turn):
+        return jnp.where(turn == 3, 3, jnp.where(turn == 4, 4, 7 - turn))
+
+    def second_step(kind, turn, carry):
+        @pl.when(turn < 8)
         def _():
-            sib_copy(slot2).wait_send()
-            pl.semaphore_wait(credit_sem, 1)
-
-        send_first = core == 1
-        stage = stage_base + slot2 * message
-        place = sum_base + held * message
-        sib_start = sib_base + slot2 * message
-        for start in range(0, width, 512):
-            columns = pl.ds(start, 512)
-            out_part = product(hidden, w_out_half[:, columns])
-            in_part = product_rows(g_block, w_in_half[columns, :])
-            arena[at_rows(stage, tokens, 128), columns] = halves(out_part, send_first).astype(bf16)
-            arena[at_rows(stage + tokens, tokens, 128), columns] = halves(
-                in_part, send_first
+            slot2 = lax.rem(turn, 2)
+            held = turn_held(turn)
+            here = block_rows(held)
+
+            @pl.when(turn >= 2)
+            def _():
+                sib_copy(kind, slot2).wait_send()
+                pl.semaphore_wait(credit_sem, 1)
+
+            place = arena_slot("sum", kind, held)
+            for start in range(0, width, 512):
+                columns = pl.ds(start, 512)
+                if kind == 0:
+                    result = product_rows(g_all[here, :], w_in_half[columns, :])
+                else:
+                    result = product(hidden_all[here, :], w_out_half[:, columns])
+                arena[arena_slot("stage", kind, slot2), columns] = halves(
+                    result, core == 1
+                ).astype(bf16)
+                arena[place, columns] = halves(result, core == 0).astype(bf16)
+            sib_copy(kind, slot2).start()
+
+        @pl.when(turn > 0)
+        def _():
+            last = turn - 1
+            slot2 = lax.rem(last, 2)
+            held = turn_held(last)
+            place = arena_slot("sum", kind, held)
+            sib_copy(kind, slot2).wait_recv()
+            arena[place] = (
+                arena[place].astype(f32) + arena[arena_slot("sib", kind, slot2)].astype(f32)
             ).astype(bf16)
-            arena[at_rows(place, tokens, 128), columns] = halves(out_part, core == 0).astype(bf16)
-            arena[at_rows(place + tokens, tokens, 128), columns] = halves(
-                in_part, core == 0
-            ).astype(bf16)
-        sib_copy(slot2).start()
-        sib_copy(slot2).wait_recv()
-        both = at_rows(place, message, 128)
-        arena[both] = (
-            arena[both].astype(f32) + arena[at_rows(sib_start, message, 128)].astype(f32)
-        ).astype(bf16)
-
-        @pl.when(turn < 6)
-        def _():
-            pl.semaphore_signal(credit_sem, inc=1, device_id=sibling, device_id_type=MESH)
-
-        for part in range(3):
-
-            @pl.when(held & (1 << part) > 0)
+
+            @pl.when(last < 6)
             def _():
-                ret_copy(part, held, 0).start()
+                pl.semaphore_signal(credit_sem, inc=1, device_id=sibling, device_id_type=MESH)
+
+            for part in range(3):
+
+                @pl.when(held & (1 << part) > 0)
+                def _():
+                    ret_copy(kind, part, held, 0).start()
 
         return carry
+
+    def second_loop(kind):
+        lax.fori_loop(0, 9, functools.partial(second_step, kind), 0)
+        for slot in (0, 1):
+            sib_copy(kind, slot).wait_send()
 
     for kind in (1, 2):
         turn_start(kind)
-    lax.fori_loop(0, 8, second_step, 0)
-    for slot in (0, 1):
-        sib_copy(slot).wait_send()
+    second_loop(0)
     sib_gate_copy().wait()
     gate_buf[pl.ds(0, 8)] = (
         gate_buf[pl.ds(0, 8)].astype(f32) + gate_buf[pl.ds(16, 8)].astype(f32)
     ).astype(bf16)
     for held in range(1, 8):
         ret_gate_copy(held).start()
-
-    def ret_sum(part, held, slots):
-        columns = pl.ds(parts[part], 512)
-        total = arena[arena_slot(sum_base, held), columns].astype(f32)
-        for slot in slots:
-            total = total + arena[arena_slot(recv_base, slot), columns].astype(f32)
-        return total
-
-    for part in range(3):
-        first, second, third = part_order(part)
-        for held, slot in ((second, 1), (second | third, 3)):
-            ret_arrived(part, slot).wait_recv()
-            arena[arena_slot(sum_base, held), pl.ds(parts[part], 512)] = ret_sum(
-                part, held, (slot,)
-            ).astype(bf16)
-            ret_copy(part, held, 1).start()
+    ret_second(0)
 
     def gin_copy(step):
         source = w_in_half.at[at_rows(xor(plane, step) * quarter, quarter)]
@@ -1112,15 +1176,15 @@
             source, grad_in_ref.at[step], gin_sems, (step,), (xor(plane, step), member)
         )
 
-    for step in (2, 1, 3, 0):
+    for step in (2, 3, 1, 0):
         start = xor(plane, step) * quarter
         for piece in range(0, quarter, 128):
             columns = n2_all[:, at_rows(start + piece, 128, 128)]
             w_in_half[at_rows(start + piece, 128, 128)] = product_columns(
                 columns, g_all[...]
             ).astype(bf16)
-        if step == 2:
-            gin_copy(2).start()
+        if step in (2, 3):
+            gin_copy(step).start()
 
     def gout_copy(slot):
         source = w_out_half.at[pl.ds(slot * quarter_out, quarter_out)]
@@ -1139,22 +1203,16 @@
         source = w_out_half.at[pl.ds(0, quarter_out)]
         return remote(source, grad_out_ref.at[turn], gout_sems, (turn,), (xor(plane, 1), member))
 
+    own_n2 = n2_all[token_rows(0, 0), :]
+    own_mask = cot_all[token_rows(0, 0), pl.ds(width, 128)]
+    own_gates = masked_gates(own_n2, full_a[:, pl.ds(2 * kv_width, 128)], own_mask)
+    gin_copy(0).start()
+    ret_third(0)
+    second_loop(1)
     for start in range(0, half, 128):
         w_out_half[pl.ds(start, 128)] = product_columns(
             hidden_all[:, pl.ds(start, 128)], cot_all[:, pl.ds(0, width)]
         ).astype(bf16)
-    own_n2 = n2_all[token_rows(0, 0), :]
-    own_mask = mask_ref[...]
-    own_gates = masked_gates(own_n2, full_a[:, pl.ds(2 * kv_width, 128)], own_mask)
-    for part in range(3):
-        third = part_order(part)[2]
-        for slot in (2, 5):
-            ret_arrived(part, slot).wait_recv()
-        arena[arena_slot(sum_base, third), pl.ds(parts[part], 512)] = ret_sum(
-            part, third, (2, 5)
-        ).astype(bf16)
-        ret_copy(part, third, 2).start()
-    gin_copy(0).start()
 
     load_b = pltpu.make_async_copy(
         spill_b, cot_all.at[pl.ds(0, width), pl.ds(0, width)], local_sems.at[3]
@@ -1163,18 +1221,12 @@
     load_b.start()
     load_c.start()
 
-    for part in range(3):
-        for slot in (0, 4, 6):
-            ret_arrived(part, slot).wait_recv()
-    totals = [ret_sum(part, 0, (0, 4, 6)) for part in range(3)]
-    total_out = after_buf[...] + jnp.concatenate([total[:tokens] for total in totals], axis=1)
-    total_in = jnp.concatenate([total[tokens:] for total in totals], axis=1)
+    total_in = ret_total(0)
     total_gate = gate_buf[0].astype(f32)
     for held in range(1, 8):
         ret_gate_copy(held).wait_recv()
         total_gate = total_gate + gate_buf[24 + held].astype(f32)
-    for step in (3, 1):
-        gin_copy(step).start()
+    gin_copy(1).start()
     for slot in (0, 1):
 
         @pl.when(parity * 2 + slot != plane)
@@ -1185,7 +1237,6 @@
         def _():
             gout_local(slot).start()
 
-    block_out_ref[...] = total_out.astype(bf16)
     gate_grad = total_gate + pltpu.roll(total_gate, 64, 1)
     gate_inner = jnp.sum(own_gates * gate_grad, axis=1, keepdims=True)
     logit_grad = own_gates * (gate_grad - gate_inner)
@@ -1204,7 +1255,7 @@
 
     two_back, gain_m_row = norm_backward(after, gain_buf[pl.ds(1, 1), :], total_in)
     mid = cot_ref[...].astype(f32) + two_back
-    after_buf[...] = mid
+    dx_ref[...] = mid
     out_grad = mid.astype(bf16)
     og_all[own_block, pl.ds(0, width)] = out_grad
     og_all[own_block, pl.ds(width, 128)] = (
@@ -1223,17 +1274,36 @@
             ].astype(bf16)
     gather_pass(og_all, og_sems)
 
+    def dkv_rows(kind_core, chip):
+        return at_rows((kind_core * 4 + chip) * tokens, tokens, 128)
+
+    def dkv_columns(group):
+        return pl.ds(group * 2 * HEAD_DIM, 2 * HEAD_DIM)
+
+    def dkv_sibling(group):
+        source = g_all.at[at_rows((1 - core) * 4 * tokens, 4 * tokens, 128), dkv_columns(group)]
+        target = dkv_recv.at[group, pl.ds(4 * tokens, 4 * tokens)]
+        return remote(source, target, dkv_sems, (group, 0), sibling)
+
     def dkv_copy(group, step):
+        chip = xor(lax.div(member, 2), step)
         return remote(
-            g_all.at[
-                at_rows(xor(member, step) * tokens, tokens, 128),
-                pl.ds(group * 2 * HEAD_DIM, 2 * HEAD_DIM),
-            ],
-            dkv_recv.at[group, step],
+            g_all.at[dkv_rows(core, chip), dkv_columns(group)],
+            dkv_recv.at[group, pl.ds(step * tokens, tokens)],
             dkv_sems,
             (group, step),
-            in_plane(step),
-        )
+            in_plane(2 * step),
+        )
+
+    def dkv_pass(group):
+        dkv_sibling(group).wait_recv()
+        mine = at_rows(core * 4 * tokens, 4 * tokens, 128)
+        g_all[mine, dkv_columns(group)] = (
+            g_all[mine, dkv_columns(group)].astype(f32)
+            + dkv_recv[group, pl.ds(4 * tokens, 4 * tokens)].astype(f32)
+        ).astype(bf16)
+        for step in (1, 2, 3):
+            dkv_copy(group, step).start()
 
     planes = turn_recv.shape[1]
 
@@ -1303,28 +1373,38 @@
                     piece, -1.0
                 ).astype(bf16)
         start = group * 2 * HEAD_DIM
-        g_all[pl.ds(0, seq_len), pl.ds(start, HEAD_DIM)] = (dk * score_scale).astype(bf16)
-        g_all[pl.ds(0, seq_len), pl.ds(start + HEAD_DIM, HEAD_DIM)] = dv.astype(bf16)
-        for step in range(1, 8):
-            dkv_copy(group, step).start()
+        dk = (dk * score_scale).astype(bf16)
+        dv = dv.astype(bf16)
+        for block in range(8):
+            place = pl.ds((block % 2 * 4 + block // 2) * tokens, tokens)
+            here = slice(block * tokens, (block + 1) * tokens)
+            g_all[place, pl.ds(start, HEAD_DIM)] = dk[here]
+            g_all[place, pl.ds(start + HEAD_DIM, HEAD_DIM)] = dv[here]
+        dkv_sibling(group).start()
         span = width // KEY_VALUE_HEADS
         gather_start(qg_all, qg_sems, (group,), group * span, (group + 1) * span)
         if group == 0:
             gather_pass_last(og_all, og_sems)
-
+            dkv_pass(0)
+            ret_second(1)
+
+    dkv_pass(1)
     gather_pass(qg_all, qg_sems, (0,), 0, span)
 
     for group in range(KEY_VALUE_HEADS):
         start = group * 2 * HEAD_DIM
-        dk = g_all[own_block, pl.ds(start, HEAD_DIM)].astype(f32)
-        dv = g_all[own_block, pl.ds(start + HEAD_DIM, HEAD_DIM)].astype(f32)
-        for step in range(1, 8):
+        mine = dkv_rows(core, lax.div(member, 2))
+        dk = g_all[mine, pl.ds(start, HEAD_DIM)].astype(f32)
+        dv = g_all[mine, pl.ds(start + HEAD_DIM, HEAD_DIM)].astype(f32)
+        for step in (1, 2, 3):
             dkv_copy(group, step).wait_recv()
-            dk = dk + dkv_recv[group, step, :, pl.ds(0, HEAD_DIM)].astype(f32)
-            dv = dv + dkv_recv[group, step, :, pl.ds(HEAD_DIM, HEAD_DIM)].astype(f32)
+            block = pl.ds(step * tokens, tokens)
+            dk = dk + dkv_recv[group, block, pl.ds(0, HEAD_DIM)].astype(f32)
+            dv = dv + dkv_recv[group, block, pl.ds(HEAD_DIM, HEAD_DIM)].astype(f32)
         kvg_all[own_block, pl.ds(group * HEAD_DIM, HEAD_DIM)] = turned(dk, -1.0).astype(bf16)
         kvg_all[own_block, pl.ds(kv_width + group * HEAD_DIM, HEAD_DIM)] = dv.astype(bf16)
     gather_start(kvg_all, kvg_sems)
+    ret_third(1)
     gather_finish(og_all, og_sems)
     for kind in range(3):
         for step in range(1, 8):
@@ -1354,7 +1434,7 @@
     one_back, gain_a_row = norm_backward(
         x_ref[...].astype(f32), gain_buf[pl.ds(0, 1), :], normed_grad
     )
-    dx_ref[...] = after_buf[...] + one_back
+    dx_ref[...] = dx_ref[...] + one_back
     line = lax.broadcasted_iota(jnp.int32, (128, width), 0)
     gain_lines = jnp.zeros((128, width), f32)
     for offset, part in enumerate(split_three(gain_a_row) + split_three(gain_m_row)):
@@ -1401,18 +1481,15 @@
     own_aux = pltpu.make_async_copy(aux_send.at[plane], grad_aux_ref.at[0], local_sems.at[7])
     own_aux.start()
 
+    block_out_ref[...] = (after_buf[...] + ret_total(1)).astype(bf16)
+
     for held in range(1, 8):
         ret_gate_copy(held).wait_send()
-    for part in range(3):
-        first, second, third = part_order(part)
-        for held in range(8):
-            if held & first:
-                ret_copy(part, held, 0).wait_send()
-        for held in (second, second | third):
-            ret_copy(part, held, 1).wait_send()
-        ret_copy(part, third, 2).wait_send()
+    for kind in (0, 1):
+        ret_sent(kind)
     for group in range(KEY_VALUE_HEADS):
-        for step in range(1, 8):
+        dkv_sibling(group).wait_send()
+        for step in (1, 2, 3):
             dkv_copy(group, step).wait_send()
     gin_copy(0).wait()
     for step in (1, 2, 3):
@@ -1475,20 +1552,6 @@
     positions = lax.axis_index("expert") * total_rows + jnp.arange(total_rows, dtype=jnp.int32)
     cos_table, sin_table = rope_tables(positions, HEAD_DIM)
     rope = jnp.concatenate([cos_table, cos_table, -sin_table, sin_table], axis=1)
-    lanes = jnp.arange(128, dtype=jnp.int32)
-    mask = jnp.any(routes[0][:, :, None] == lanes[None, None, :], axis=1).astype(bf16)
-    padding = jnp.zeros((rows, 128 - EXPERT_LANES - 2), bf16)
-    shard_a = jnp.concatenate(
-        [
-            key_weight[0],
-            value_weight[0],
-            w_router[0],
-            gain_attn[0][:, None],
-            gain_moe[0][:, None],
-            padding,
-        ],
-        axis=1,
-    )
     in_vmem = pl.BlockSpec(memory_space=pltpu.VMEM)
     anywhere = pl.BlockSpec(memory_space=pl.ANY)
     pair_rows = 2 * seq_len
@@ -1518,7 +1581,7 @@
             shape((width, width), bf16),
             shape((width, width), bf16),
         ),
-        in_specs=[in_vmem] * 7 + [anywhere] * 2,
+        in_specs=[in_vmem] * 11 + [anywhere] * 2,
         out_specs=(in_vmem,) * 2 + (anywhere,) * 7,
         scratch_shapes=[
             pltpu.VMEM((pair_rows, width), bf16),
@@ -1544,7 +1607,7 @@
             pltpu.VMEM((seq_len, width + 128), bf16),
             pltpu.VMEM((seq_len, width), bf16),
             pltpu.VMEM((seq_len, 2 * kv_width), bf16),
-            pltpu.VMEM((KEY_VALUE_HEADS, members, total_rows, 2 * HEAD_DIM), bf16),
+            pltpu.VMEM((KEY_VALUE_HEADS, seq_len, 2 * HEAD_DIM), bf16),
             pltpu.VMEM((planes, rows, 128), f32),
             pltpu.VMEM((16, width), f32),
             dma((2, 3, 4)),
@@ -1556,8 +1619,8 @@
             dma((2, 4, 8)),
             dma((2, 4, 2)),
             dma((2, 2)),
-            dma((2, 4)),
-            dma((2, 3, 7)),
+            dma((2, 3, 2)),
+            dma((2, 2, 3, 7)),
             dma((2, 8)),
             dma((2, 4)),
             dma((2, 2)),
@@ -1576,9 +1639,13 @@
     )(
         tokens,
         cotangent,
-        mask,
+        routes[0].T,
         rope,
-        shard_a,
+        key_weight[0],
+        value_weight[0],
+        w_router[0].T,
+        gain_attn,
+        gain_moe,
         w_query[0],
         w_output[0],
         w_in.reshape(quarter, 2 * FF),

time: 310 us -> 291 us (0.939); the launches traced: 307 us -> 291 us
  Pallas kernels: 285 us -> 275 us
  local copies, waits for them, and re-layouts: 14.9 us -> 11.1 us
    pallas_call x1, Pallas kernels: 285 us -> 275 us  [fast_body(): pl.pallas_call(layer_kernel, out_shape=(shape((total_rows, width), bf16),...]
    unnamed x16 -> x15, local copies, waits for them, and re-layouts: 10.2 us -> 9.46 us
where the time goes in v4:
time: 291 us
  Pallas kernels  275 us (95%)
  local copies, waits for them, and re-layouts  11.1 us (4%)
  other arithmetic  4.62 us (2%)
    pallas_call x1, Pallas kernels, fast_body(): pl.pallas_call(layer_kernel, out_shape=(shape((total_rows, width), bf16),...  275 us
    unnamed x15, local copies, waits for them, and re-layouts  9.46 us

profile of v4, /device:TPU:0, one launch (start us, length us, event | category | flops | bytes accessed | tf_op | source)
XLA Modules:
  0.0 291.2 jit_solution(1238024002815690047)
XLA Ops:
  0.7 0.3 multiply_cosine_fusion
  1.0 0.8 pad_maximum_fusion.rope_ref
  1.8 274.7 %shard_map.203 = (bf16[128,1536]{1,0:T(8,128)(2,1)}, f32[128,1536]{1,0:T(8,128)}, bf16[4,384,768]{2,1,0:T(8,128)(2,1)}, bf16[2,192,1536]{2,1,0:T(8,128)(2,1)}, b...) custom-call(bf16[128,1536]{1,0:T(8,128)(2,1)} %x_ref.1, ...), custom_call_target="tpu_custom_call" | custom-call | tf_op jit(solution)/shard_map/pallas_call | solution.py:1571
  276.5 0.0 copy-start.3
  276.5 1.0 reduce_sum.36
  277.5 0.7 slice_reduce_fusion
  278.2 0.1 fusion
  278.3 0.7 copy.29
  278.9 1.0 convert_reduce_fusion
  279.9 0.6 slice_bitcast_fusion.2
  280.6 0.0 copy-done.3
  280.6 0.1 add_bitcast_fusion.1
  280.6 0.8 slice_bitcast_fusion
  281.5 0.6 copy-done.1
  282.0 0.1 add_bitcast_fusion
  282.2 2.2 copy.31
  284.4 0.3 select_bitcast_fusion.1
  284.8 0.2 fusion.2
  284.9 0.3 maximum_bitcast_fusion
  285.2 0.0 copy-start.4
  285.2 3.8 %copy.30 = f32[1,384,1,1536]{3,2,1,0:T(1,128)} copy(f32[1,384,1,1536]{3,1,2,0:T(8,128)S(1)} %maximum_bitcast_fusion) | data formatting | bytes 4718592
  289.1 0.7 copy.34
  289.8 0.5 copy-done.2
  290.3 0.9 copy.35
  (7 shorter events, 0.0 us)
Async XLA Ops:
  276.5 4.0 %copy-start.3 = (bf16[2,48,3072]{2,1,0:T(8,128)(2,1)S(1)}, bf16[2,48,3072]{2,1,0:T(8,128)(2,1)}, u32[]{:S(2)}) copy-start(bf16[2,48,3072]{2,1,0:T(8,128)(2,1)} %get-tuple-element.21) | copy-start | bytes 1769476
  280.6 1.5 copy-start.1
  282.2 2.2 copy-start
  285.2 3.8 %copy-start.4 = (bf16[128,1536]{1,0:T(8,128)(2,1)S(1)}, bf16[128,1536]{1,0:T(8,128)(2,1)}, u32[]{:S(2)}) copy-start(bf16[128,1536]{1,0:T(8,128)(2,1)} %get-tuple-element.86) | copy-start | bytes 1179652
  289.1 1.3 copy-start.2

commit v5 on v4

--- a/solution.py
+++ b/solution.py
@@ -1523,6 +1523,69 @@
 
 
 EXPERT_LANES = 8
+
+
+def final_kernel(
+    block_ref,
+    dx_ref,
+    in_ref,
+    out_ref,
+    dense_ref,
+    kv_ref,
+    aux_ref,
+    block_out,
+    tokens_grad,
+    gain_a_out,
+    query_out,
+    key_out,
+    value_out,
+    output_out,
+    gain_m_out,
+    router_out,
+    w_in_out,
+    w_out_out,
+):
+    f32 = jnp.float32
+    half = FF // 2
+    block_out[...] = block_ref[...]
+    tokens_grad[...] = dx_ref[...]
+    even = lax.rem(lax.axis_index("dp"), 2) == 0
+    own = in_ref[0].astype(f32) + in_ref[2].astype(f32)
+    other = in_ref[1].astype(f32) + in_ref[3].astype(f32)
+    halves = (jnp.where(even, own, other), jnp.where(even, other, own))
+    count = own.shape[0]
+    tiles = half // 128
+    for tile in range(4 * tiles):
+        piece, rest = divmod(tile, 2 * tiles)
+        which, lane = divmod(rest, tiles)
+        start = piece * half + lane * 128
+        w_in_out[pl.ds(tile, count, 4 * tiles), :] = halves[which][:, start : start + 128]
+    total = out_ref[0].astype(f32) + out_ref[1].astype(f32)
+    count, width = total.shape
+    for tile in range(width // 128):
+        w_out_out[pl.ds(tile, count, width // 128), :] = total[:, tile * 128 : tile * 128 + 128]
+
+    @pl.when(pl.program_id(0) == 0)
+    def _():
+        dense = dense_ref[0].astype(f32) + dense_ref[1].astype(f32)
+        query_out[0] = dense[:, :width]
+        output_out[0] = dense[:, width:]
+        kv = (
+            kv_ref[0].astype(f32)
+            + kv_ref[1].astype(f32)
+            + kv_ref[2].astype(f32)
+            + kv_ref[3].astype(f32)
+        )
+        key_out[0] = kv[:, : kv.shape[1] // 2]
+        value_out[0] = kv[:, kv.shape[1] // 2 :]
+        aux = aux_ref[0] + aux_ref[1] + aux_ref[2] + aux_ref[3]
+        rows = aux.shape[0]
+        lines = jnp.transpose(
+            jnp.concatenate([aux, jnp.zeros((128 - rows, 128), f32)], axis=0)
+        )
+        router_out[...] = (lines[0:8] + lines[8:16] + lines[16:24])[:, :rows]
+        gain_a_out[...] = (lines[32:33] + lines[33:34] + lines[34:35])[:, :rows]
+        gain_m_out[...] = (lines[35:36] + lines[36:37] + lines[37:38])[:, :rows]
 
 
 def fast_body(
@@ -1651,29 +1714,52 @@
         w_in.reshape(quarter, 2 * FF),
         w_out.reshape(quarter_out, width),
     )
-    own = grad_in[0].astype(f32) + grad_in[2].astype(f32)
-    other = grad_in[1].astype(f32) + grad_in[3].astype(f32)
-    even = lax.rem(lax.axis_index("dp"), 2) == 0
-    low, high = jnp.where(even, own, other), jnp.where(even, other, own)
-    w_in_grad = jnp.concatenate(
-        [low[:, :half], high[:, :half], low[:, half:], high[:, half:]], axis=1
-    )
-    w_out_grad = grad_out[0].astype(f32) + grad_out[1].astype(f32)
-    dense = grad_dense[0].astype(f32) + grad_dense[1].astype(f32)
-    dense_kv = jnp.sum(grad_kv.astype(f32), axis=0)
-    aux = jnp.sum(grad_aux, axis=0)
-    return (
-        block_out,
-        tokens_grad,
-        jnp.sum(aux[:, 32:35], axis=1)[None],
-        dense[None, :, :width],
-        dense_kv[None, :, :kv_width],
-        dense_kv[None, :, kv_width:],
-        dense[None, :, width:],
-        jnp.sum(aux[:, 35:38], axis=1)[None],
-        (aux[:, :8] + aux[:, 8:16] + aux[:, 16:24])[None],
-        w_in_grad[None, :, None, :],
-        w_out_grad[None, :, None, :],
+    steps = 4
+    whole = lambda *dims: pl.BlockSpec(dims, lambda i: (0,) * len(dims))
+    final = pl.pallas_call(
+        final_kernel,
+        grid=(steps,),
+        out_shape=(
+            shape((total_rows, width), bf16),
+            shape((total_rows, width), f32),
+            shape((1, rows), f32),
+            shape((1, rows, width), f32),
+            shape((1, rows, kv_width), f32),
+            shape((1, rows, kv_width), f32),
+            shape((1, rows, width), f32),
+            shape((1, rows), f32),
+            shape((EXPERT_LANES, rows), f32),
+            shape((quarter * 2 * FF // 128, 128), f32),
+            shape((quarter_out * width // 128, 128), f32),
+        ),
+        in_specs=[
+            pl.BlockSpec((total_rows // steps, width), lambda i: (i, 0)),
+            pl.BlockSpec((total_rows // steps, width), lambda i: (i, 0)),
+            pl.BlockSpec((planes, quarter // steps, 2 * half), lambda i: (0, i, 0)),
+            pl.BlockSpec((2, quarter_out // steps, width), lambda i: (0, i, 0)),
+            whole(2, rows, 2 * width),
+            whole(planes, rows, 2 * kv_width),
+            whole(planes, rows, 128),
+        ],
+        out_specs=(
+            pl.BlockSpec((total_rows // steps, width), lambda i: (i, 0)),
+            pl.BlockSpec((total_rows // steps, width), lambda i: (i, 0)),
+            whole(1, rows),
+            whole(1, rows, width),
+            whole(1, rows, kv_width),
+            whole(1, rows, kv_width),
+            whole(1, rows, width),
+            whole(1, rows),
+            whole(EXPERT_LANES, rows),
+            pl.BlockSpec((quarter * 2 * FF // 128 // steps, 128), lambda i: (i, 0)),
+            pl.BlockSpec((quarter_out * width // 128 // steps, 128), lambda i: (i, 0)),
+        ),
+        compiler_params=pltpu.CompilerParams(vmem_limit_bytes=63 * 2**20),
+    )(block_out, tokens_grad, grad_in, grad_out, grad_dense, grad_kv, grad_aux)
+    return final[:8] + (
+        final[8].T[None],
+        final[9].reshape(1, quarter, 1, 2 * FF),
+        final[10].reshape(1, quarter_out, 1, width),
     )
 
 

time: 291 us -> 283 us (0.973)
  local copies, waits for them, and re-layouts: 11.1 us -> 0 us
  Pallas kernels: 275 us -> 280 us
  other arithmetic: 4.62 us -> 1.11 us
    unnamed x15 -> x0, local copies, waits for them, and re-layouts: 9.46 us -> none
    pallas_call x0 -> x1, Pallas kernels: none -> 5.8 us  [fast_body(): pl.pallas_call(final_kernel, grid=(steps,), out_shape=(shape((total_rows,...]
where the time goes in v5:
time: 283 us; the launch traced here: 282 us
  Pallas kernels  280 us (99%)
    pallas_call x1, Pallas kernels, fast_body(): pl.pallas_call(layer_kernel, out_shape=(shape((total_rows, width), bf16),...  275 us
    pallas_call x1, Pallas kernels, fast_body(): pl.pallas_call(final_kernel, grid=(steps,), out_shape=(shape((total_rows,...  5.8 us

profile of v5, /device:TPU:0, one launch (start us, length us, event | category | flops | bytes accessed | tf_op | source)
XLA Modules:
  0.0 282.4 jit_solution(16411203321554716495)
XLA Ops:
  0.7 0.3 multiply_cosine_fusion
  1.0 0.8 pad_maximum_fusion.rope_ref
  1.8 274.6 %shard_map.203 = (bf16[128,1536]{1,0:T(8,128)(2,1)}, f32[128,1536]{1,0:T(8,128)}, bf16[4,384,768]{2,1,0:T(8,128)(2,1)}, bf16[2,192,1536]{2,1,0:T(8,128)(2,1)}, b...) custom-call(bf16[128,1536]{1,0:T(8,128)(2,1)} %x_ref.1, ...), custom_call_target="tpu_custom_call" | custom-call | tf_op jit(solution)/shard_map/pallas_call | solution.py:1634
  276.4 5.8 %shard_map.204 = (bf16[128,1536]{1,0:T(8,128)(2,1)}, f32[128,1536]{1,0:T(8,128)}, f32[1,48]{1,0:T(1,128)}, f32[1,48,1536]{2,1,0:T(8,128)}, f32[1,48,256]{2,1,0:T...) custom-call(bf16[128,1536]{1,0:T(8,128)(2,1)} %get-tuple-element.29., ...), custom_call_target="tpu_custom_call" | custom-call | tf_op jit(solution)/shard_map/pallas_call | solution.py:1719
  (2 shorter events, 0.0 us)

commit v6 on v5

--- a/solution.py
+++ b/solution.py
@@ -508,12 +508,12 @@
     w_out_half,
     hidden_all,
     g_all,
+    gin_early,
     kv_all,
     k_t,
     v_t,
     q_rows,
     do_rows,
-    normed_buf,
     attn_buf,
     after_buf,
     lse_buf,
@@ -819,7 +819,6 @@
     gain_m = gain_buf[pl.ds(1, 1), :]
     residual = x_ref[...].astype(f32)
     normed = (residual * norm_factor(residual) * gain_a).astype(bf16)
-    normed_buf[...] = normed
     cos_part = rope_ref[:, pl.ds(0, HEAD_DIM)]
     sin_part = rope_ref[:, pl.ds(HEAD_DIM, HEAD_DIM)]
 
@@ -839,7 +838,7 @@
 
     def turn_copy(kind, step):
         return remote(
-            turn_send.at[kind, :, xor(member, step)],
+            turn_send.at[kind % 3, :, xor(member, step)],
             turn_recv.at[kind, :, :, at_rows(member * tokens, tokens, 128)],
             turn_sems,
             (kind, step),
@@ -850,7 +849,7 @@
         for step in range(1, 8):
             turn_copy(kind, step).start()
         turn_recv[kind, :, :, at_rows(member * tokens, tokens, 128)] = turn_send[
-            kind, :, pl.ds(member, 1)
+            kind % 3, :, pl.ds(member, 1)
         ].reshape(turn_recv.shape[1], rows, tokens)
 
     turn_start(0)
@@ -1152,6 +1151,27 @@
 
         return carry
 
+    def gin_copy(step):
+        if step >= 2:
+            source = gin_early.at[step - 2]
+        else:
+            source = w_in_half.at[at_rows(xor(plane, step) * quarter, quarter)]
+        if step == 0:
+            return pltpu.make_async_copy(source, grad_in_ref.at[0], local_sems.at[5])
+        return remote(
+            source, grad_in_ref.at[step], gin_sems, (step,), (xor(plane, step), member)
+        )
+
+    def gin_quarter(step):
+        start = xor(plane, step) * quarter
+        for piece in range(0, quarter, 128):
+            columns = n2_all[:, at_rows(start + piece, 128, 128)]
+            result = product_columns(columns, g_all[...]).astype(bf16)
+            if step >= 2:
+                gin_early[step - 2, pl.ds(piece, 128)] = result
+            else:
+                w_in_half[at_rows(start + piece, 128, 128)] = result
+
     def second_loop(kind):
         lax.fori_loop(0, 9, functools.partial(second_step, kind), 0)
         for slot in (0, 1):
@@ -1159,6 +1179,8 @@
 
     for kind in (1, 2):
         turn_start(kind)
+    gin_quarter(2)
+    gin_copy(2).start()
     second_loop(0)
     sib_gate_copy().wait()
     gate_buf[pl.ds(0, 8)] = (
@@ -1168,23 +1190,11 @@
         ret_gate_copy(held).start()
     ret_second(0)
 
-    def gin_copy(step):
-        source = w_in_half.at[at_rows(xor(plane, step) * quarter, quarter)]
-        if step == 0:
-            return pltpu.make_async_copy(source, grad_in_ref.at[0], local_sems.at[5])
-        return remote(
-            source, grad_in_ref.at[step], gin_sems, (step,), (xor(plane, step), member)
-        )
-
-    for step in (2, 3, 1, 0):
-        start = xor(plane, step) * quarter
-        for piece in range(0, quarter, 128):
-            columns = n2_all[:, at_rows(start + piece, 128, 128)]
-            w_in_half[at_rows(start + piece, 128, 128)] = product_columns(
-                columns, g_all[...]
-            ).astype(bf16)
-        if step in (2, 3):
-            gin_copy(step).start()
+    gin_quarter(3)
+    gin_copy(3).start()
+    for step in (1, 0):
+        gin_quarter(step)
+    gin_copy(0).start()
 
     def gout_copy(slot):
         source = w_out_half.at[pl.ds(slot * quarter_out, quarter_out)]
@@ -1206,7 +1216,6 @@
     own_n2 = n2_all[token_rows(0, 0), :]
     own_mask = cot_all[token_rows(0, 0), pl.ds(width, 128)]
     own_gates = masked_gates(own_n2, full_a[:, pl.ds(2 * kv_width, 128)], own_mask)
-    gin_copy(0).start()
     ret_third(0)
     second_loop(1)
     for start in range(0, half, 128):
@@ -1439,7 +1448,7 @@
     gain_lines = jnp.zeros((128, width), f32)
     for offset, part in enumerate(split_three(gain_a_row) + split_three(gain_m_row)):
         gain_lines = jnp.where(line == 32 + offset, part.astype(f32), gain_lines)
-    turn_send[3] = jnp.transpose(gain_lines.astype(bf16)).reshape(turn_send.shape[1:])
+    turn_send[0] = jnp.transpose(gain_lines.astype(bf16)).reshape(turn_send.shape[1:])
     turn_start(3)
 
     turned_normed = turn_recv[0].reshape(planes * rows, seq_len)
@@ -1656,16 +1665,16 @@
             pltpu.VMEM((half, width), bf16),
             pltpu.VMEM((pair_rows, half), bf16),
             pltpu.VMEM((pair_rows, 2 * half), bf16),
+            pltpu.VMEM((2, quarter, 2 * half), bf16),
             pltpu.VMEM((seq_len, 2 * kv_width), bf16),
             pltpu.VMEM((KEY_VALUE_HEADS, HEAD_DIM, seq_len), bf16),
             pltpu.VMEM((KEY_VALUE_HEADS, HEAD_DIM, seq_len), bf16),
             pltpu.VMEM((heads * total_rows, HEAD_DIM), bf16),
             pltpu.VMEM((heads * total_rows, HEAD_DIM), bf16),
-            pltpu.VMEM((total_rows, width), bf16),
             pltpu.VMEM((heads, HEAD_DIM, total_rows), bf16),
             pltpu.VMEM((total_rows, width), f32),
             pltpu.VMEM((heads // 2, 8, 2 * total_rows), f32),
-            pltpu.VMEM((4, planes, members, rows, total_rows), bf16),
+            pltpu.VMEM((3, planes, members, rows, total_rows), bf16),
             pltpu.VMEM((4, planes, rows, seq_len), bf16),
             pltpu.VMEM((seq_len, width + 128), bf16),
             pltpu.VMEM((seq_len, width), bf16),

time: 283 us -> 279 us (0.986)
  Pallas kernels: 280 us -> 276 us
    pallas_call x1, Pallas kernels: 275 us -> 271 us  [fast_body(): pl.pallas_call(layer_kernel, out_shape=(shape((total_rows, width), bf16),...]
where the time goes in v6:
time: 279 us; the launch traced here: 278 us
  Pallas kernels  276 us (99%)
    pallas_call x1, Pallas kernels, fast_body(): pl.pallas_call(layer_kernel, out_shape=(shape((total_rows, width), bf16),...  271 us
    pallas_call x1, Pallas kernels, fast_body(): pl.pallas_call(final_kernel, grid=(steps,), out_shape=(shape((total_rows,...  5.8 us

profile of v6, /device:TPU:0, one launch (start us, length us, event | category | flops | bytes accessed | tf_op | source)
XLA Modules:
  0.0 278.3 jit_solution(18124358547851549270)
XLA Ops:
  0.7 0.3 multiply_cosine_fusion
  1.0 0.8 pad_maximum_fusion.rope_ref
  1.8 270.5 %shard_map.203 = (bf16[128,1536]{1,0:T(8,128)(2,1)}, f32[128,1536]{1,0:T(8,128)}, bf16[4,384,768]{2,1,0:T(8,128)(2,1)}, bf16[2,192,1536]{2,1,0:T(8,128)(2,1)}, b...) custom-call(bf16[128,1536]{1,0:T(8,128)(2,1)} %x_ref.1, ...), custom_call_target="tpu_custom_call" | custom-call | tf_op jit(solution)/shard_map/pallas_call | solution.py:1643
  272.3 5.8 %shard_map.204 = (bf16[128,1536]{1,0:T(8,128)(2,1)}, f32[128,1536]{1,0:T(8,128)}, f32[1,48]{1,0:T(1,128)}, f32[1,48,1536]{2,1,0:T(8,128)}, f32[1,48,256]{2,1,0:T...) custom-call(bf16[128,1536]{1,0:T(8,128)(2,1)} %get-tuple-element.29., ...), custom_call_target="tpu_custom_call" | custom-call | tf_op jit(solution)/shard_map/pallas_call | solution.py:1728
  (2 shorter events, 0.0 us)

commit v7 on v6

--- a/solution.py
+++ b/solution.py
@@ -1723,7 +1723,7 @@
         w_in.reshape(quarter, 2 * FF),
         w_out.reshape(quarter_out, width),
     )
-    steps = 4
+    steps = 2
     whole = lambda *dims: pl.BlockSpec(dims, lambda i: (0,) * len(dims))
     final = pl.pallas_call(
         final_kernel,

time: 279 us -> 278 us (level)
  no operation moved by 1% of the time
where the time goes in v7:
time: 278 us; the launch traced here: 277 us
  Pallas kernels  275 us (99%)
    pallas_call x1, Pallas kernels, fast_body(): pl.pallas_call(layer_kernel, out_shape=(shape((total_rows, width), bf16),...  271 us

profile of v7, /device:TPU:0, one launch (start us, length us, event | category | flops | bytes accessed | tf_op | source)
XLA Modules:
  0.0 277.4 jit_solution(14662474659385579784)
XLA Ops:
  0.7 0.3 multiply_cosine_fusion
  1.0 0.8 pad_maximum_fusion.rope_ref
  1.8 270.5 %shard_map.203 = (bf16[128,1536]{1,0:T(8,128)(2,1)}, f32[128,1536]{1,0:T(8,128)}, bf16[4,384,768]{2,1,0:T(8,128)(2,1)}, bf16[2,192,1536]{2,1,0:T(8,128)(2,1)}, b...) custom-call(bf16[128,1536]{1,0:T(8,128)(2,1)} %x_ref.1, ...), custom_call_target="tpu_custom_call" | custom-call | tf_op jit(solution)/shard_map/pallas_call | solution.py:1643
  272.3 4.8 %shard_map.204 = (bf16[128,1536]{1,0:T(8,128)(2,1)}, f32[128,1536]{1,0:T(8,128)}, f32[1,48]{1,0:T(1,128)}, f32[1,48,1536]{2,1,0:T(8,128)}, f32[1,48,256]{2,1,0:T...) custom-call(bf16[128,1536]{1,0:T(8,128)(2,1)} %get-tuple-element.29., ...), custom_call_target="tpu_custom_call" | custom-call | tf_op jit(solution)/shard_map/pallas_call | solution.py:1728
  (2 shorter events, 0.0 us)
